TPU v7x, 32 devices: a whole 2x2x4 slice. The times are simulated.
32 devices in a mesh: row: 8 (over y, x, core), col: 4 (over z).
Axes of the slice: x: 2, y: 2, z: 4, core: 2. Of those that a mesh axis runs over, the one named last changes fastest.
Arguments:
- tokens: bfloat16 [2, 16384, 768], P(None, ('row', 'col')), may hold values from -6 to 6
- seg_ids: int32 [2, 16384], P(None, ('row', 'col')), may hold values from 0 to 3, as said below
- pad_mask: int32 [2, 16384], P(None, ('row', 'col')), may hold values from 0 to 1, as said below
- rand_blocks: int32 [2, 256, 3], P(None, ('row', 'col')), may hold values from 0 to 15
- w_qkv: bfloat16 [2, 768, 2304], P(None, 'row', 'col'), may hold values from -0.21875 to 0.21875
- w_out: bfloat16 [2, 768, 768], P(None, 'row', 'col'), may hold values from -2.5 to 2.5
- w_up: bfloat16 [2, 768, 3072], P(None, 'row', 'col'), may hold values from -0.21875 to 0.21875
- w_down: bfloat16 [2, 3072, 768], P(None, 'row', 'col'), may hold values from -0.109375 to 0.109375
- layer_vectors: bfloat16 [2, 8, 768], P(None, None, 'col'), may hold values from -1.5 to 1.5, as said below
- bias_up: bfloat16 [2, 3072], P(None, 'col'), may hold values from -1.5 to 1.5
- d_out: bfloat16 [2, 16384, 768], P(None, ('row', 'col')), may hold values from -6 to 6
Outputs:
- output: bfloat16 [2, 16384, 768], P(None, ('row', 'col'))
- d_tokens: float32 [2, 16384, 768], P(None, ('row', 'col'))
- grad_qkv: float32 [2, 768, 2304], P(None, 'row', 'col')
- grad_out: float32 [2, 768, 768], P(None, 'row', 'col')
- grad_up: float32 [2, 768, 3072], P(None, 'row', 'col')
- grad_down: float32 [2, 3072, 768], P(None, 'row', 'col')
- grad_vectors: float32 [2, 8, 768], P(None, None, 'col')
- grad_bias_up: float32 [2, 3072], P(None, 'col')
Inputs may be any that keep to these rules, and one draw needn't show every extreme that they name: `seg_ids`: within each aligned sequence of 1024 tokens the numbers never fall, start at 0 and end at 3, each step by one; every document has at least 204 tokens. `pad_mask`: within each aligned sequence of 1024 tokens the ones come first, followed by 1 to 256 zeros. `layer_vectors`: gains near 1, biases near 0.
All inputs are finite; a program needn't handle non-finite values.
Results may differ from a plain program's by a relative error of at most 0.02.
Values may be sent and summed in bfloat16 or wider, within the bound.
A program may use at most 256 MiB of HBM per device.

v0:
```python
import jax
import jax.numpy as jnp
from jax import lax
from jax.sharding import PartitionSpec as P

BLOCK = 64
HEAD = 64


NEG_FILL = -1e30
EPS = 1e-06
ROOT_HALF = 0.7071067811865476
INV_ROOT_TAU = 0.3989422804014327


def swapped(block, axis, apart):
    count = lax.axis_size(axis)
    route = []
    for low in range(count):
        high = low | 1 << apart
        if high != low and high < count:
            route += [(low, high), (high, low)]
    return lax.ppermute(block, axis, route)


def norm_forward(residual, norm_gain, norm_shift):
    center = residual - jnp.mean(residual, axis=-1, keepdims=True)
    scale_inv = lax.rsqrt(jnp.mean(center * center, axis=-1, keepdims=True) + EPS)
    normed = center * scale_inv
    return (normed * norm_gain + norm_shift, normed, scale_inv)


def norm_backward(grad_y, normed, scale_inv, norm_gain):
    grad_n = grad_y * norm_gain
    return scale_inv * (
        grad_n
        - jnp.mean(grad_n, axis=-1, keepdims=True)
        - normed * jnp.mean(grad_n * normed, axis=-1, keepdims=True)
    )


def gelu_value(pre_act):
    return 0.5 * pre_act * (1.0 + lax.erf(pre_act * ROOT_HALF))


def gelu_slope(pre_act):
    return 0.5 * (1.0 + lax.erf(pre_act * ROOT_HALF)) + pre_act * INV_ROOT_TAU * jnp.exp(
        -0.5 * pre_act * pre_act
    )


def to_groups(matrix):
    return matrix.reshape(matrix.shape[0], -1, 2 * HEAD).transpose(1, 0, 2)


def from_groups(stacked):
    return stacked.transpose(1, 0, 2).reshape(stacked.shape[1], -1)


def key_pattern(own_marks, marks_peer, parity):
    seg_own, pad_own, rand_own = own_marks
    half_rows = seg_own.shape[0]
    seg_peer = marks_peer[0].astype(jnp.int32)
    pad_peer = marks_peer[1].astype(jnp.int32)
    first_half = parity == 0
    seg_all = jnp.where(
        first_half, jnp.concatenate([seg_own, seg_peer]), jnp.concatenate([seg_peer, seg_own])
    )
    pad_all = jnp.where(
        first_half, jnp.concatenate([pad_own, pad_peer]), jnp.concatenate([pad_peer, pad_own])
    )
    length = 2 * half_rows
    places = jnp.arange(length, dtype=jnp.int32)
    starts_at = jnp.concatenate(
        [jnp.ones((1,), jnp.int32), (seg_all[1:] != seg_all[:-1]).astype(jnp.int32)]
    )
    starts = lax.cummax(places * starts_at, axis=0)
    global_key = places - starts < 2 * BLOCK
    offset = parity * half_rows
    global_query = lax.dynamic_slice_in_dim(global_key, offset, half_rows)
    query_pos = offset + jnp.arange(half_rows, dtype=jnp.int32)
    near_block = jnp.abs(query_pos[:, None] // BLOCK - places[None, :] // BLOCK) <= 1
    blocks_all = length // BLOCK
    hit_table = jnp.any(
        rand_own[:, :, None] == jnp.arange(blocks_all, dtype=jnp.int32)[None, None, :], axis=1
    )
    random_hit = jnp.broadcast_to(
        hit_table[:, None, :, None], (half_rows // BLOCK, BLOCK, blocks_all, BLOCK)
    ).reshape(half_rows, length)
    same_doc = seg_own[:, None] == seg_all[None, :]
    allowed = (
        same_doc
        & (pad_all[None, :] > 0)
        & (global_query[:, None] | global_key[None, :] | near_block | random_hit)
    )
    return allowed | (query_pos[:, None] == places[None, :])


def group_scores(query_heads, key_heads, allowed):
    scores = jnp.einsum(
        "qge,kge->gqk", query_heads, key_heads, preferred_element_type=jnp.float32
    ) * HEAD ** (-0.5)
    return jnp.where(allowed[None], scores, NEG_FILL)


def attend_forward(queries, key_rows, values, allowed):
    half_rows = queries.shape[0]
    length = key_rows.shape[0]

    def one_group(inputs):
        query_grp, key_grp, value_grp = inputs
        scores = group_scores(
            query_grp.reshape(half_rows, 2, HEAD), key_grp.reshape(length, 2, HEAD), allowed
        )
        row_peak = jnp.max(scores, axis=-1, keepdims=True)
        exponent = jnp.exp(scores - row_peak)
        row_total = jnp.sum(exponent, axis=-1, keepdims=True)
        prob_low = (exponent / row_total).astype(jnp.bfloat16)
        mixture = jnp.einsum(
            "gqk,kge->qge",
            prob_low,
            value_grp.reshape(length, 2, HEAD),
            preferred_element_type=jnp.float32,
        )
        return (mixture.reshape(half_rows, 2 * HEAD), row_peak[..., 0] + jnp.log(row_total[..., 0]))

    mixture, log_total = lax.map(
        one_group, (to_groups(queries), to_groups(key_rows), to_groups(values))
    )
    return (from_groups(mixture), log_total)


def attend_backward(queries, key_rows, values, allowed, log_total, grad_mix):
    half_rows = queries.shape[0]
    length = key_rows.shape[0]
    scale_factor = HEAD ** (-0.5)

    def one_group(inputs):
        query_grp, key_grp, value_grp, lse_grp, grad_grp = inputs
        query_heads = query_grp.reshape(half_rows, 2, HEAD)
        key_heads = key_grp.reshape(length, 2, HEAD)
        value_heads = value_grp.reshape(length, 2, HEAD)
        grad_heads = grad_grp.reshape(half_rows, 2, HEAD)
        weights = jnp.exp(group_scores(query_heads, key_heads, allowed) - lse_grp[..., None])
        weights_low = weights.astype(jnp.bfloat16)
        grad_w = jnp.einsum(
            "qge,kge->gqk", grad_heads, value_heads, preferred_element_type=jnp.float32
        )
        row_dot = jnp.sum(grad_w * weights, axis=-1, keepdims=True)
        grad_s = (weights * (grad_w - row_dot)).astype(jnp.bfloat16)
        grad_q = (
            jnp.einsum("gqk,kge->qge", grad_s, key_heads, preferred_element_type=jnp.float32)
            * scale_factor
        )
        grad_k = (
            jnp.einsum("gqk,qge->kge", grad_s, query_heads, preferred_element_type=jnp.float32)
            * scale_factor
        )
        grad_v = jnp.einsum(
            "gqk,qge->kge", weights_low, grad_heads, preferred_element_type=jnp.float32
        )
        return (
            grad_q.reshape(half_rows, 2 * HEAD),
            grad_k.reshape(length, 2 * HEAD),
            grad_v.reshape(length, 2 * HEAD),
        )

    grad_q, grad_k, grad_v = lax.map(
        one_group,
        (
            to_groups(queries),
            to_groups(key_rows),
            to_groups(values),
            log_total,
            to_groups(grad_mix),
        ),
    )
    return (from_groups(grad_q), from_groups(grad_k), from_groups(grad_v))


def layer_forward(hidden, weights, mark_rows, own_marks, allowed, parity):
    mat_qkv, mat_out, mat_up, mat_down, vectors, up_bias = weights
    width = hidden.shape[1]
    projected = jnp.dot(hidden, mat_qkv, preferred_element_type=jnp.float32)
    queries = (projected[:, :width] + vectors[0]).astype(jnp.bfloat16)
    key_rows = projected[:, width : 2 * width].astype(jnp.bfloat16)
    values = (projected[:, 2 * width :] + vectors[1]).astype(jnp.bfloat16)
    keys_peer, values_peer, marks_peer = swapped((key_rows, values, mark_rows), "col", 0)
    if allowed is None:
        allowed = key_pattern(own_marks, marks_peer, parity)
    first_half = parity == 0
    keys_all = jnp.where(
        first_half, jnp.concatenate([key_rows, keys_peer]), jnp.concatenate([keys_peer, key_rows])
    )
    values_all = jnp.where(
        first_half, jnp.concatenate([values, values_peer]), jnp.concatenate([values_peer, values])
    )
    mixture, log_total = attend_forward(queries, keys_all, values_all, allowed)
    mixture_low = mixture.astype(jnp.bfloat16)
    branch = jnp.dot(mixture_low, mat_out, preferred_element_type=jnp.float32) + vectors[2]
    first_norm, normed_one, inv_one = norm_forward(
        hidden.astype(jnp.float32) + branch, vectors[4], vectors[5]
    )
    first_out = first_norm.astype(jnp.bfloat16)
    pre_act = jnp.dot(first_out, mat_up, preferred_element_type=jnp.float32) + up_bias
    act_low = gelu_value(pre_act).astype(jnp.bfloat16)
    down_out = jnp.dot(act_low, mat_down, preferred_element_type=jnp.float32) + vectors[3]
    final_out, normed_two, inv_two = norm_forward(
        first_out.astype(jnp.float32) + down_out, vectors[6], vectors[7]
    )
    saved_set = (
        hidden,
        queries,
        keys_all,
        values_all,
        log_total,
        mixture_low,
        normed_one,
        inv_one,
        first_out,
        pre_act,
        act_low,
        normed_two,
        inv_two,
    )
    return (final_out, saved_set, allowed)


def layer_backward(grad_y, weights, saved_set, allowed, parity):
    mat_qkv, mat_out, mat_up, mat_down, vectors, up_bias = weights
    (
        hidden,
        queries,
        keys_all,
        values_all,
        log_total,
        mixture_low,
        normed_one,
        inv_one,
        first_out,
        pre_act,
        act_low,
        normed_two,
        inv_two,
    ) = saved_set
    grad_gain_two = jnp.sum(grad_y * normed_two, axis=0)
    grad_shift_two = jnp.sum(grad_y, axis=0)
    grad_two = norm_backward(grad_y, normed_two, inv_two, vectors[6])
    grad_down_low = grad_two.astype(jnp.bfloat16)
    grad_bias_down = jnp.sum(grad_down_low.astype(jnp.float32), axis=0)
    grad_mat_down = jnp.einsum(
        "tf,td->fd", act_low, grad_down_low, preferred_element_type=jnp.float32
    )
    grad_act = jnp.einsum("td,fd->tf", grad_down_low, mat_down, preferred_element_type=jnp.float32)
    grad_pre = (grad_act * gelu_slope(pre_act)).astype(jnp.bfloat16)
    grad_bias_hidden = jnp.sum(grad_pre.astype(jnp.float32), axis=0)
    grad_mat_up = jnp.einsum("td,tf->df", first_out, grad_pre, preferred_element_type=jnp.float32)
    grad_first = grad_two + jnp.einsum(
        "tf,df->td", grad_pre, mat_up, preferred_element_type=jnp.float32
    )
    grad_gain_one = jnp.sum(grad_first * normed_one, axis=0)
    grad_shift_one = jnp.sum(grad_first, axis=0)
    grad_one = norm_backward(grad_first, normed_one, inv_one, vectors[4])
    grad_branch = grad_one.astype(jnp.bfloat16)
    grad_bias_out = jnp.sum(grad_branch.astype(jnp.float32), axis=0)
    grad_mat_out = jnp.einsum(
        "td,te->de", mixture_low, grad_branch, preferred_element_type=jnp.float32
    )
    grad_mix = jnp.einsum(
        "te,de->td", grad_branch, mat_out, preferred_element_type=jnp.float32
    ).astype(jnp.bfloat16)
    grad_q, grad_k, grad_v = attend_backward(
        queries, keys_all, values_all, allowed, log_total, grad_mix
    )
    half_rows = queries.shape[0]
    first_half = parity == 0
    own_k = jnp.where(first_half, grad_k[:half_rows], grad_k[half_rows:])
    peer_k = jnp.where(first_half, grad_k[half_rows:], grad_k[:half_rows])
    own_v = jnp.where(first_half, grad_v[:half_rows], grad_v[half_rows:])
    peer_v = jnp.where(first_half, grad_v[half_rows:], grad_v[:half_rows])
    back_k, back_v = (
        swapped(peer_k.astype(jnp.bfloat16), "col", 0).astype(peer_k.dtype),
        swapped(peer_v.astype(jnp.bfloat16), "col", 0).astype(peer_v.dtype),
    )
    grad_queries = grad_q.astype(jnp.bfloat16)
    grad_keys = (own_k + back_k).astype(jnp.bfloat16)
    grad_values = (own_v + back_v).astype(jnp.bfloat16)
    grad_proj = jnp.concatenate([grad_queries, grad_keys, grad_values], axis=1)
    grad_mat_qkv = jnp.einsum("td,te->de", hidden, grad_proj, preferred_element_type=jnp.float32)
    grad_hidden = grad_one + jnp.einsum(
        "te,de->td", grad_proj, mat_qkv, preferred_element_type=jnp.float32
    )
    grad_vector_rows = jnp.stack(
        [
            jnp.sum(grad_queries.astype(jnp.float32), axis=0),
            jnp.sum(grad_values.astype(jnp.float32), axis=0),
            grad_bias_out,
            grad_bias_down,
            grad_gain_one,
            grad_shift_one,
            grad_gain_two,
            grad_shift_two,
        ]
    )
    return (
        grad_hidden,
        (
            grad_mat_qkv,
            grad_mat_out,
            grad_mat_up,
            grad_mat_down,
            grad_vector_rows,
            grad_bias_hidden,
        ),
    )


def settle(grad_set):
    matrices = (
        lax.psum_scatter(
            grad_set[0].astype(jnp.bfloat16), "row", scatter_dimension=0, tiled=True
        ).astype(jnp.float32),
        lax.psum_scatter(
            grad_set[1].astype(jnp.bfloat16), "row", scatter_dimension=0, tiled=True
        ).astype(jnp.float32),
        lax.psum_scatter(
            grad_set[2].astype(jnp.bfloat16), "row", scatter_dimension=0, tiled=True
        ).astype(jnp.float32),
        lax.psum_scatter(
            grad_set[3].astype(jnp.bfloat16), "row", scatter_dimension=0, tiled=True
        ).astype(jnp.float32),
    )
    columns = (
        lax.psum_scatter(
            matrices[0].astype(jnp.bfloat16), "col", scatter_dimension=1, tiled=True
        ).astype(jnp.float32),
        lax.psum_scatter(
            matrices[1].astype(jnp.bfloat16), "col", scatter_dimension=1, tiled=True
        ).astype(jnp.float32),
        lax.psum_scatter(
            matrices[2].astype(jnp.bfloat16), "col", scatter_dimension=1, tiled=True
        ).astype(jnp.float32),
        lax.psum_scatter(
            matrices[3].astype(jnp.bfloat16), "col", scatter_dimension=1, tiled=True
        ).astype(jnp.float32),
        lax.psum_scatter(
            grad_set[4].astype(jnp.bfloat16), "col", scatter_dimension=1, tiled=True
        ).astype(jnp.float32),
        lax.psum_scatter(
            grad_set[5].astype(jnp.bfloat16), "col", scatter_dimension=0, tiled=True
        ).astype(jnp.float32),
    )
    smalls = lax.psum((columns[4], columns[5]), "row")
    return (columns[0], columns[1], columns[2], columns[3], smalls[0], smalls[1])


def shards(
    tokens,
    seg_ids,
    pad_mask,
    rand_blocks,
    w_qkv,
    w_out,
    w_up,
    w_down,
    layer_vectors,
    bias_up,
    d_out,
):
    micro_count = tokens.shape[0]
    layer_count = w_qkv.shape[0]
    parity = lax.axis_index("col") % 2

    def fetch_layer(layer_idx):
        columns = (
            lax.all_gather(w_qkv[layer_idx], "col", axis=1, tiled=True),
            lax.all_gather(w_out[layer_idx], "col", axis=1, tiled=True),
            lax.all_gather(w_up[layer_idx], "col", axis=1, tiled=True),
            lax.all_gather(w_down[layer_idx], "col", axis=1, tiled=True),
            lax.all_gather(layer_vectors[layer_idx], "col", axis=1, tiled=True),
            lax.all_gather(bias_up[layer_idx], "col", axis=0, tiled=True),
        )
        matrices = (
            lax.all_gather(columns[0], "row", axis=0, tiled=True),
            lax.all_gather(columns[1], "row", axis=0, tiled=True),
            lax.all_gather(columns[2], "row", axis=0, tiled=True),
            lax.all_gather(columns[3], "row", axis=0, tiled=True),
        )
        return (
            matrices[0],
            matrices[1],
            matrices[2],
            matrices[3],
            columns[4].astype(jnp.float32),
            columns[5].astype(jnp.float32),
        )

    totals = [None] * layer_count
    outputs = []
    input_grads = []
    for micro_idx in range(micro_count):
        own_marks = (seg_ids[micro_idx], pad_mask[micro_idx], rand_blocks[micro_idx])
        mark_rows = jnp.stack([seg_ids[micro_idx], pad_mask[micro_idx]]).astype(jnp.bfloat16)
        hidden = tokens[micro_idx]
        allowed = None
        kept_layers = []
        for layer_idx in range(layer_count):
            weights = fetch_layer(layer_idx)
            final_out, saved_set, allowed = layer_forward(
                hidden, weights, mark_rows, own_marks, allowed, parity
            )
            kept_layers.append(saved_set)
            hidden = final_out.astype(jnp.bfloat16)
        outputs.append(hidden)
        grad_flow = d_out[micro_idx].astype(jnp.float32)
        for layer_idx in reversed(range(layer_count)):
            weights = fetch_layer(layer_idx)
            grad_flow, grad_set = layer_backward(
                grad_flow, weights, kept_layers[layer_idx], allowed, parity
            )
            totals[layer_idx] = (
                grad_set
                if totals[layer_idx] is None
                else jax.tree.map(jnp.add, totals[layer_idx], grad_set)
            )
        input_grads.append(grad_flow)
    totals = [settle(layer_sum) for layer_sum in totals]

    def collect(member):
        return jnp.stack([totals[layer_idx][member] for layer_idx in range(layer_count)])

    return (
        jnp.stack(outputs),
        jnp.stack(input_grads),
        collect(0),
        collect(1),
        collect(2),
        collect(3),
        collect(4),
        collect(5),
    )


def solution(mesh):
    in_specs = (
        P(None, ("row", "col"), None),
        P(None, ("row", "col")),
        P(None, ("row", "col")),
        P(None, ("row", "col"), None),
        P(None, "row", "col"),
        P(None, "row", "col"),
        P(None, "row", "col"),
        P(None, "row", "col"),
        P(None, None, "col"),
        P(None, "col"),
        P(None, ("row", "col"), None),
    )
    out_specs = (
        P(None, ("row", "col"), None),
        P(None, ("row", "col"), None),
        P(None, "row", "col"),
        P(None, "row", "col"),
        P(None, "row", "col"),
        P(None, "row", "col"),
        P(None, None, "col"),
        P(None, "col"),
    )
    return jax.shard_map(shards, mesh=mesh, in_specs=in_specs, out_specs=out_specs, check_vma=False)
```

profile of v0, /device:TPU:0, one launch (start us, length us, event | category | flops | bytes accessed | tf_op | source)
XLA Modules:
  0.0 1949.5 jit_solution(10381244715600672308)
XLA Ops:
  8.4 25.8 %all-gather = bf16[1,96,2304]{1,0,2:T(2,128)(2,1)S(1)} all-gather(bf16[1,96,576]{1,0,2:T(2,128)(2,1)S(1)} %copy.224), channel_id=2, replica_groups=mesh['row'=8,'col'=4] {'col'}, dimensions={2}, use_global_device_ids=true | all-gather | bytes 552960 | tf_op jit(solution)/shard_map/all_gather | solution.py:376
  52.2 17.2 all-gather.5
  70.1 17.4 all-gather.8
  87.8 19.6 %all-gather.10 = bf16[1,96,2304]{1,0,2:T(2,128)(2,1)S(1)} all-gather(bf16[1,96,576]{1,0,2:T(2,128)(2,1)S(1)} %copy.227), channel_id=12, replica_groups=mesh['row'=8,'col'=4] {'col'}, dimensions={2}, use_global_device_ids=true | all-gather | bytes 552960 | tf_op jit(solution)/shard_map/all_gather | solution.py:376
  109.9 14.8 all-gather.13
  128.5 17.1 all-gather.15
  160.7 19.9 %slice_reduce_fusion.9 = (f32[768]{0:T(1024)}, f32[768]{0:T(1024)}, f32[768]{0:T(1024)}, f32[768]{0:T(1024)}, f32[768]{0:T(1024)}, /*index=5*/f32[768]{0:T(1024)S(1)}, f32[768]{0:T(1024)S(1)}, f32[768]{0:T(1024)}) fusion(f32[1,8,768]{1,0,2:T(1,128)S(1)} %convert_element_type.682), kind=kLoop, calls=%fused_computation.478 | loop fusion | bytes 49152 | tf_op jit(solution)/shard_map/slice | solution.py:209
  182.6 14.6 all-gather.12
  197.6 19.9 %slice_reduce_fusion.1 = (f32[768]{0:T(1024)}, f32[768]{0:T(1024)}, f32[768]{0:T(1024)}, f32[768]{0:T(1024)}, f32[768]{0:T(1024)}, /*index=5*/f32[768]{0:T(1024)}, f32[768]{0:T(1024)}, f32[768]{0:T(1024)}) fusion(f32[1,8,768]{1,0,2:T(1,128)S(1)} %convert_element_type.684), kind=kLoop, calls=%fused_computation.470 | loop fusion | bytes 49152 | tf_op jit(solution)/shard_map/slice | solution.py:209
  282.0 71.2 %while.114 = (s32[]{:T(128)}, bf16[6,512,128]{1,2,0:T(8,128)(2,1)}, f32[6,2,512]{2,1,0:T(2,128)}, bf16[6,1024,128]{1,2,0:T(8,128)(2,1)S(1)}, bf16[6,512,128]{1,2...) while((s32[]{:T(128)}, bf16[6,512,128]{1,2,0:T(8,128)(2,1)}, ...), condition=%wide.region_25.26_spmd.clone, body=%wide.region_22.25_spmd.clone.sunk | while | flops 286784512 | bytes 19187484 | solution.py:127
  367.5 72.1 %while.112 = (s32[]{:T(128)}, bf16[6,512,128]{1,2,0:T(8,128)(2,1)}, f32[6,2,512]{2,1,0:T(2,128)}, bf16[6,1024,128]{1,2,0:T(8,128)(2,1)}, bf16[6,512,128]{1,2,0:T...) while((s32[]{:T(128)}, bf16[6,512,128]{1,2,0:T(8,128)(2,1)}, ...), condition=%wide.region_6.7_spmd.clone, body=%wide.region_3.6_spmd.clone.sunk | while | flops 286784512 | bytes 19187484 | solution.py:127
  483.7 30.4 %all-gather.18 = bf16[1,384,768]{1,2,0:T(8,128)(2,1)} all-gather(bf16[1,384,192]{1,2,0:T(8,128)(2,1)S(1)} %copy-done.97), channel_id=20, replica_groups=mesh['row'=8,'col'=4] {'col'}, dimensions={2}, use_global_device_ids=true | all-gather | bytes 737280 | tf_op jit(solution)/shard_map/all_gather | solution.py:379
  549.9 71.6 %while.115 = (s32[]{:T(128)}, bf16[6,512,128]{1,2,0:T(8,128)(2,1)}, f32[6,2,512]{2,1,0:T(2,128)}, bf16[6,1024,128]{1,2,0:T(8,128)(2,1)}, bf16[6,512,128]{1,2,0:T...) while((s32[]{:T(128)}, bf16[6,512,128]{1,2,0:T(8,128)(2,1)}, ...), condition=%wide.region_33.34_spmd.clone, body=%wide.region_30.33_spmd.clone.sunk | while | flops 286784512 | bytes 19187484 | solution.py:127
  629.7 68.2 %while.113 = (s32[]{:T(128)}, bf16[6,512,128]{1,2,0:T(8,128)(2,1)}, f32[6,2,512]{2,1,0:T(2,128)S(1)}, bf16[6,1024,128]{1,2,0:T(8,128)(2,1)}, bf16[6,512,128]{1,2...) while((s32[]{:T(128)}, bf16[6,512,128]{1,2,0:T(8,128)(2,1)}, ...), condition=%wide.region_14.15_spmd.clone, body=%wide.region_11.14_spmd.clone.sunk | while | flops 286784512 | bytes 19186976 | solution.py:127
  768.0 131.9 %while.118 = (s32[]{:T(128)}, bf16[6,512,128]{1,2,0:T(8,128)(2,1)}, f32[6,1024,128]{1,2,0:T(8,128)}, f32[6,1024,128]{1,2,0:T(8,128)}, bf16[6,1024,128]{1,2,0:T(8...) while((s32[]{:T(128)}, bf16[6,512,128]{1,2,0:T(8,128)(2,1)}, ...), condition=%wide.region_58.59_spmd.clone, body=%wide.region_56.58_spmd.clone.sunk | while | flops 692845568 | bytes 58898268 | solution.py:168
  918.7 126.2 %while.116 = (s32[]{:T(128)}, bf16[6,512,128]{1,2,0:T(8,128)(2,1)}, f32[6,1024,128]{1,2,0:T(8,128)}, f32[6,1024,128]{1,2,0:T(8,128)}, bf16[6,1024,128]{1,2,0:T(8...) while((s32[]{:T(128)}, bf16[6,512,128]{1,2,0:T(8,128)(2,1)}, ...), condition=%wide.region_44.45_spmd.clone, body=%wide.region_42.44_spmd.clone.sunk | while | flops 692845568 | bytes 58898268 | solution.py:168
  1122.7 132.3 %while.119 = (s32[]{:T(128)}, bf16[6,512,128]{1,2,0:T(8,128)(2,1)}, f32[6,1024,128]{1,2,0:T(8,128)}, f32[6,1024,128]{1,2,0:T(8,128)}, bf16[6,1024,128]{1,2,0:T(8...) while((s32[]{:T(128)}, bf16[6,512,128]{1,2,0:T(8,128)(2,1)}, ...), condition=%wide.region_65.66_spmd.clone, body=%wide.region_63.65_spmd.clone.sunk | while | flops 692845568 | bytes 58898268 | solution.py:168
  1273.4 129.1 %while.117 = (s32[]{:T(128)}, bf16[6,512,128]{1,2,0:T(8,128)(2,1)S(1)}, f32[6,1024,128]{1,2,0:T(8,128)}, f32[6,1024,128]{1,2,0:T(8,128)}, bf16[6,1024,128]{1,2,0...) while((s32[]{:T(128)}, ...), condition=%wide.region_51.52_spmd.clone, body=%wide.region_49.51_spmd.clone.sunk | while | flops 692845568 | bytes 58897760 | solution.py:168
  1505.1 44.6 %reduce-scatter.53.cloned.1.call-done = bf16[384,768]{1,0:T(8,128)(2,1)} async-done(((bf16[3072,768]{1,0:T(8,128)(2,1)}), bf16[384,768]{1,0:T(8,128)(2,1)}) %reduce-scatter.53.cloned.1.call-update) | async-done | bytes 589840 | tf_op jit(solution)/shard_map/reduce_scatter | solution.py:329
  1551.8 55.4 %reduce-scatter.51.cloned.1.call-done = bf16[384,768]{1,0:T(8,128)(2,1)} async-done(((bf16[3072,768]{1,0:T(8,128)(2,1)}), bf16[384,768]{1,0:T(8,128)(2,1)}) %reduce-scatter.51.cloned.1.call-update) | async-done | bytes 589840 | tf_op jit(solution)/shard_map/reduce_scatter | solution.py:329
  1612.0 52.4 %reduce-scatter.47.cloned.1.call-done = bf16[96,3072]{1,0:T(8,128)(2,1)} async-done(((bf16[768,3072]{1,0:T(8,128)(2,1)}), bf16[96,3072]{1,0:T(8,128)(2,1)}) %reduce-scatter.47.cloned.1.call-update) | async-done | bytes 589840 | tf_op jit(solution)/shard_map/reduce_scatter | solution.py:326
  1664.5 18.9 all-reduce.3
  1693.8 48.1 %reduce-scatter.43.cloned.1.call-done = bf16[96,3072]{1,0:T(8,128)(2,1)} async-done(((bf16[768,3072]{1,0:T(8,128)(2,1)}), bf16[96,3072]{1,0:T(8,128)(2,1)}) %reduce-scatter.43.cloned.1.call-update) | async-done | bytes 589840 | tf_op jit(solution)/shard_map/reduce_scatter | solution.py:326
  1748.5 15.0 reduce-scatter.67.cloned.1.call-done
  1764.4 22.4 %all-reduce.2 = (f32[1,8,192]{2,1,0:T(8,128)S(1)}, f32[1,8,192]{2,1,0:T(8,128)S(1)}, f32[1,768]{1,0:T(1,128)S(1)}, f32[1,768]{1,0:T(1,128)S(1)}) all-reduce(f32[1,8,192]{2,1,0:T(8,128)S(1)} %bitcast_convert_fusion, f32[1,8,192]{2,1,0:T(8,128)S(1)} %bitcast_convert_fusion.1, ...), channel_id=1, replica_groups=mesh['row'=8,'col'=4] {'row'}, use_global_device_ids=true, to_apply=%region_117.118 | all-reduce | flops 4608 | bytes 36864 | tf_op jit(solution)/shard_map/psum | solution.py:353
  1788.9 15.4 reduce-scatter.59.cloned.1.call-done
  1805.9 21.4 %reduce-scatter.37.cloned.1.call-done = bf16[96,576]{0,1:T(8,128)(2,1)} async-done(((bf16[96,2304]{0,1:T(8,128)(2,1)}), bf16[96,576]{0,1:T(8,128)(2,1)}) %reduce-scatter.37.cloned.1.call-update) | async-done | bytes 110608 | tf_op jit(solution)/shard_map/reduce_scatter | solution.py:334
  1827.3 23.2 %reduce-scatter.35.cloned.1.call-done = bf16[96,576]{0,1:T(8,128)(2,1)} async-done(((bf16[96,2304]{0,1:T(8,128)(2,1)}), bf16[96,576]{0,1:T(8,128)(2,1)}) %reduce-scatter.35.cloned.1.call-update) | async-done | bytes 110608 | tf_op jit(solution)/shard_map/reduce_scatter | solution.py:334
  1852.6 20.7 %reduce-scatter.65.cloned.1.call-done = bf16[192,384]{1,0:T(8,128)(2,1)} async-done(((bf16[768,384]{1,0:T(8,128)(2,1)}), bf16[192,384]{1,0:T(8,128)(2,1)}) %reduce-scatter.65.cloned.1.call-update) | async-done | bytes 147472
  1874.4 21.4 %reduce-scatter.63.cloned.1.call-done = bf16[192,384]{1,0:T(8,128)(2,1)} async-done(((bf16[768,384]{1,0:T(8,128)(2,1)}), bf16[192,384]{1,0:T(8,128)(2,1)}) %reduce-scatter.63.cloned.1.call-update) | async-done | bytes 147472
  1898.0 20.4 %reduce-scatter.49.cloned.1.call-done = bf16[96,768]{1,0:T(8,128)(2,1)} async-done(((bf16[96,3072]{1,0:T(8,128)(2,1)}), bf16[96,768]{1,0:T(8,128)(2,1)}) %reduce-scatter.49.cloned.1.call-update) | async-done | bytes 147472 | tf_op jit(solution)/shard_map/reduce_scatter | solution.py:340
  1918.4 22.5 %reduce-scatter.45.cloned.1.call-done = bf16[96,768]{1,0:T(8,128)(2,1)} async-done(((bf16[96,3072]{1,0:T(8,128)(2,1)}), bf16[96,768]{1,0:T(8,128)(2,1)}) %reduce-scatter.45.cloned.1.call-update) | async-done | bytes 147472 | tf_op jit(solution)/shard_map/reduce_scatter | solution.py:340
  (1471 shorter events, 1327.5 us)
Async XLA Ops:
  7.2 226.8 %all-gather.29.cloned.1.call-start = ((), (), s32[]{:S(2)}) async-start(), calls=%async_computation.28 | async-start | bytes 3981312 | tf_op jit(solution)/shard_map/all_gather | solution.py:384
  36.5 319.6 %all-gather.31.cloned.1.call-start = ((), (), s32[]{:S(2)}) async-start(), calls=%async_computation.29 | async-start | bytes 1327104 | tf_op jit(solution)/shard_map/all_gather | solution.py:385
  52.1 392.8 %all-gather.33.cloned.1.call-start = ((), (), s32[]{:S(2)}) async-start(), calls=%async_computation.30 | async-start | bytes 5308416 | tf_op jit(solution)/shard_map/all_gather | solution.py:386
  69.4 391.1 %all-gather.35.cloned.1.call-start = ((), (), s32[]{:S(2)}) async-start(), calls=%async_computation.31 | async-start | bytes 5308416 | tf_op jit(solution)/shard_map/all_gather | solution.py:387
  87.6 384.3 %all-gather.37.cloned.1.call-start = ((), (), s32[]{:S(2)}) async-start(), calls=%async_computation.32 | async-start | bytes 3981312 | tf_op jit(solution)/shard_map/all_gather | solution.py:384
  109.7 588.2 %all-gather.39.cloned.1.call-start = ((), (), s32[]{:S(2)}) async-start(), calls=%async_computation.33 | async-start | bytes 1327104 | tf_op jit(solution)/shard_map/all_gather | solution.py:385
  125.6 579.4 %all-gather.41.cloned.1.call-start = ((), (), s32[]{:S(2)}) async-start(), calls=%async_computation.34 | async-start | bytes 5308416 | tf_op jit(solution)/shard_map/all_gather | solution.py:386
  126.3 105.3 %collective-permute-start.1 = (bf16[2,512]{1,0:T(2,128)(2,1)S(1)}, bf16[2,512]{1,0:T(2,128)(2,1)S(1)}, u32[]{:S(2)}, u32[]{:S(2)}) collective-permute-start(bf16[2,512]{1,0:T(2,128)(2,1)S(1)} %pad_maximum_fusion.16), channel_id=1, source_target_pairs={{0,1},{1,0},{2,3},{3,2},{4,5},{5,4},{6,7},{7,6},{8,9},{9,8},{10,11... | collective-permute-start | bytes 6152 | tf_op jit(solution)/shard_map/ppermute | solution.py:23
  127.9 103.7 %collective-permute-start.6 = (bf16[2,512]{1,0:T(2,128)(2,1)S(1)}, bf16[2,512]{1,0:T(2,128)(2,1)S(1)}, u32[]{:S(2)}, u32[]{:S(2)}) collective-permute-start(bf16[2,512]{1,0:T(2,128)(2,1)S(1)} %pad_maximum_fusion.17), channel_id=1, source_target_pairs={{0,1},{1,0},{2,3},{3,2},{4,5},{5,4},{6,7},{7,6},{8,9},{9,8},{10,11... | collective-permute-start | bytes 6152 | tf_op jit(solution)/shard_map/ppermute | solution.py:23
  145.6 574.0 %all-gather.43.cloned.1.call-start = ((), (), s32[]{:S(2)}) async-start(), calls=%async_computation.35 | async-start | bytes 5308416 | tf_op jit(solution)/shard_map/all_gather | solution.py:387
  258.7 100.8 %collective-permute-start.2 = (bf16[512,768]{1,0:T(8,128)(2,1)}, bf16[512,768]{1,0:T(8,128)(2,1)}, u32[]{:S(2)}, u32[]{:S(2)}) collective-permute-start(bf16[512,768]{1,0:T(8,128)(2,1)} %slice.597), channel_id=1, source_target_pairs={{0,1},{1,0},{2,3},{3,2},{4,5},{5,4},{6,7},{7,6},{8,9},{9,8},{10,11... | collective-permute-start | bytes 2359304 | tf_op jit(solution)/shard_map/ppermute | solution.py:23
  514.1 982.6 %reduce-scatter.41.cloned.1.call-start = ((), (), s32[]{:S(2)}) async-start(), calls=%async_computation.21 | async-start | bytes 1327104 | tf_op jit(solution)/shard_map/reduce_scatter | solution.py:323
  906.4 167.6 %collective-permute-start.14 = (bf16[512,768]{0,1:T(8,128)(2,1)}, bf16[512,768]{0,1:T(8,128)(2,1)}, u32[]{:S(2)}, u32[]{:S(2)}) collective-permute-start(bf16[512,768]{0,1:T(8,128)(2,1)} %bitcast.98), channel_id=1, source_target_pairs={{0,1},{1,0},{2,3},{3,2},{4,5},{5,4},{6,7},{7,6},{8,9},{9,8},{10,11... | collective-permute-start | bytes 2359304 | tf_op jit(solution)/shard_map/ppermute | solution.py:23
  907.7 168.1 %collective-permute-start.15 = (bf16[512,768]{0,1:T(8,128)(2,1)}, bf16[512,768]{0,1:T(8,128)(2,1)}, u32[]{:S(2)}, u32[]{:S(2)}) collective-permute-start(bf16[512,768]{0,1:T(8,128)(2,1)} %bitcast.101), channel_id=1, source_target_pairs={{0,1},{1,0},{2,3},{3,2},{4,5},{5,4},{6,7},{7,6},{8,9},{9,8},{10,11... | collective-permute-start | bytes 2359304 | tf_op jit(solution)/shard_map/ppermute | solution.py:23
  1054.8 443.7 %reduce-scatter.39.cloned.1.call-start = ((), (), s32[]{:S(2)}) async-start(), calls=%async_computation.20 | async-start | bytes 1327104 | tf_op jit(solution)/shard_map/reduce_scatter | solution.py:323
  1117.6 382.8 %reduce-scatter.57.cloned.1.call-start = ((), (), s32[]{:S(2)}) async-start(), calls=%async_computation.37 | async-start | bytes 3981312
  1258.0 156.2 %collective-permute-start.17 = (bf16[512,768]{0,1:T(8,128)(2,1)}, bf16[512,768]{0,1:T(8,128)(2,1)}, u32[]{:S(2)}, u32[]{:S(2)}) collective-permute-start(bf16[512,768]{0,1:T(8,128)(2,1)} %bitcast.112), channel_id=1, source_target_pairs={{0,1},{1,0},{2,3},{3,2},{4,5},{5,4},{6,7},{7,6},{8,9},{9,8},{10,11... | collective-permute-start | bytes 2359304 | tf_op jit(solution)/shard_map/ppermute | solution.py:23
  1269.0 233.7 %reduce-scatter.55.cloned.1.call-start = ((), (), s32[]{:S(2)}) async-start(), calls=%async_computation.36 | async-start | bytes 3981312
  1444.6 105.0 %reduce-scatter.53.cloned.1.call-start = ((), (), s32[]{:S(2)}) async-start(), calls=%async_computation.27 | async-start | bytes 5308416 | tf_op jit(solution)/shard_map/reduce_scatter | solution.py:329
  1454.3 153.0 %reduce-scatter.51.cloned.1.call-start = ((), (), s32[]{:S(2)}) async-start(), calls=%async_computation.26 | async-start | bytes 5308416 | tf_op jit(solution)/shard_map/reduce_scatter | solution.py:329
  1464.6 199.9 %reduce-scatter.47.cloned.1.call-start = ((), (), s32[]{:S(2)}) async-start(), calls=%async_computation.24 | async-start | bytes 5308416 | tf_op jit(solution)/shard_map/reduce_scatter | solution.py:326
  1475.3 211.3 %reduce-scatter.69.cloned.1.call-start = ((), (), s32[]{:S(2)}) async-start(), calls=%async_computation.43 | async-start | bytes 245760
  1486.1 255.8 %reduce-scatter.43.cloned.1.call-start = ((), (), s32[]{:S(2)}) async-start(), calls=%async_computation.22 | async-start | bytes 5308416 | tf_op jit(solution)/shard_map/reduce_scatter | solution.py:326
  1494.0 269.5 %reduce-scatter.67.cloned.1.call-start = ((), (), s32[]{:S(2)}) async-start(), calls=%async_computation.42 | async-start | bytes 245760
  1496.7 291.3 %reduce-scatter.61.cloned.1.call-start = ((), (), s32[]{:S(2)}) async-start(), calls=%async_computation.39 | async-start | bytes 245760
  1498.5 305.8 %reduce-scatter.59.cloned.1.call-start = ((), (), s32[]{:S(2)}) async-start(), calls=%async_computation.38 | async-start | bytes 245760
  1500.3 327.0 %reduce-scatter.37.cloned.1.call-start = ((), (), s32[]{:S(2)}) async-start(), calls=%async_computation.19 | async-start | bytes 737280 | tf_op jit(solution)/shard_map/reduce_scatter | solution.py:334
  1502.6 347.9 %reduce-scatter.35.cloned.1.call-start = ((), (), s32[]{:S(2)}) async-start(), calls=%async_computation.18 | async-start | bytes 737280 | tf_op jit(solution)/shard_map/reduce_scatter | solution.py:334
  1505.0 368.3 %reduce-scatter.65.cloned.1.call-start = ((), (), s32[]{:S(2)}) async-start(), calls=%async_computation.41 | async-start | bytes 737280
  1551.8 344.0 %reduce-scatter.63.cloned.1.call-start = ((), (), s32[]{:S(2)}) async-start(), calls=%async_computation.40 | async-start | bytes 737280
  1609.4 309.0 %reduce-scatter.49.cloned.1.call-start = ((), (), s32[]{:S(2)}) async-start(), calls=%async_computation.25 | async-start | bytes 737280 | tf_op jit(solution)/shard_map/reduce_scatter | solution.py:340
  1664.5 276.4 %reduce-scatter.45.cloned.1.call-start = ((), (), s32[]{:S(2)}) async-start(), calls=%async_computation.23 | async-start | bytes 737280 | tf_op jit(solution)/shard_map/reduce_scatter | solution.py:340
  (228 other events, 2654.4 us)
Sparse Core Ops, SparseCore 0:
  36.6 34.8 all-gather.28
  73.9 24.0 all-gather.30
  99.9 38.9 all-gather.32
  140.6 39.7 all-gather.34
  182.7 33.9 all-gather.36
  218.4 24.0 all-gather.38
  244.4 38.9 all-gather.40
  514.2 39.1 all-gather.42
  1055.0 36.1 reduce-scatter.40
  1117.7 36.1 reduce-scatter.38
  1269.1 47.8 reduce-scatter.56
  1444.7 47.5 reduce-scatter.54
  1495.7 53.8 reduce-scatter.52
  1553.3 53.8 reduce-scatter.50
  1610.5 53.8 reduce-scatter.46
  1667.2 19.3 reduce-scatter.68
  1690.0 51.9 reduce-scatter.42
  1744.1 19.3 reduce-scatter.66
  1766.3 17.5 reduce-scatter.60
  1786.7 17.5 reduce-scatter.58
  1807.2 20.1 reduce-scatter.36
  1830.2 20.3 reduce-scatter.34
  1852.9 20.4 reduce-scatter.64
  1875.5 20.2 reduce-scatter.62
  1898.1 20.2 reduce-scatter.48
  1920.6 20.2 reduce-scatter.44
where the time goes:
time: 1970 us; the launch traced here: 1950 us
  local copies, waits for them, and re-layouts  498 us (25%)
  matrix products  488 us (25%)
  waiting for transfers between devices  396 us (20%)
  other arithmetic  271 us (14%)
  blocking collectives  254 us (13%)
  starting transfers between devices  20.3 us (1%)
    dynamic_slice x144, local copies, waits for them, and re-layouts, attend_forward(): lax.map(one_group, (to_groups(queries), to_groups(key_rows), to_groups(va...  131 us
    or x48, other arithmetic, key_pattern(): return allowed | (query_pos[:, None] == places[None, :])  113 us
    reduce_scatter x2, waiting for transfers between devices, settle(): lax.psum_scatter(grad_set[2].astype(jnp.bfloat16), 'row', scatter_dimensi...  101 us
    reduce_scatter x2, waiting for transfers between devices, settle(): lax.psum_scatter(grad_set[3].astype(jnp.bfloat16), 'row', scatter_dimensi...  99.9 us
    dot_general x24, matrix products, one_group(): jnp.einsum('qge,kge->gqk', grad_heads, value_heads, preferred_element_typ...  98.8 us
    dot_general x48, matrix products, group_scores(): jnp.einsum('qge,kge->gqk', query_heads, key_heads, preferred_element_type...  90.6 us
    reshape x48, local copies, waits for them, and re-layouts, key_pattern(): random_hit = jnp.broadcast_to(hit_table[:, None, :, None], (half_rows //...  77.4 us
    unnamed x34, waiting for transfers between devices  76 us
  transfers between devices with their start and end apart: 44, of which 19 were waited for; matrix products, arithmetic and copies ran while one was open for 54% of the time, Pallas kernels for 0%

commit v1 on v0

v1 whole, which is shorter than its diff:
```python
import functools
import jax
import jax.numpy as jnp
from jax import lax
from jax.experimental import pallas as pl
from jax.experimental.pallas import tpu as pltpu
from jax.sharding import PartitionSpec as P

HEAD = 64
PAIR = 2 * HEAD
TILE = 128
UNROLL = 6
UNROLL_BACK = 6
WIDTHS = (3, 4, 5, 6, 8)
SCALE = HEAD ** (-0.5)
NT = (((1,), (1,)), ((), ()))
F32 = jnp.float32
BF16 = jnp.bfloat16


def stack_heads(rows):
    first = lax.broadcasted_iota(jnp.int32, rows.shape, 1) < HEAD
    zero = jnp.zeros_like(rows)
    return jnp.concatenate([jnp.where(first, rows, zero), jnp.where(first, zero, rows)], axis=0)


def unstack_heads(both):
    half = both.shape[1] // 2
    first = lax.broadcasted_iota(jnp.int32, (both.shape[0], half), 0) < HEAD
    return jnp.where(first, both[:, :half], both[:, half:])


def by_width(count, blocks, run):
    low = 0
    for width in WIDTHS:
        width = min(width, blocks)
        if width == low:
            continue
        pl.when((count > low) & (count <= width))(functools.partial(run, width))
        low = width


def attend_kernel(first_ref, count_ref, qkv_ref, bias_ref, mix_ref, lse_ref, vt_ref):
    length, width3 = qkv_ref.shape
    model = width3 // 3
    blocks = length // TILE
    pairs = model // PAIR
    vt_ref[...] = qkv_ref[:, 2 * model :].T

    def one_tile(tile, carry):
        rows = pl.ds(pl.multiple_of(tile * TILE, TILE), TILE)

        def run(width):
            begin = jnp.minimum(first_ref[tile], blocks - width)
            keys = pl.ds(pl.multiple_of(begin * TILE, TILE), width * TILE)

            def one_pair(pair):
                cols = pl.ds(pl.multiple_of(pair * PAIR, PAIR), PAIR)
                k_cols = pl.ds(pl.multiple_of(model + pair * PAIR, PAIR), PAIR)
                both_q = stack_heads(qkv_ref[rows, cols] * SCALE)
                bias = bias_ref[keys, rows]
                scores = lax.dot_general(
                    qkv_ref[keys, k_cols], both_q, NT, preferred_element_type=F32
                ) + jnp.concatenate([bias, bias], axis=1)
                peak = jnp.max(scores, axis=0, keepdims=True)
                exponent = jnp.exp(scores - peak)
                total = jnp.sum(exponent, axis=0, keepdims=True)
                mixed = jnp.dot(
                    vt_ref[cols, keys], exponent.astype(BF16), preferred_element_type=F32
                )
                mixed = unstack_heads(mixed / total)
                mix_ref[rows, cols] = mixed.T.astype(BF16)
                lse_ref[pair, pl.ds(tile, 1), :] = peak + jnp.log(total)

            def some_pairs(step, carry):
                for offset in range(UNROLL):
                    one_pair(step * UNROLL + offset)
                return carry

            lax.fori_loop(0, pairs // UNROLL, some_pairs, 0)

        by_width(count_ref[tile], blocks, run)
        return carry

    lax.fori_loop(0, blocks, one_tile, 0)


def attend_back_kernel(
    first_ref, count_ref, qkv_ref, grad_ref, bias_ref, lse_ref, out_ref, kt_ref, dk_ref, dv_ref
):
    length, width3 = qkv_ref.shape
    model = width3 // 3
    blocks = length // TILE
    pairs = model // PAIR
    kt_ref[...] = qkv_ref[:, model : 2 * model].T
    dk_ref[...] = jnp.zeros_like(dk_ref)
    dv_ref[...] = jnp.zeros_like(dv_ref)

    def one_tile(tile, carry):
        rows = pl.ds(pl.multiple_of(tile * TILE, TILE), TILE)

        def run(width):
            begin = jnp.minimum(first_ref[tile], blocks - width)
            keys = pl.ds(pl.multiple_of(begin * TILE, TILE), width * TILE)

            def one_pair(pair):
                cols, k_cols, v_cols = (
                    pl.ds(pl.multiple_of(part * model + pair * PAIR, PAIR), PAIR)
                    for part in range(3)
                )
                both_q = stack_heads(qkv_ref[rows, cols] * SCALE)
                both_g = stack_heads(grad_ref[rows, cols])
                lse = lse_ref[pair, pl.ds(tile, 1), :]
                bias = bias_ref[keys, rows]
                scores = lax.dot_general(
                    qkv_ref[keys, k_cols], both_q, NT, preferred_element_type=F32
                ) + jnp.concatenate([bias, bias], axis=1)
                prob = jnp.exp(scores - lse)
                grad_p = lax.dot_general(
                    qkv_ref[keys, v_cols], both_g, NT, preferred_element_type=F32
                )
                delta = jnp.sum(grad_p * prob, axis=0, keepdims=True)
                grad_s = (prob * (grad_p - delta)).astype(BF16)
                dv = jnp.dot(prob.astype(BF16), both_g, preferred_element_type=F32)
                dk = jnp.dot(grad_s, both_q, preferred_element_type=F32)
                grad_q = jnp.dot(kt_ref[cols, keys], grad_s, preferred_element_type=F32)
                return (cols, dv, dk, (unstack_heads(grad_q) * SCALE).T.astype(BF16))

            def some_pairs(step, carry):
                done = [one_pair(step * UNROLL_BACK + offset) for offset in range(UNROLL_BACK)]
                for cols, dv, dk, dq in done:
                    dv_ref[keys, cols] += dv
                    dk_ref[keys, cols] += dk
                    out_ref[rows, cols] = dq
                return carry

            lax.fori_loop(0, pairs // UNROLL_BACK, some_pairs, 0)

        by_width(count_ref[tile], blocks, run)
        return carry

    lax.fori_loop(0, blocks, one_tile, 0)
    out_ref[:, model : 2 * model] = dk_ref[...].astype(BF16)
    out_ref[:, 2 * model :] = dv_ref[...].astype(BF16)


VMEM_SPEC = pl.BlockSpec(memory_space=pltpu.VMEM)
SMEM_SPEC = pl.BlockSpec(memory_space=pltpu.SMEM)


def attend(first, count, qkv, bias):
    length, width3 = qkv.shape
    model = width3 // 3
    pairs, blocks = model // PAIR, length // TILE
    return pl.pallas_call(
        attend_kernel,
        out_shape=(
            jax.ShapeDtypeStruct((length, model), BF16),
            jax.ShapeDtypeStruct((pairs, blocks, 2 * TILE), F32),
        ),
        in_specs=[SMEM_SPEC, SMEM_SPEC, VMEM_SPEC, VMEM_SPEC],
        out_specs=(VMEM_SPEC, VMEM_SPEC),
        scratch_shapes=[pltpu.VMEM((model, length), BF16)],
        compiler_params=pltpu.CompilerParams(vmem_limit_bytes=40 << 20),
    )(first, count, qkv, bias)


def attend_back(first, count, qkv, grad_mix, bias, lse):
    length, width3 = qkv.shape
    model = width3 // 3
    return pl.pallas_call(
        attend_back_kernel,
        out_shape=jax.ShapeDtypeStruct((length, width3), BF16),
        in_specs=[SMEM_SPEC, SMEM_SPEC] + [VMEM_SPEC] * 4,
        out_specs=VMEM_SPEC,
        scratch_shapes=[
            pltpu.VMEM((model, length), BF16),
            pltpu.VMEM((length, model), F32),
            pltpu.VMEM((length, model), F32),
        ],
        compiler_params=pltpu.CompilerParams(vmem_limit_bytes=48 << 20),
    )(first, count, qkv, grad_mix, bias, lse)

NEG_FILL = -1e30
EPS = 1e-06
ROOT_HALF = 0.7071067811865476
INV_ROOT_TAU = 0.3989422804014327
BLOCK = 64


def norm_forward(residual, norm_gain, norm_shift):
    center = residual - jnp.mean(residual, axis=-1, keepdims=True)
    scale_inv = lax.rsqrt(jnp.mean(center * center, axis=-1, keepdims=True) + EPS)
    normed = center * scale_inv
    return (normed * norm_gain + norm_shift, normed, scale_inv)


def norm_backward(grad_y, normed, scale_inv, norm_gain):
    grad_n = grad_y * norm_gain
    return scale_inv * (
        grad_n
        - jnp.mean(grad_n, axis=-1, keepdims=True)
        - normed * jnp.mean(grad_n * normed, axis=-1, keepdims=True)
    )


def gelu_value(pre_act):
    return 0.5 * pre_act * (1.0 + lax.erf(pre_act * ROOT_HALF))


def gelu_slope(pre_act):
    return 0.5 * (1.0 + lax.erf(pre_act * ROOT_HALF)) + pre_act * INV_ROOT_TAU * jnp.exp(
        -0.5 * pre_act * pre_act
    )


def swapped(block):
    count = lax.axis_size("col")
    return lax.ppermute(block, "col", [(i, i ^ 1) for i in range(count)])


def pick(array, index):
    return lax.dynamic_index_in_dim(array, index, 0, keepdims=False)


def to_sequence(halves, parity):
    own = pick(halves, parity)
    other = swapped(pick(halves, 1 - parity))
    first = parity == 0
    return jnp.concatenate([jnp.where(first, own, other), jnp.where(first, other, own)])


def from_sequence(whole, parity, narrow):
    halves = whole.reshape((2, -1) + whole.shape[1:])
    own = pick(halves, parity)
    other = swapped(pick(halves, 1 - parity).astype(narrow)).astype(whole.dtype)
    first = parity == 0
    return jnp.stack([jnp.where(first, own, other), jnp.where(first, other, own)])


def key_pattern(seg, pad, rand):
    length = seg.shape[0]
    places = jnp.arange(length, dtype=jnp.int32)
    starts = jnp.sum((seg[None, :] < seg[:, None]).astype(jnp.int32), axis=1)
    ends = jnp.sum((seg[None, :] <= seg[:, None]).astype(jnp.int32), axis=1)
    whole = places - starts < 2 * BLOCK
    block = places // BLOCK
    chosen = jnp.repeat(rand, BLOCK, axis=0)
    near = jnp.abs(block[:, None] - block[None, :]) <= 1
    hit = jnp.zeros((length, length), bool)
    for slot in range(rand.shape[1]):
        hit = hit | (block[:, None] == chosen[None, :, slot])
    allowed = (
        (seg[:, None] == seg[None, :])
        & (pad[:, None] > 0)
        & (whole[:, None] | whole[None, :] | near | hit)
    )
    allowed = allowed | (places[:, None] == places[None, :])
    bias = jnp.where(allowed, 0.0, NEG_FILL).astype(F32)
    first = starts[::TILE] // TILE
    count = (ends[TILE - 1 :: TILE] + TILE - 1) // TILE - first
    return bias, first, count


def layer_forward(hidden, weights, pattern):
    mat_qkv, mat_out, mat_up, mat_down, vectors, up_bias = weights
    bias, first, count = pattern
    qkv_bias = jnp.concatenate([vectors[0], jnp.zeros_like(vectors[0]), vectors[1]])
    qkv = (jnp.dot(hidden, mat_qkv, preferred_element_type=F32) + qkv_bias).astype(BF16)
    mixture, lse = attend(first, count, qkv, bias)
    branch = jnp.dot(mixture, mat_out, preferred_element_type=F32) + vectors[2]
    first_norm, normed_one, inv_one = norm_forward(
        hidden.astype(F32) + branch, vectors[4], vectors[5]
    )
    first_out = first_norm.astype(BF16)
    pre_act = jnp.dot(first_out, mat_up, preferred_element_type=F32) + up_bias
    act_low = gelu_value(pre_act).astype(BF16)
    down_out = jnp.dot(act_low, mat_down, preferred_element_type=F32) + vectors[3]
    final_out, normed_two, inv_two = norm_forward(
        first_out.astype(F32) + down_out, vectors[6], vectors[7]
    )
    saved = (
        hidden, qkv, lse, mixture, normed_one, inv_one, first_out, pre_act, act_low, normed_two, inv_two,
    )
    return final_out.astype(BF16), saved


def layer_backward(grad_y, weights, saved, pattern):
    mat_qkv, mat_out, mat_up, mat_down, vectors, up_bias = weights
    (
        hidden, qkv, lse, mixture, normed_one, inv_one, first_out, pre_act, act_low, normed_two, inv_two,
    ) = saved
    bias, first, count = pattern
    width = hidden.shape[1]
    grad_gain_two = jnp.sum(grad_y * normed_two, axis=0)
    grad_shift_two = jnp.sum(grad_y, axis=0)
    grad_two = norm_backward(grad_y, normed_two, inv_two, vectors[6])
    grad_down_low = grad_two.astype(BF16)
    grad_bias_down = jnp.sum(grad_down_low.astype(F32), axis=0)
    grad_mat_down = jnp.einsum("tf,td->fd", act_low, grad_down_low, preferred_element_type=F32)
    grad_act = jnp.einsum("td,fd->tf", grad_down_low, mat_down, preferred_element_type=F32)
    grad_pre = (grad_act * gelu_slope(pre_act)).astype(BF16)
    grad_bias_hidden = jnp.sum(grad_pre.astype(F32), axis=0)
    grad_mat_up = jnp.einsum("td,tf->df", first_out, grad_pre, preferred_element_type=F32)
    grad_first = grad_two + jnp.einsum("tf,df->td", grad_pre, mat_up, preferred_element_type=F32)
    grad_gain_one = jnp.sum(grad_first * normed_one, axis=0)
    grad_shift_one = jnp.sum(grad_first, axis=0)
    grad_one = norm_backward(grad_first, normed_one, inv_one, vectors[4])
    grad_branch = grad_one.astype(BF16)
    grad_bias_out = jnp.sum(grad_branch.astype(F32), axis=0)
    grad_mat_out = jnp.einsum("td,te->de", mixture, grad_branch, preferred_element_type=F32)
    grad_mix = jnp.einsum("te,de->td", grad_branch, mat_out, preferred_element_type=F32)
    grad_qkv = attend_back(first, count, qkv, grad_mix.astype(BF16), bias, lse)
    grad_mat_qkv = jnp.einsum("td,te->de", hidden, grad_qkv, preferred_element_type=F32)
    grad_hidden = grad_one + jnp.einsum("te,de->td", grad_qkv, mat_qkv, preferred_element_type=F32)
    bias_qkv = jnp.sum(grad_qkv.astype(F32), axis=0)
    grad_rows = jnp.stack(
        [
            bias_qkv[:width], bias_qkv[2 * width :], grad_bias_out, grad_bias_down,
            grad_gain_one, grad_shift_one, grad_gain_two, grad_shift_two,
        ]
    )
    return grad_hidden, (grad_mat_qkv, grad_mat_out, grad_mat_up, grad_mat_down), grad_rows, grad_bias_hidden


def shards(
    tokens, seg_ids, pad_mask, rand_blocks, w_qkv, w_out, w_up, w_down, layer_vectors, bias_up, d_out
):
    layers = w_qkv.shape[0]
    parity = lax.axis_index("col") % 2
    marks = jnp.concatenate(
        [seg_ids, pad_mask, rand_blocks.reshape(rand_blocks.shape[0], -1)], axis=1
    )
    half = seg_ids.shape[1]
    marks = to_sequence(marks[:, None], parity)
    seg, pad = marks[:, :half].reshape(-1), marks[:, half : 2 * half].reshape(-1)
    rand = marks[:, 2 * half :].reshape(-1, rand_blocks.shape[2])
    pattern = key_pattern(seg, pad, rand)

    def fetch(layer):
        mats = tuple(
            lax.all_gather(
                lax.all_gather(w[layer], "col", axis=1, tiled=True), "row", axis=0, tiled=True
            )
            for w in (w_qkv, w_out, w_up, w_down)
        )
        return mats + (
            lax.all_gather(layer_vectors[layer], "col", axis=1, tiled=True).astype(F32),
            lax.all_gather(bias_up[layer], "col", axis=0, tiled=True).astype(F32),
        )

    weights = [fetch(layer) for layer in range(layers)]
    hidden = to_sequence(tokens, parity)
    kept = []
    for layer in range(layers):
        hidden, saved = layer_forward(hidden, weights[layer], pattern)
        kept.append(saved)
    output = from_sequence(hidden, parity, BF16)
    flow = to_sequence(d_out, parity).astype(F32)
    grads, vec_grads, up_grads = [None] * layers, [None] * layers, [None] * layers
    for layer in reversed(range(layers)):
        flow, mats, vec_grads[layer], up_grads[layer] = layer_backward(
            flow, weights[layer], kept[layer], pattern
        )
        grads[layer] = [
            lax.psum_scatter(
                lax.psum_scatter(m.astype(BF16), "row", scatter_dimension=0, tiled=True),
                "col", scatter_dimension=1, tiled=True,
            ).astype(F32)
            for m in mats
        ]
    d_tokens = from_sequence(flow, parity, BF16)
    vec = lax.psum_scatter(jnp.stack(vec_grads), "col", scatter_dimension=2, tiled=True)
    ups = lax.psum_scatter(jnp.stack(up_grads), "col", scatter_dimension=1, tiled=True)
    vec, ups = lax.psum((vec, ups), "row")
    mats = [jnp.stack([grads[layer][i] for layer in range(layers)]) for i in range(4)]
    return output, d_tokens, *mats, vec, ups


def solution(mesh):
    in_specs = (
        P(None, ("row", "col"), None),
        P(None, ("row", "col")),
        P(None, ("row", "col")),
        P(None, ("row", "col"), None),
        P(None, "row", "col"),
        P(None, "row", "col"),
        P(None, "row", "col"),
        P(None, "row", "col"),
        P(None, None, "col"),
        P(None, "col"),
        P(None, ("row", "col"), None),
    )
    out_specs = (
        P(None, ("row", "col"), None),
        P(None, ("row", "col"), None),
        P(None, "row", "col"),
        P(None, "row", "col"),
        P(None, "row", "col"),
        P(None, "row", "col"),
        P(None, None, "col"),
        P(None, "col"),
    )
    return jax.shard_map(shards, mesh=mesh, in_specs=in_specs, out_specs=out_specs, check_vma=False)
```

time: 1970 us -> 1160 us (0.59); the launches traced: 1950 us -> 1160 us
  local copies, waits for them, and re-layouts: 498 us -> 92.7 us
  matrix products: 488 us -> 193 us
  other arithmetic: 271 us -> 38.7 us
  Pallas kernels: 0 us -> 104 us
  waiting for transfers between devices: 396 us -> 454 us
    dot_general x216 -> x24, matrix products: 488 us -> 193 us  [the longest x2 27.6 us: layer_backward(): jnp.einsum('td,fd->tf', grad_down_low, mat_down, preferred_element_type=F32)]
    dynamic_slice x146 -> x0, local copies, waits for them, and re-layouts: 134 us -> none  [the longest x144 131 us: attend_forward(): lax.map(one_group, (to_groups(queries), to_groups(key_rows), to_groups(va...]
    or x48 -> x0, other arithmetic: 113 us -> none  [key_pattern(): return allowed | (query_pos[:, None] == places[None, :])]
    unnamed x34, waiting for transfers between devices: 76 us -> 186 us
    pallas_call x0 -> x4, Pallas kernels: none -> 104 us  [the longest x2 57.9 us: attend_back(): pl.pallas_call(attend_back_kernel, out_shape=jax.ShapeDtypeStruct((length...]
    reshape x48 -> x4, local copies, waits for them, and re-layouts: 77.4 us -> 0.34 us  [the longest x2 0.16 us: shards(): rand = marks[:, 2 * half:].reshape(-1, rand_blocks.shape[2])]
    convert_element_type x51 -> x4, other arithmetic: 63.5 us -> 2.03 us  [the longest x2 1.22 us: fetch(): lax.all_gather(bias_up[layer], 'col', axis=0, tiled=True).astype(F32)]
    dynamic_update_slice x72 -> x0, local copies, waits for them, and re-layouts: 54.4 us -> none  [the longest x48 27.9 us: attend_forward(): lax.map(one_group, (to_groups(queries), to_groups(key_rows), to_groups(va...]
  transfers between devices with their start and end apart: 44 -> 31, of which waited for: 19 -> 15; matrix products, arithmetic and copies ran while one was open for 54% -> 23% of each run, Pallas kernels for 0% -> 9%
where the time goes in v1:
time: 1160 us
  waiting for transfers between devices  454 us (39%)
  blocking collectives  254 us (22%)
  matrix products  193 us (17%)
  Pallas kernels  104 us (9%)
  local copies, waits for them, and re-layouts  92.7 us (8%)
  other arithmetic  38.7 us (3%)
  between operations  15.7 us (1%)
    reduce_scatter x8, waiting for transfers between devices, shards(): lax.psum_scatter(m.astype(BF16), 'row', scatter_dimension=0, tiled=True)  225 us
    unnamed x34, waiting for transfers between devices  186 us
    all_gather x8, blocking collectives, fetch(): lax.all_gather(w[layer], 'col', axis=1, tiled=True)  166 us
    pallas_call x2, Pallas kernels, attend_back(): pl.pallas_call(attend_back_kernel, out_shape=jax.ShapeDtypeStruct((length...  57.9 us
    pallas_call x2, Pallas kernels, attend(): pl.pallas_call(attend_kernel, out_shape=(jax.ShapeDtypeStruct((length, mo...  45.8 us
    reduce_scatter x2, waiting for transfers between devices, shards(): lax.psum_scatter(lax.psum_scatter(m.astype(BF16), 'row', scatter_dimensio...  43.1 us
    unnamed x147, local copies, waits for them, and re-layouts  42.6 us
    slice x2, local copies, waits for them, and re-layouts, layer_forward(): vectors[6]  39.8 us
  transfers between devices with their start and end apart: 31, of which 15 were waited for; matrix products, arithmetic and copies ran while one was open for 23% of the time, Pallas kernels for 9%

profile of v1, /device:TPU:0, one launch (start us, length us, event | category | flops | bytes accessed | tf_op | source)
XLA Modules:
  0.0 1159.7 jit_solution(17638717991070834232)
XLA Ops:
  8.5 25.8 %all-gather = bf16[1,96,2304]{1,0,2:T(2,128)(2,1)S(1)} all-gather(bf16[1,96,576]{1,0,2:T(2,128)(2,1)S(1)} %copy.62), channel_id=2, replica_groups=mesh['row'=8,'col'=4] {'col'}, dimensions={2}, use_global_device_ids=true | all-gather | bytes 552960 | tf_op jit(solution)/shard_map/all_gather | solution.py:343
  36.7 14.5 %all-gather.3 = bf16[1,96,768]{1,0,2:T(2,128)(2,1)S(1)} all-gather(bf16[1,96,192]{1,0,2:T(2,128)(2,1)S(1)} %copy.64), channel_id=5, replica_groups=mesh['row'=8,'col'=4] {'col'}, dimensions={2}, use_global_device_ids=true | all-gather | bytes 184320 | tf_op jit(solution)/shard_map/all_gather | solution.py:343
  52.2 17.2 %all-gather.5 = bf16[1,96,3072]{2,1,0:T(8,128)(2,1)} all-gather(bf16[1,96,768]{2,1,0:T(8,128)(2,1)S(1)} %get-tuple-element.106), channel_id=7, replica_groups=mesh['row'=8,'col'=4] {'col'}, dimensions={2}, use_global_device_ids=true | all-gather | bytes 737280 | tf_op jit(solution)/shard_map/all_gather | solution.py:343
  70.2 17.4 %all-gather.8 = bf16[1,384,768]{1,2,0:T(8,128)(2,1)} all-gather(bf16[1,384,192]{1,2,0:T(8,128)(2,1)S(1)} %get-tuple-element.104), channel_id=10, replica_groups=mesh['row'=8,'col'=4] {'col'}, dimensions={2}, use_global_device_ids=true | all-gather | bytes 737280 | tf_op jit(solution)/shard_map/all_gather | solution.py:343
  87.9 19.9 %all-gather.10 = bf16[1,96,2304]{1,0,2:T(2,128)(2,1)S(1)} all-gather(bf16[1,96,576]{1,0,2:T(2,128)(2,1)S(1)} %copy.65), channel_id=12, replica_groups=mesh['row'=8,'col'=4] {'col'}, dimensions={2}, use_global_device_ids=true | all-gather | bytes 552960 | tf_op jit(solution)/shard_map/all_gather | solution.py:343
  110.2 14.6 %all-gather.13 = bf16[1,96,768]{1,0,2:T(2,128)(2,1)S(1)} all-gather(bf16[1,96,192]{1,0,2:T(2,128)(2,1)S(1)} %copy.67), channel_id=15, replica_groups=mesh['row'=8,'col'=4] {'col'}, dimensions={2}, use_global_device_ids=true | all-gather | bytes 184320 | tf_op jit(solution)/shard_map/all_gather | solution.py:343
  125.8 17.8 %all-gather.15 = bf16[1,96,3072]{2,1,0:T(8,128)(2,1)} all-gather(bf16[1,96,768]{2,1,0:T(8,128)(2,1)S(1)} %get-tuple-element.105), channel_id=17, replica_groups=mesh['row'=8,'col'=4] {'col'}, dimensions={2}, use_global_device_ids=true | all-gather | bytes 737280 | tf_op jit(solution)/shard_map/all_gather | solution.py:343
  148.7 39.1 %all-gather.18 = bf16[1,384,768]{1,2,0:T(8,128)(2,1)} all-gather(bf16[1,384,192]{1,2,0:T(8,128)(2,1)S(1)} %copy-done.31), channel_id=20, replica_groups=mesh['row'=8,'col'=4] {'col'}, dimensions={2}, use_global_device_ids=true | all-gather | bytes 737280 | tf_op jit(solution)/shard_map/all_gather | solution.py:343
  202.8 19.9 %slice_reduce_fusion.9 = (f32[768]{0:T(1024)}, f32[768]{0:T(1024)}, f32[768]{0:T(1024)}, f32[768]{0:T(1024)S(1)}, f32[768]{0:T(1024)}, /*index=5*/f32[768]{0:T(1024)S(1)}, f32[768]{0:T(1024)S(1)}, f32[768]{0:T(1024)}) fusion(f32[1,8,768]{1,0,2:T(1,128)S(1)} %convert_element_type.192), kind=kLoop, calls=%fused_computation.141 | loop fusion | bytes 49152 | tf_op jit(solution)/shard_map/slice | solution.py:280
  222.7 24.0 %all-gather.12 = bf16[1,8,768]{1,0,2:T(2,128)(2,1)S(1)} all-gather(bf16[1,8,192]{1,0,2:T(2,128)(2,1)S(1)} %copy.66), channel_id=14, replica_groups=mesh['row'=8,'col'=4] {'col'}, dimensions={2}, use_global_device_ids=true | all-gather | bytes 15360 | tf_op jit(solution)/shard_map/all_gather | solution.py:348
  247.1 19.9 %slice_reduce_fusion.1 = (f32[768]{0:T(1024)S(1)}, f32[768]{0:T(1024)}, f32[768]{0:T(1024)}, f32[768]{0:T(1024)S(1)}, f32[768]{0:T(1024)}, /*index=5*/f32[768]{0:T(1024)S(1)}, f32[768]{0:T(1024)S(1)}, f32[768]{0:T(1024)S(1)}) fusion(f32[1,8,768]{1,0,2:T(1,128)S(1)} %convert_element_type.194), kind=kLoop, calls=%fused_computation.133 | loop fusion | bytes 49152 | tf_op jit(solution)/shard_map/slice | solution.py:280
  312.3 22.9 %shard_map.170 = (bf16[1024,768]{1,0:T(8,128)(2,1)S(1)}, f32[6,8,256]{2,1,0:T(8,128)S(1)}) custom-call(s32[8]{0:T(128)S(1)} %get-tuple-element.93.first_ref, s32[8]{0:T(128)S(1)} %get-tuple-element.92.count_ref, bf16[1024,2304]{1,0:T(8,128)(2,1)S(1)} %add_convert_fusion.1.qkv_ref, f32[1024,1024]{1,0:T(8,128)S(1)} %copy-done), custom_call_target="tpu_custom_call" | custom-call | tf_op jit(solution)/shard_map/pallas_call | solution.py:155
  374.1 22.9 %shard_map.171 = (bf16[1024,768]{1,0:T(8,128)(2,1)S(1)}, f32[6,8,256]{2,1,0:T(8,128)S(1)}) custom-call(s32[8]{0:T(128)S(1)} %get-tuple-element.93.first_ref, s32[8]{0:T(128)S(1)} %get-tuple-element.92.count_ref, bf16[1024,2304]{1,0:T(8,128)(2,1)S(1)} %add_convert_fusion.qkv_ref, f32[1024,1024]{1,0:T(8,128)S(1)} %copy-done.1), custom_call_target="tpu_custom_call" | custom-call | tf_op jit(solution)/shard_map/pallas_call | solution.py:155
  434.4 14.5 %convert_reduce_fusion = (f32[3072]{0:T(1024)S(1)}, bf16[1024,3072]{1,0:T(8,128)(2,1)}) fusion(f32[1024,3072]{1,0:T(8,128)} %get-tuple-element.135, f32[3072]{0:T(1024)S(1)} %bitcast.200, bf16[1,3072,768]{1,2,0:T(8,128)(2,1)S(1)} %copy-done.52, f32[1024,768]{1,0:T(8,128)S(1)} %get-tuple-element.89), kind=kOutput, calls=%fused_computation.12 | convolution fusion | flops 4873516032 | bytes 26763264 | tf_op jit(solution)/shard_map/td,fd->tf/dot_general | solution.py:301
  466.2 29.0 %shard_map.172 = bf16[1024,2304]{1,0:T(8,128)(2,1)} custom-call(s32[8]{0:T(128)S(1)} %get-tuple-element.93.first_ref, s32[8]{0:T(128)S(1)} %get-tuple-element.92.count_ref, bf16[1024,2304]{1,0:T(8,128)(2,1)} %copy-done.5, bf16[1024,768]{1,0:T(8,128)(2,1)S(1)} %convolution_convert_fusion.7.grad_ref, f32[1024,1024]{1,0:T(8,128)S(1)} %copy-done.2, ...), custom_call_target="tpu_custom_call" | custom-call | tf_op jit(solution)/shard_map/pallas_call | solution.py:171
  542.1 29.0 %shard_map.173 = bf16[1024,2304]{1,0:T(8,128)(2,1)} custom-call(s32[8]{0:T(128)S(1)} %get-tuple-element.93.first_ref, s32[8]{0:T(128)S(1)} %get-tuple-element.92.count_ref, bf16[1024,2304]{1,0:T(8,128)(2,1)} %copy-done.4, bf16[1024,768]{1,0:T(8,128)(2,1)S(1)} %convolution_convert_fusion.6.grad_ref, f32[1024,1024]{1,0:T(8,128)S(1)} %copy-done.3, ...), custom_call_target="tpu_custom_call" | custom-call | tf_op jit(solution)/shard_map/pallas_call | solution.py:171
  637.8 29.6 %reduce-scatter.35.cloned.1.call-done = bf16[96,2304]{1,0:T(8,128)(2,1)} async-done(((bf16[768,2304]{1,0:T(8,128)(2,1)}), bf16[96,2304]{1,0:T(8,128)(2,1)}) %reduce-scatter.35.cloned.1.call-update) | async-done | bytes 442384 | tf_op jit(solution)/shard_map/reduce_scatter | solution.py:367
  669.5 55.2 %reduce-scatter.53.cloned.1.call-done = bf16[384,768]{1,0:T(8,128)(2,1)} async-done(((bf16[3072,768]{1,0:T(8,128)(2,1)}), bf16[384,768]{1,0:T(8,128)(2,1)}) %reduce-scatter.53.cloned.1.call-update) | async-done | bytes 589840 | tf_op jit(solution)/shard_map/reduce_scatter | solution.py:367
  726.9 55.4 %reduce-scatter.51.cloned.1.call-done = bf16[384,768]{1,0:T(8,128)(2,1)} async-done(((bf16[3072,768]{1,0:T(8,128)(2,1)}), bf16[384,768]{1,0:T(8,128)(2,1)}) %reduce-scatter.51.cloned.1.call-update) | async-done | bytes 589840 | tf_op jit(solution)/shard_map/reduce_scatter | solution.py:367
  786.2 53.4 %reduce-scatter.47.cloned.1.call-done = bf16[96,3072]{1,0:T(8,128)(2,1)} async-done(((bf16[768,3072]{1,0:T(8,128)(2,1)}), bf16[96,3072]{1,0:T(8,128)(2,1)}) %reduce-scatter.47.cloned.1.call-update) | async-done | bytes 589840 | tf_op jit(solution)/shard_map/reduce_scatter | solution.py:367
  851.1 42.9 %reduce-scatter.69.cloned.1.call-done = f32[768,2]{1,0:T(8,128)} async-done(((f32[3072,2]{1,0:T(8,128)}), f32[768,2]{1,0:T(8,128)}) %reduce-scatter.69.cloned.1.call-update) | async-done | bytes 6160
  895.1 21.2 %reduce-scatter.67.cloned.1.call-done = f32[192,16]{1,0:T(8,128)} async-done(((f32[768,16]{1,0:T(8,128)}), f32[192,16]{1,0:T(8,128)}) %reduce-scatter.67.cloned.1.call-update) | async-done | bytes 12304
  917.5 23.4 %all-reduce = (f32[2,8,192]{2,1,0:T(8,128)}, f32[2,768]{1,0:T(2,128)}) all-reduce(f32[2,8,192]{2,1,0:T(8,128)S(1)} %copy.59, f32[2,768]{1,0:T(2,128)S(1)} %copy.61), channel_id=1, replica_groups=mesh['row'=8,'col'=4] {'row'}, use_global_device_ids=true, to_apply=%region_49.50 | all-reduce | flops 4608 | bytes 36864 | tf_op jit(solution)/shard_map/psum | solution.py:375
  940.9 31.0 %reduce-scatter.43.cloned.1.call-done = bf16[96,3072]{1,0:T(8,128)(2,1)} async-done(((bf16[768,3072]{1,0:T(8,128)(2,1)}), bf16[96,3072]{1,0:T(8,128)(2,1)}) %reduce-scatter.43.cloned.1.call-update) | async-done | bytes 589840 | tf_op jit(solution)/shard_map/reduce_scatter | solution.py:367
  977.9 16.3 %reduce-scatter.61.cloned.1.call-done = bf16[192,96]{1,0:T(8,128)(2,1)} async-done(((bf16[768,96]{1,0:T(8,128)(2,1)}), bf16[192,96]{1,0:T(8,128)(2,1)}) %reduce-scatter.61.cloned.1.call-update) | async-done | bytes 36880
  995.1 18.8 %reduce-scatter.59.cloned.1.call-done = bf16[192,96]{1,0:T(8,128)(2,1)} async-done(((bf16[768,96]{1,0:T(8,128)(2,1)}), bf16[192,96]{1,0:T(8,128)(2,1)}) %reduce-scatter.59.cloned.1.call-update) | async-done | bytes 36880
  1015.5 21.6 %reduce-scatter.57.cloned.1.call-done = bf16[576,96]{1,0:T(8,128)(2,1)} async-done(((bf16[2304,96]{1,0:T(8,128)(2,1)}), bf16[576,96]{1,0:T(8,128)(2,1)}) %reduce-scatter.57.cloned.1.call-update) | async-done | bytes 110608
  1038.1 22.2 %reduce-scatter.55.cloned.1.call-done = bf16[576,96]{1,0:T(8,128)(2,1)} async-done(((bf16[2304,96]{1,0:T(8,128)(2,1)}), bf16[576,96]{1,0:T(8,128)(2,1)}) %reduce-scatter.55.cloned.1.call-update) | async-done | bytes 110608
  1062.3 20.9 %reduce-scatter.65.cloned.1.call-done = bf16[192,384]{1,0:T(8,128)(2,1)} async-done(((bf16[768,384]{1,0:T(8,128)(2,1)}), bf16[192,384]{1,0:T(8,128)(2,1)}) %reduce-scatter.65.cloned.1.call-update) | async-done | bytes 147472
  1084.2 21.6 %reduce-scatter.63.cloned.1.call-done = bf16[192,384]{1,0:T(8,128)(2,1)} async-done(((bf16[768,384]{1,0:T(8,128)(2,1)}), bf16[192,384]{1,0:T(8,128)(2,1)}) %reduce-scatter.63.cloned.1.call-update) | async-done | bytes 147472
  1108.0 20.4 %reduce-scatter.49.cloned.1.call-done = bf16[96,768]{1,0:T(8,128)(2,1)} async-done(((bf16[96,3072]{1,0:T(8,128)(2,1)}), bf16[96,768]{1,0:T(8,128)(2,1)}) %reduce-scatter.49.cloned.1.call-update) | async-done | bytes 147472 | tf_op jit(solution)/shard_map/reduce_scatter | solution.py:366
  1128.4 22.7 %reduce-scatter.45.cloned.1.call-done = bf16[96,768]{1,0:T(8,128)(2,1)} async-done(((bf16[96,3072]{1,0:T(8,128)(2,1)}), bf16[96,768]{1,0:T(8,128)(2,1)}) %reduce-scatter.45.cloned.1.call-update) | async-done | bytes 147472 | tf_op jit(solution)/shard_map/reduce_scatter | solution.py:366
  (346 shorter events, 319.2 us)
Async XLA Ops:
  7.2 297.7 %all-gather.29.cloned.1.call-start = ((), (), s32[]{:S(2)}) async-start(), calls=%async_computation.28 | async-start | bytes 3981312 | tf_op jit(solution)/shard_map/all_gather | solution.py:342
  36.5 300.8 %all-gather.31.cloned.1.call-start = ((), (), s32[]{:S(2)}) async-start(), calls=%async_computation.29 | async-start | bytes 1327104 | tf_op jit(solution)/shard_map/all_gather | solution.py:342
  52.1 290.9 %all-gather.33.cloned.1.call-start = ((), (), s32[]{:S(2)}) async-start(), calls=%async_computation.30 | async-start | bytes 5308416 | tf_op jit(solution)/shard_map/all_gather | solution.py:342
  69.4 286.2 %all-gather.35.cloned.1.call-start = ((), (), s32[]{:S(2)}) async-start(), calls=%async_computation.31 | async-start | bytes 5308416 | tf_op jit(solution)/shard_map/all_gather | solution.py:342
  87.6 279.3 %all-gather.37.cloned.1.call-start = ((), (), s32[]{:S(2)}) async-start(), calls=%async_computation.32 | async-start | bytes 3981312 | tf_op jit(solution)/shard_map/all_gather | solution.py:342
  110.1 289.1 %all-gather.39.cloned.1.call-start = ((), (), s32[]{:S(2)}) async-start(), calls=%async_computation.33 | async-start | bytes 1327104 | tf_op jit(solution)/shard_map/all_gather | solution.py:342
  125.8 279.8 %all-gather.41.cloned.1.call-start = ((), (), s32[]{:S(2)}) async-start(), calls=%async_computation.34 | async-start | bytes 5308416 | tf_op jit(solution)/shard_map/all_gather | solution.py:342
  143.7 274.2 %all-gather.43.cloned.1.call-start = ((), (), s32[]{:S(2)}) async-start(), calls=%async_computation.35 | async-start | bytes 5308416 | tf_op jit(solution)/shard_map/all_gather | solution.py:342
  144.0 150.9 %collective-permute-start.1 = (s32[1,1048]{1,0:T(1,128)S(1)}, s32[1,1048]{1,0:T(1,128)S(1)}, u32[]{:S(2)}, u32[]{:S(2)}) collective-permute-start(s32[1,1048]{1,0:T(1,128)S(1)} %constant_dynamic-slice_fusion), channel_id=1, source_target_pairs={{0,1},{1,0},{2,3},{3,2},{4,5},{5,4},{6,7},{7,6},{8,9},{9,8},{10,11... | collective-permute-start | bytes 12584 | tf_op jit(solution)/shard_map/ppermute | solution.py:219
  145.3 156.0 %collective-permute-start.3 = (bf16[512,768]{1,0:T(8,128)(2,1)S(1)}, bf16[512,768]{1,0:T(8,128)(2,1)}, u32[]{:S(2)}, u32[]{:S(2)}) collective-permute-start(bf16[512,768]{1,0:T(8,128)(2,1)S(1)} %dynamic-slice_bitcast_fusion), channel_id=1, source_target_pairs={{0,1},{1,0},{2,3},{3,2},{4,5},{5,4},{6,7},{7,6},{8,9},{9,8},{10,11... | collective-permute-start | bytes 2359304 | tf_op jit(solution)/shard_map/ppermute | solution.py:219
  147.5 156.2 %collective-permute-start = (bf16[512,768]{1,0:T(8,128)(2,1)S(1)}, bf16[512,768]{1,0:T(8,128)(2,1)}, u32[]{:S(2)}, u32[]{:S(2)}) collective-permute-start(bf16[512,768]{1,0:T(8,128)(2,1)S(1)} %dynamic-slice_bitcast_fusion.2), channel_id=1, source_target_pairs={{0,1},{1,0},{2,3},{3,2},{4,5},{5,4},{6,7},{7,6},{8,9},{9,8},{10,11... | collective-permute-start | bytes 2359304 | tf_op jit(solution)/shard_map/ppermute | solution.py:219
  187.8 444.3 %reduce-scatter.41.cloned.1.call-start = ((), (), s32[]{:S(2)}) async-start(), calls=%async_computation.21 | async-start | bytes 1327104 | tf_op jit(solution)/shard_map/reduce_scatter | solution.py:367
  462.6 171.2 %reduce-scatter.39.cloned.1.call-start = ((), (), s32[]{:S(2)}) async-start(), calls=%async_computation.20 | async-start | bytes 1327104 | tf_op jit(solution)/shard_map/reduce_scatter | solution.py:367
  528.7 107.0 %reduce-scatter.37.cloned.1.call-start = ((), (), s32[]{:S(2)}) async-start(), calls=%async_computation.19 | async-start | bytes 3981312 | tf_op jit(solution)/shard_map/reduce_scatter | solution.py:367
  538.2 129.2 %reduce-scatter.35.cloned.1.call-start = ((), (), s32[]{:S(2)}) async-start(), calls=%async_computation.18 | async-start | bytes 3981312 | tf_op jit(solution)/shard_map/reduce_scatter | solution.py:367
  579.1 145.7 %reduce-scatter.53.cloned.1.call-start = ((), (), s32[]{:S(2)}) async-start(), calls=%async_computation.27 | async-start | bytes 5308416 | tf_op jit(solution)/shard_map/reduce_scatter | solution.py:367
  589.1 193.3 %reduce-scatter.51.cloned.1.call-start = ((), (), s32[]{:S(2)}) async-start(), calls=%async_computation.26 | async-start | bytes 5308416 | tf_op jit(solution)/shard_map/reduce_scatter | solution.py:367
  599.2 240.4 %reduce-scatter.47.cloned.1.call-start = ((), (), s32[]{:S(2)}) async-start(), calls=%async_computation.24 | async-start | bytes 5308416 | tf_op jit(solution)/shard_map/reduce_scatter | solution.py:367
  609.9 284.1 %reduce-scatter.69.cloned.1.call-start = ((), (), s32[]{:S(2)}) async-start(), calls=%async_computation.43 | async-start | bytes 1966080
  618.2 298.1 %reduce-scatter.67.cloned.1.call-start = ((), (), s32[]{:S(2)}) async-start(), calls=%async_computation.42 | async-start | bytes 491520
  621.9 350.0 %reduce-scatter.43.cloned.1.call-start = ((), (), s32[]{:S(2)}) async-start(), calls=%async_computation.22 | async-start | bytes 5308416 | tf_op jit(solution)/shard_map/reduce_scatter | solution.py:367
  632.0 362.2 %reduce-scatter.61.cloned.1.call-start = ((), (), s32[]{:S(2)}) async-start(), calls=%async_computation.39 | async-start | bytes 245760
  633.8 380.1 %reduce-scatter.59.cloned.1.call-start = ((), (), s32[]{:S(2)}) async-start(), calls=%async_computation.38 | async-start | bytes 245760
  635.6 401.5 %reduce-scatter.57.cloned.1.call-start = ((), (), s32[]{:S(2)}) async-start(), calls=%async_computation.37 | async-start | bytes 737280
  637.8 146.8 %copy-start.17 = (bf16[1024,768]{1,0:T(8,128)(2,1)S(1)}, bf16[1024,768]{1,0:T(8,128)(2,1)}, u32[]{:S(2)}) copy-start(bf16[1024,768]{1,0:T(8,128)(2,1)} %get-tuple-element.96) | copy-start | bytes 4718596
  637.8 422.6 %reduce-scatter.55.cloned.1.call-start = ((), (), s32[]{:S(2)}) async-start(), calls=%async_computation.36 | async-start | bytes 737280
  669.5 413.7 %reduce-scatter.65.cloned.1.call-start = ((), (), s32[]{:S(2)}) async-start(), calls=%async_computation.41 | async-start | bytes 737280
  726.9 378.9 %reduce-scatter.63.cloned.1.call-start = ((), (), s32[]{:S(2)}) async-start(), calls=%async_computation.40 | async-start | bytes 737280
  784.5 343.9 %reduce-scatter.49.cloned.1.call-start = ((), (), s32[]{:S(2)}) async-start(), calls=%async_computation.25 | async-start | bytes 737280 | tf_op jit(solution)/shard_map/reduce_scatter | solution.py:366
  784.6 187.3 %collective-permute-start.2 = (bf16[512,768]{1,0:T(8,128)(2,1)S(1)}, bf16[512,768]{1,0:T(8,128)(2,1)}, u32[]{:S(2)}, u32[]{:S(2)}) collective-permute-start(bf16[512,768]{1,0:T(8,128)(2,1)S(1)} %dynamic-slice_bitcast_fusion.1), channel_id=1, source_target_pairs={{0,1},{1,0},{2,3},{3,2},{4,5},{5,4},{6,7},{7,6},{8,9},{9,8},{10,11... | collective-permute-start | bytes 2359304 | tf_op jit(solution)/shard_map/ppermute | solution.py:219
  839.6 311.5 %reduce-scatter.45.cloned.1.call-start = ((), (), s32[]{:S(2)}) async-start(), calls=%async_computation.23 | async-start | bytes 737280 | tf_op jit(solution)/shard_map/reduce_scatter | solution.py:366
  849.6 125.0 %collective-permute-start.4 = (bf16[512,768]{1,0:T(8,128)(2,1)S(1)}, bf16[512,768]{1,0:T(8,128)(2,1)}, u32[]{:S(2)}, u32[]{:S(2)}) collective-permute-start(bf16[512,768]{1,0:T(8,128)(2,1)S(1)} %fusion.64), channel_id=1, source_target_pairs={{0,1},{1,0},{2,3},{3,2},{4,5},{5,4},{6,7},{7,6},{8,9},{9,8},{10,11... | collective-permute-start | bytes 2359304 | tf_op jit(solution)/shard_map/ppermute | solution.py:219
  (58 other events, 994.9 us)
Sparse Core Ops, SparseCore 0:
  36.7 34.8 all-gather.28
  74.0 24.0 all-gather.30
  100.0 38.9 all-gather.32
  140.7 39.7 all-gather.34
  182.7 33.9 all-gather.36
  218.5 24.0 all-gather.38
  244.5 38.9 all-gather.40
  285.3 39.7 all-gather.42
  462.7 35.5 reduce-scatter.40
  528.8 35.5 reduce-scatter.38
  567.8 48.0 reduce-scatter.36
  619.3 48.0 reduce-scatter.34
  670.8 53.8 reduce-scatter.52
  728.4 53.8 reduce-scatter.50
  785.6 53.8 reduce-scatter.46
  841.8 52.0 reduce-scatter.68
  896.8 19.5 reduce-scatter.66
  919.7 52.1 reduce-scatter.42
  974.8 19.3 reduce-scatter.60
  996.3 17.5 reduce-scatter.58
  1016.8 20.2 reduce-scatter.56
  1040.0 20.2 reduce-scatter.54
  1062.8 20.3 reduce-scatter.64
  1085.4 20.3 reduce-scatter.62
  1108.2 20.2 reduce-scatter.48
  1130.7 20.4 reduce-scatter.44

commit v2 on v1

--- a/solution.py
+++ b/solution.py
@@ -9,6 +9,7 @@
 HEAD = 64
 PAIR = 2 * HEAD
 TILE = 128
+VMEM_SPEC = pl.BlockSpec(memory_space=pltpu.VMEM)
 UNROLL = 6
 UNROLL_BACK = 6
 WIDTHS = (3, 4, 5, 6, 8)
@@ -144,7 +145,6 @@
     out_ref[:, 2 * model :] = dv_ref[...].astype(BF16)
 
 
-VMEM_SPEC = pl.BlockSpec(memory_space=pltpu.VMEM)
 SMEM_SPEC = pl.BlockSpec(memory_space=pltpu.SMEM)
 
 
@@ -323,34 +323,612 @@
     return grad_hidden, (grad_mat_qkv, grad_mat_out, grad_mat_up, grad_mat_down), grad_rows, grad_bias_hidden
 
 
+ANY_SPEC = pl.BlockSpec(memory_space=pl.ANY)
+DMA = pltpu.SemaphoreType.DMA
+
+
+class Place:
+    def __init__(self, rows, cols):
+        self.rows, self.cols = rows, cols
+        self.row, self.col = lax.axis_index("row"), lax.axis_index("col")
+        self.core = self.row % 2
+        self.bits = list(range(1, rows.bit_length() - 1))
+        self.orders = (self.bits, self.bits[::-1])
+
+    def flipped(self, row, bit):
+        return row + (1 - 2 * ((row // 2**bit) % 2)) * 2**bit
+
+    def partner(self, bit):
+        return (self.flipped(self.row, bit), self.col)
+
+    def others(self, bits):
+        found = [self.row]
+        for bit in bits:
+            found += [self.flipped(row, bit) for row in found]
+        return found
+
+    def greet(self):
+        barrier = pltpu.get_barrier_semaphore()
+
+        def signal(row, col):
+            pl.semaphore_signal(
+                barrier, inc=1, device_id=(row, col), device_id_type=pl.DeviceIdType.MESH
+            )
+
+        for bit in [0, *self.bits]:
+            signal(*self.partner(bit))
+        pl.when(self.col > 0)(lambda: signal(self.row, self.col - 1))
+        pl.when(self.col < self.cols - 1)(lambda: signal(self.row, self.col + 1))
+        inside = jnp.where((self.col > 0) & (self.col < self.cols - 1), 1, 0)
+        pl.semaphore_wait(barrier, len(self.bits) + 2 + inside)
+
+
+def remote(src, dst, send, recv, target):
+    return pltpu.make_async_remote_copy(
+        src_ref=src,
+        dst_ref=dst,
+        send_sem=send,
+        recv_sem=recv,
+        device_id=target,
+        device_id_type=pl.DeviceIdType.MESH,
+    )
+
+
+def run_stages(items):
+    plan = []
+    for order, (time, stages) in enumerate(items):
+        for index, stage in enumerate(stages):
+            plan.append((time + index, order, stage))
+    for _, _, stage in sorted(plan, key=lambda step: step[:2]):
+        stage()
+
+
+class LineGather:
+    def __init__(self, place, own, slot, sems):
+        self.place, self.own, self.slot, self.sems = place, own, slot, sems
+
+    def copies(self, hop, receiving):
+        place = self.place
+        col, cols = place.col, place.cols
+        for way, step in ((0, 1), (1, -1)):
+            target = col + step
+            if receiving:
+                slot = col - step * (hop + 1)
+                valid = (slot >= 0) & (slot < cols)
+            else:
+                slot = col - step * hop
+                valid = (slot >= 0) & (slot < cols) & (target >= 0) & (target < cols)
+            src = self.own if hop == 0 and not receiving else self.slot(slot)
+            yield valid, lambda src=src, slot=slot, way=way, target=target: remote(
+                src,
+                self.slot(slot),
+                self.sems.at[0, way, hop],
+                self.sems.at[1, way, hop],
+                (place.row, target),
+            )
+
+    def start(self, hop):
+        for valid, copy in self.copies(hop, False):
+            pl.when(valid)(lambda copy=copy: copy().start())
+
+    def wait_recv(self, hop):
+        for valid, copy in self.copies(hop, True):
+            pl.when(valid)(lambda copy=copy: copy().wait_recv())
+
+    def wait_send(self, hop):
+        for valid, copy in self.copies(hop, False):
+            pl.when(valid)(lambda copy=copy: copy().wait_send())
+
+
+def gather_item(place, own, whole, local_sem, line_sems, chip_sems, core_sems):
+    hops = place.cols - 1
+    row_slot = lambda col: whole.at[col, place.row // 2, place.core]
+    line = LineGather(place, own, row_slot, line_sems)
+    mine = lambda: pltpu.make_async_copy(own, row_slot(place.col), local_sem)
+    half = place.cols // 2
+
+    def chip_copies(phase, receiving):
+        for part in range(2):
+            order = place.orders[part]
+            bit = order[phase]
+            for index, row in enumerate(place.others(order[:phase])):
+                if receiving:
+                    row = place.flipped(row, bit)
+                ref = whole.at[pl.ds(part * half, half), row // 2, row % 2]
+                yield remote(
+                    ref,
+                    ref,
+                    chip_sems.at[0, phase, part, index],
+                    chip_sems.at[1, phase, part, index],
+                    place.partner(bit),
+                )
+
+    def core_copy(receiving):
+        ref = whole.at[:, :, 1 - place.core if receiving else place.core]
+        return remote(ref, ref, core_sems.at[0], core_sems.at[1], place.partner(0))
+
+    phases = len(place.bits)
+
+    def first():
+        mine().start()
+        line.start(0)
+
+    def hop_stage(hop):
+        line.wait_recv(hop - 1)
+        line.start(hop)
+
+    def chip_stage(phase):
+        if phase == 0:
+            line.wait_recv(hops - 1)
+            mine().wait()
+        else:
+            for copy in chip_copies(phase - 1, True):
+                copy.wait_recv()
+        for copy in chip_copies(phase, False):
+            copy.start()
+
+    def core_stage():
+        for copy in chip_copies(phases - 1, True):
+            copy.wait_recv()
+        core_copy(False).start()
+
+    def last():
+        core_copy(True).wait_recv()
+        core_copy(False).wait_send()
+        for hop in range(hops):
+            line.wait_send(hop)
+        for phase in range(phases):
+            for copy in chip_copies(phase, False):
+                copy.wait_send()
+
+    return (
+        [first]
+        + [functools.partial(hop_stage, hop) for hop in range(1, hops)]
+        + [functools.partial(chip_stage, phase) for phase in range(phases)]
+        + [core_stage, last]
+    )
+
+
+def gather_small_item(place, own, whole, local_sem, line_sems):
+    hops = place.cols - 1
+    line = LineGather(place, own, lambda col: whole.at[col], line_sems)
+    mine = lambda: pltpu.make_async_copy(own, whole.at[place.col], local_sem)
+
+    def first():
+        mine().start()
+        line.start(0)
+
+    def hop_stage(hop):
+        line.wait_recv(hop - 1)
+        line.start(hop)
+
+    def last():
+        line.wait_recv(hops - 1)
+        mine().wait()
+        for hop in range(hops):
+            line.wait_send(hop)
+
+    return [first] + [functools.partial(hop_stage, hop) for hop in range(1, hops)] + [last]
+
+
+def exchange_item(place, halves, whole, sems, delay):
+    parity = place.col % 2
+    copy = lambda: remote(
+        halves.at[1 - parity],
+        whole.at[parity],
+        sems.at[0],
+        sems.at[1],
+        (place.row, place.col + 1 - 2 * parity),
+    )
+    arriving = lambda: remote(
+        halves.at[1 - parity],
+        whole.at[1 - parity],
+        sems.at[0],
+        sems.at[1],
+        (place.row, place.col + 1 - 2 * parity),
+    )
+    mine = lambda: pltpu.make_async_copy(halves.at[parity], whole.at[parity], sems.at[2])
+
+    def first():
+        copy().start()
+        mine().start()
+
+    def last():
+        arriving().wait_recv()
+        copy().wait_send()
+        mine().wait()
+
+    return [first] + [lambda: None] * delay + [last]
+
+
+def row_pieces(rs):
+    return [(0, rs // 2), (rs // 2, rs // 2)] if rs % 32 == 0 and rs > 32 else [(0, rs)]
+
+
+def gather_kernel(rows, cols, *refs):
+    (full, lined), (small, tokens, marks) = (refs[:4], refs[4:8]), refs[8:11]
+    (full_out, lined_out), (small_out, hidden, marks_out) = (refs[11:15], refs[15:19]), refs[19:22]
+    local_sems, line_sems, chip_sems, core_sems, exchange_sems = refs[22:]
+    place = Place(rows, cols)
+    place.greet()
+    items = [
+        (0, exchange_item(place, marks, marks_out, exchange_sems.at[1], 16)),
+        (0, gather_small_item(place, small, small_out, local_sems.at[0], line_sems.at[0])),
+    ]
+    number = 0
+    for own, whole in zip(full, full_out):
+        for begin, size in row_pieces(own.shape[0]):
+            stages = gather_item(
+                place,
+                own.at[pl.ds(begin, size)],
+                whole.at[:, :, :, pl.ds(begin, size)],
+                local_sems.at[number + 1],
+                line_sems.at[number + 1],
+                chip_sems.at[number],
+                core_sems.at[number],
+            )
+            items.append((number, stages))
+            number += 1
+    items.append((number, exchange_item(place, tokens, hidden, exchange_sems.at[0], 16)))
+    for index, (own, whole) in enumerate(zip(lined, lined_out)):
+        at = number + index
+        items.append(
+            (at, gather_small_item(place, own, whole, local_sems.at[at + 1], line_sems.at[at + 1]))
+        )
+    run_stages(items)
+
+
+def gather_all(rows, cols, full, lined, small, tokens, marks):
+    number = sum(len(row_pieces(x.shape[0])) for x in full)
+    phases = rows.bit_length() - 2
+    like = lambda x, lead=(): jax.ShapeDtypeStruct(lead + x.shape, x.dtype)
+    outs = [like(x, (cols, rows // 2, 2)) for x in full] + [like(x, (cols,)) for x in lined]
+    outs += [like(small, (cols,)), like(tokens), like(marks)]
+    return pl.pallas_call(
+        functools.partial(gather_kernel, rows, cols),
+        out_shape=tuple(outs),
+        in_specs=[ANY_SPEC] * 11,
+        out_specs=(ANY_SPEC,) * 11,
+        scratch_shapes=[
+            DMA((number + len(lined) + 1,)),
+            DMA((number + len(lined) + 1, 2, 2, cols - 1)),
+            DMA((number, 2, phases, 2, 2 ** (phases - 1))),
+            DMA((number, 2)),
+            DMA((2, 3)),
+        ],
+        compiler_params=pltpu.CompilerParams(collective_id=0, has_side_effects=True),
+    )(*full, *lined, small, tokens, marks)
+
+
+class LineReduce:
+    def __init__(self, place, slot, arrived, sems):
+        self.place, self.slot, self.arrived, self.sems = place, slot, arrived, sems
+
+    def copies(self, hop, receiving):
+        place = self.place
+        last = place.cols - 1
+        for way, step in ((0, 1), (1, -1)):
+            here = place.col if way == 0 else last - place.col
+            from_start = here if not receiving else here - 1
+            slot = last - hop + from_start
+            valid = (from_start <= hop) & (from_start >= 0) & (from_start < last)
+            slot = slot if way == 0 else last - slot
+            yield valid, slot, way, lambda way=way, slot=slot, step=step: remote(
+                self.slot(slot),
+                self.arrived.at[way, hop],
+                self.sems.at[0, way, hop],
+                self.sems.at[1, way, hop],
+                (place.row, place.col + step),
+            )
+
+    def start(self, hop):
+        for valid, _, _, copy in self.copies(hop, False):
+            pl.when(valid)(lambda copy=copy: copy().start())
+
+    def wait_send(self, hop):
+        for valid, _, _, copy in self.copies(hop, False):
+            pl.when(valid)(lambda copy=copy: copy().wait_send())
+
+    def take(self, hop):
+        for valid, slot, way, copy in self.copies(hop, True):
+
+            def add(slot=slot, way=way, copy=copy):
+                pltpu.make_async_copy(
+                    self.arrived.at[way, hop], self.arrived.at[way, hop], self.sems.at[1, way, hop]
+                ).wait()
+                ref = self.slot(slot)
+                ref[...] = ref[...] + self.arrived.at[way, hop][...]
+
+            pl.when(valid)(add)
+
+    def finish(self, out):
+        hop = self.place.cols - 2
+        own = self.slot(self.place.col)
+        out[...] = own[...].astype(F32)
+        for valid, _, way, copy in self.copies(hop, True):
+
+            def add(way=way):
+                pltpu.make_async_copy(
+                    self.arrived.at[way, hop], self.arrived.at[way, hop], self.sems.at[1, way, hop]
+                ).wait()
+                out[...] = out[...] + self.arrived.at[way, hop][...].astype(F32)
+
+            pl.when(valid)(add)
+        for hop in range(self.place.cols - 1):
+            self.wait_send(hop)
+
+
+def line_stages(line, out, before):
+    hops = line.place.cols - 1
+
+    def first():
+        before()
+        line.start(0)
+
+    def hop_stage(hop):
+        line.take(hop - 1)
+        line.start(hop)
+
+    return (
+        [first]
+        + [functools.partial(hop_stage, hop) for hop in range(1, hops)]
+        + [lambda: line.finish(out)]
+    )
+
+
+def reduce_item(place, partial, out, sums, from_core, from_chips, from_line, sems):
+    local_sem, core_sems, chip_sems, line_sems = sems
+    half = place.cols // 2
+    phases = len(place.bits)
+    core_copy = lambda: remote(
+        partial.at[:, :, 1 - place.core], from_core, core_sems.at[0], core_sems.at[1], place.partner(0)
+    )
+    load = lambda: pltpu.make_async_copy(partial.at[:, :, place.core], sums, local_sem)
+    line = LineReduce(
+        place, lambda col: sums.at[col, place.row // 2], from_line, line_sems
+    )
+
+    def chip_parts(phase):
+        for part in range(2):
+            order = place.orders[part][::-1]
+            yield part, order[phase], order[phase + 1 :]
+
+    def chip_copies(phase):
+        for part, bit, rest in chip_parts(phase):
+            for index, row in enumerate(place.others(rest)):
+                row = place.flipped(row, bit)
+                yield remote(
+                    sums.at[pl.ds(part * half, half), row // 2],
+                    from_chips[phase].at[part, index],
+                    chip_sems.at[0, phase, part, index],
+                    chip_sems.at[1, phase, part, index],
+                    place.partner(bit),
+                )
+
+    def chip_take(phase):
+        for part, _, rest in chip_parts(phase):
+            for index, row in enumerate(place.others(rest)):
+                arrived = from_chips[phase].at[part, index]
+                pltpu.make_async_copy(arrived, arrived, chip_sems.at[1, phase, part, index]).wait()
+
+                def add(col, carry, part=part, index=index, row=row):
+                    ref = sums.at[part * half + col, row // 2]
+                    ref[...] = ref[...] + from_chips[phase].at[part, index, col][...]
+                    return carry
+
+                lax.fori_loop(0, half, add, 0)
+
+    def first():
+        core_copy().start()
+        load().start()
+
+    def chip_stage(phase):
+        if phase == 0:
+            load().wait()
+            core_copy().wait_recv()
+
+            def add(slot, carry):
+                col, pair = slot // (place.rows // 2), slot % (place.rows // 2)
+                ref = sums.at[col, pair]
+                ref[...] = ref[...] + from_core.at[col, pair][...]
+                return carry
+
+            lax.fori_loop(0, place.cols * (place.rows // 2), add, 0)
+        else:
+            chip_take(phase - 1)
+        for copy in chip_copies(phase):
+            copy.start()
+
+    def last():
+        core_copy().wait_send()
+        for phase in range(phases):
+            for copy in chip_copies(phase):
+                copy.wait_send()
+
+    return (
+        [first]
+        + [functools.partial(chip_stage, phase) for phase in range(phases)]
+        + line_stages(line, out, lambda: chip_take(phases - 1))
+        + [last]
+    )
+
+
+def reduce_line_item(place, partial, out, sums, from_line, local_sem, line_sems):
+    load = lambda: pltpu.make_async_copy(partial, sums, local_sem)
+    line = LineReduce(place, lambda col: sums.at[col], from_line, line_sems)
+    return [lambda: load().start()] + line_stages(line, out, lambda: load().wait())
+
+
+def reduce_small_item(place, partial, out, sums, arrived, from_line, sems, line_sems):
+    bits = [0, *place.bits]
+    line = LineReduce(place, lambda col: sums.at[col], from_line, line_sems)
+    copy = lambda index: remote(
+        sums, arrived.at[index], sems.at[0, index], sems.at[1, index], place.partner(bits[index])
+    )
+
+    def take(index):
+        copy(index).wait()
+        sums[...] = sums[...] + arrived[index]
+
+    def stage(index):
+        if index == 0:
+            sums[...] = partial[...]
+        else:
+            take(index - 1)
+        copy(index).start()
+
+    return [functools.partial(stage, index) for index in range(len(bits))] + line_stages(
+        line, out, lambda: take(len(bits) - 1)
+    )
+
+
+def reduce_kernel(rows, cols, full, lined, *refs):
+    phases = rows.bit_length() - 2
+    refs = list(refs)
+
+    def take(number):
+        taken = refs[:number]
+        del refs[:number]
+        return taken
+
+    full_in, line_in, (small_in, tokens) = take(full), take(lined), take(2)
+    full_out, line_out, (small_out, tokens_out) = take(full), take(lined), take(2)
+    place = Place(rows, cols)
+    place.greet()
+    items = []
+    small_sums, small_arrived, small_line, small_sems, small_line_sems = take(5)
+    [token_sems] = take(1)
+    parity = place.col % 2
+    token_copy = lambda: remote(
+        tokens, tokens_out, token_sems.at[0], token_sems.at[1], (place.row, place.col + 1 - 2 * parity)
+    )
+    time = 0
+    for index in range(full):
+        sums, from_core, from_line = take(3)
+        from_chips = take(phases)
+        local_sems, core_sems, chip_sems, line_sems = take(4)
+        for piece, (begin, size) in enumerate(row_pieces(full_in[index].shape[-2])):
+            rows_of = lambda ref, begin=begin, size=size: ref.at[
+                (slice(None),) * (len(ref.shape) - 2) + (pl.ds(begin, size),)
+            ]
+            stages = reduce_item(
+                place,
+                rows_of(full_in[index]),
+                rows_of(full_out[index]),
+                rows_of(sums),
+                rows_of(from_core),
+                [rows_of(ref) for ref in from_chips],
+                rows_of(from_line),
+                (local_sems.at[piece], core_sems.at[piece], chip_sems.at[piece], line_sems.at[piece]),
+            )
+            items.append((time, stages))
+            time += 1
+    for index in range(lined):
+        sums, from_line, local_sem, line_sems = take(4)
+        items.append(
+            (index, reduce_line_item(place, line_in[index], line_out[index], sums, from_line, local_sem.at[0], line_sems))
+        )
+    items.append(
+        (1, reduce_small_item(place, small_in, small_out, small_sums, small_arrived, small_line, small_sems, small_line_sems))
+    )
+    items.append(
+        (0, [lambda: token_copy().start()] + [lambda: None] * 12 + [lambda: token_copy().wait()])
+    )
+    run_stages(items)
+
+
+def reduce_all(rows, cols, full, lined, small, tokens):
+    phases = rows.bit_length() - 2
+    hops = cols - 1
+    shard = lambda x: x.shape[-2:]
+    outs = [jax.ShapeDtypeStruct(shard(x), F32) for x in (*full, *lined, small)]
+    outs.append(jax.ShapeDtypeStruct(tokens.shape, tokens.dtype))
+    scratch = [
+        pltpu.VMEM(small.shape, F32),
+        pltpu.VMEM((phases + 1,) + small.shape, F32),
+        pltpu.VMEM((2, hops) + shard(small), F32),
+        DMA((2, phases + 1)),
+        DMA((2, 2, hops)),
+        DMA((2,)),
+    ]
+    for x in full:
+        scratch += [
+            pltpu.VMEM((cols, rows // 2) + shard(x), BF16),
+            pltpu.VMEM((cols, rows // 2) + shard(x), BF16),
+            pltpu.VMEM((2, hops) + shard(x), BF16),
+        ]
+        scratch += [
+            pltpu.VMEM((2, 2 ** (phases - 1 - phase), cols // 2) + shard(x), BF16)
+            for phase in range(phases)
+        ]
+        count = len(row_pieces(x.shape[-2]))
+        scratch += [
+            DMA((count,)),
+            DMA((count, 2)),
+            DMA((count, 2, phases, 2, 2 ** (phases - 1))),
+            DMA((count, 2, 2, hops)),
+        ]
+    for x in lined:
+        scratch += [
+            pltpu.VMEM((cols,) + shard(x), BF16),
+            pltpu.VMEM((2, hops) + shard(x), BF16),
+            DMA((1,)),
+            DMA((2, 2, hops)),
+        ]
+    many = len(full) + len(lined)
+    return pl.pallas_call(
+        functools.partial(reduce_kernel, rows, cols, len(full), len(lined)),
+        out_shape=tuple(outs),
+        in_specs=[ANY_SPEC] * many + [VMEM_SPEC, ANY_SPEC],
+        out_specs=(VMEM_SPEC,) * (many + 1) + (ANY_SPEC,),
+        scratch_shapes=scratch,
+        compiler_params=pltpu.CompilerParams(
+            collective_id=1, has_side_effects=True, vmem_limit_bytes=62 << 20
+        ),
+    )(*full, *lined, small, tokens)
+
+
 def shards(
-    tokens, seg_ids, pad_mask, rand_blocks, w_qkv, w_out, w_up, w_down, layer_vectors, bias_up, d_out
+    rows, cols, tokens, seg_ids, pad_mask, rand_blocks, w_qkv, w_out, w_up, w_down, layer_vectors, bias_up, d_out
 ):
     layers = w_qkv.shape[0]
     parity = lax.axis_index("col") % 2
+    half = seg_ids.shape[1]
+    chosen = rand_blocks.reshape(2, 1, -1)
+    chosen = jnp.pad(chosen, ((0, 0), (0, 0), (0, 128 - chosen.shape[2])))
     marks = jnp.concatenate(
-        [seg_ids, pad_mask, rand_blocks.reshape(rand_blocks.shape[0], -1)], axis=1
-    )
-    half = seg_ids.shape[1]
-    marks = to_sequence(marks[:, None], parity)
-    seg, pad = marks[:, :half].reshape(-1), marks[:, half : 2 * half].reshape(-1)
-    rand = marks[:, 2 * half :].reshape(-1, rand_blocks.shape[2])
-    pattern = key_pattern(seg, pad, rand)
-
-    def fetch(layer):
-        mats = tuple(
-            lax.all_gather(
-                lax.all_gather(w[layer], "col", axis=1, tiled=True), "row", axis=0, tiled=True
-            )
-            for w in (w_qkv, w_out, w_up, w_down)
-        )
-        return mats + (
-            lax.all_gather(layer_vectors[layer], "col", axis=1, tiled=True).astype(F32),
-            lax.all_gather(bias_up[layer], "col", axis=0, tiled=True).astype(F32),
-        )
-
-    weights = [fetch(layer) for layer in range(layers)]
-    hidden = to_sequence(tokens, parity)
+        [seg_ids.reshape(2, -1, 128), pad_mask.reshape(2, -1, 128), chosen], axis=1
+    )
+    marks = jnp.pad(marks, ((0, 0), (0, -marks.shape[1] % 8), (0, 0)))
+    part = layer_vectors.shape[2]
+    small = jnp.concatenate([layer_vectors.reshape(-1, part), bias_up.reshape(-1, part)])
+    small_rows = small.shape[0]
+    small = jnp.pad(small, ((0, -small_rows % 16), (0, 0)))
+    mats = (w_qkv, w_out, w_up, w_down)
+    got = gather_all(
+        rows, cols, [w[0] for w in mats], [w[1] for w in mats], small, tokens, marks
+    )
+    vectors = got[8][:, : layers * 8].transpose(1, 0, 2).reshape(layers, 8, -1).astype(F32)
+    up_biases = got[8][:, layers * 8 : small_rows].reshape(cols, layers, -1).transpose(1, 0, 2)
+    up_biases = up_biases.reshape(layers, -1).astype(F32)
+    hidden = got[9].reshape(2 * half, -1)
+    marks = got[10]
+    lines = half // 128
+    seg, pad = marks[:, :lines].reshape(-1), marks[:, lines : 2 * lines].reshape(-1)
+    rand = marks[:, 2 * lines, : half // BLOCK * rand_blocks.shape[2]]
+    pattern = key_pattern(seg, pad, rand.reshape(-1, rand_blocks.shape[2]))
+
+    def assembled(slots):
+        return slots.transpose(1, 2, 0, 3).reshape(rows * slots.shape[2], -1)
+
+    first_mats = [assembled(g.reshape((cols, rows) + g.shape[3:])) for g in got[:4]]
+    second_mats = [
+        assembled(lax.all_gather(g, "row", axis=0).transpose(1, 0, 2, 3)) for g in got[4:8]
+    ]
+    weights = [
+        (*layer_mats, vectors[layer], up_biases[layer])
+        for layer, layer_mats in enumerate((first_mats, second_mats))
+    ]
     kept = []
     for layer in range(layers):
         hidden, saved = layer_forward(hidden, weights[layer], pattern)
@@ -359,21 +937,32 @@
     flow = to_sequence(d_out, parity).astype(F32)
     grads, vec_grads, up_grads = [None] * layers, [None] * layers, [None] * layers
     for layer in reversed(range(layers)):
-        flow, mats, vec_grads[layer], up_grads[layer] = layer_backward(
+        flow, grads[layer], vec_grads[layer], up_grads[layer] = layer_backward(
             flow, weights[layer], kept[layer], pattern
         )
-        grads[layer] = [
-            lax.psum_scatter(
-                lax.psum_scatter(m.astype(BF16), "row", scatter_dimension=0, tiled=True),
-                "col", scatter_dimension=1, tiled=True,
-            ).astype(F32)
-            for m in mats
-        ]
-    d_tokens = from_sequence(flow, parity, BF16)
-    vec = lax.psum_scatter(jnp.stack(vec_grads), "col", scatter_dimension=2, tiled=True)
-    ups = lax.psum_scatter(jnp.stack(up_grads), "col", scatter_dimension=1, tiled=True)
-    vec, ups = lax.psum((vec, ups), "row")
-    mats = [jnp.stack([grads[layer][i] for layer in range(layers)]) for i in range(4)]
+    full = []
+    for mat in grads[0]:
+        mat = mat.astype(BF16).reshape(rows // 2, 2, mat.shape[0] // rows, cols, -1)
+        full.append(mat.transpose(3, 0, 1, 2, 4))
+    lined = []
+    for mat in grads[1]:
+        mat = lax.psum_scatter(mat.astype(BF16), "row", scatter_dimension=0, tiled=True)
+        lined.append(mat.reshape(mat.shape[0], cols, -1).transpose(1, 0, 2))
+    small = jnp.concatenate(
+        [
+            jnp.stack(vec_grads).reshape(layers * 8, cols, part).transpose(1, 0, 2),
+            jnp.stack(up_grads).reshape(layers, cols, -1, part).transpose(1, 0, 2, 3).reshape(cols, -1, part),
+        ],
+        axis=1,
+    )
+    halves = flow.reshape(2, half, -1)
+    summed = reduce_all(rows, cols, full, lined, small, pick(halves, 1 - parity).astype(BF16))
+    own, other = pick(halves, parity), summed[9].astype(F32)
+    first = parity == 0
+    d_tokens = jnp.stack([jnp.where(first, own, other), jnp.where(first, other, own)])
+    mats = [jnp.stack([summed[i], summed[4 + i]]) for i in range(4)]
+    vec = summed[8][: layers * 8].reshape(layers, 8, part)
+    ups = summed[8][layers * 8 :].reshape(layers, -1)
     return output, d_tokens, *mats, vec, ups
 
 
@@ -401,4 +990,5 @@
         P(None, None, "col"),
         P(None, "col"),
     )
-    return jax.shard_map(shards, mesh=mesh, in_specs=in_specs, out_specs=out_specs, check_vma=False)
+    local = functools.partial(shards, mesh.shape["row"], mesh.shape["col"])
+    return jax.shard_map(local, mesh=mesh, in_specs=in_specs, out_specs=out_specs, check_vma=False)

time: 1160 us -> 751 us (0.65)
  waiting for transfers between devices: 454 us -> 1.51 us
  blocking collectives: 254 us -> 0 us
  Pallas kernels: 104 us -> 317 us
  local copies, waits for them, and re-layouts: 92.7 us -> 186 us
  matrix products: 193 us -> 174 us
    reduce_scatter x10 -> x4, waiting for transfers between devices: 268 us -> 0.01 us  [shards(): lax.psum_scatter(mat.astype(BF16), 'row', scatter_dimension=0, tiled=True)]
    all_gather x12 -> x0, blocking collectives: 231 us -> none  [the longest x8 166 us: fetch(): lax.all_gather(w[layer], 'col', axis=1, tiled=True)]
    pallas_call x0 -> x2, Pallas kernels: none -> 213 us  [the longest x1 108 us: reduce_all(): pl.pallas_call(functools.partial(reduce_kernel, rows, cols, len(full), le...]
    unnamed x34 -> x8, waiting for transfers between devices: 186 us -> 1.48 us
    reshape x3 -> x31, local copies, waits for them, and re-layouts: 0.24 us -> 109 us  [the longest x8 51.5 us: shards(): mat = mat.astype(BF16).reshape(rows // 2, 2, mat.shape[0] // rows, cols, -1)]
    slice x2 -> x1, local copies, waits for them, and re-layouts: 39.8 us -> 2.05 us  [layer_forward(): vectors[6]]
    psum x1 -> x0, blocking collectives: 23.4 us -> none  [shards(): vec, ups = lax.psum((vec, ups), 'row')]
    all_gather x4, local copies, waits for them, and re-layouts: 6.33 us -> 20 us  [shards(): lax.all_gather(g, 'row', axis=0).transpose(1, 0, 2, 3)]
  transfers between devices with their start and end apart: 31 -> 10, of which waited for: 15 -> 0; matrix products, arithmetic and copies ran while one was open for 23% -> 42% of each run, Pallas kernels for 9% -> 14%
where the time goes in v2:
time: 751 us; the launch traced here: 742 us
  Pallas kernels  317 us (42%)
  local copies, waits for them, and re-layouts  186 us (25%)
  matrix products  174 us (23%)
  other arithmetic  46.6 us (6%)
  between operations  15.5 us (2%)
    pallas_call x1, Pallas kernels, reduce_all(): pl.pallas_call(functools.partial(reduce_kernel, rows, cols, len(full), le...  108 us
    pallas_call x1, Pallas kernels, gather_all(): pl.pallas_call(functools.partial(gather_kernel, rows, cols), out_shape=tu...  105 us
    pallas_call x2, Pallas kernels, attend_back(): pl.pallas_call(attend_back_kernel, out_shape=jax.ShapeDtypeStruct((length...  57.8 us
    reshape x8, local copies, waits for them, and re-layouts, shards(): mat = mat.astype(BF16).reshape(rows // 2, 2, mat.shape[0] // rows, cols, -1)  51.5 us
    pallas_call x2, Pallas kernels, attend(): pl.pallas_call(attend_kernel, out_shape=(jax.ShapeDtypeStruct((length, mo...  45.8 us
    unnamed x164, local copies, waits for them, and re-layouts  33 us
    dot_general x2, matrix products, layer_backward(): jnp.einsum('td,fd->tf', grad_down_low, mat_down, preferred_element_type=F32)  29 us
    reshape x4, local copies, waits for them, and re-layouts, shards(): g.reshape((cols, rows) + g.shape[3:])  24.4 us
  transfers between devices with their start and end apart: 10, of which 0 were waited for; matrix products, arithmetic and copies ran while one was open for 42% of the time, Pallas kernels for 14%

profile of v2, /device:TPU:0, one launch (start us, length us, event | category | flops | bytes accessed | tf_op | source)
XLA Modules:
  0.0 742.3 jit_solution(18130696984928225246)
XLA Ops:
  19.8 104.6 %shard_map.170 = (bf16[4,4,2,96,576]{4,3,2,1,0:T(8,128)(2,1)}, bf16[4,4,2,96,192]{4,3,2,1,0:T(8,128)(2,1)}, bf16[4,4,2,96,768]{4,3,2,1,0:T(8,128)(2,1)}, bf16[4,...) custom-call(bf16[96,576]{1,0:T(8,128)(2,1)} %get-tuple-element.138.r, ...), custom_call_target="tpu_custom_call" | custom-call | tf_op jit(solution)/shard_map/pallas_call | solution.py:587
  132.5 7.1 copy.100
  139.6 6.9 reshape.308
  158.1 7.4 %add_convert_fusion.1.qkv_ref = bf16[1024,2304]{1,0:T(8,128)(2,1)} fusion(bf16[1024,768]{1,0:T(8,128)(2,1)} %bitcast.252, bf16[768,2304]{1,0:T(8,128)(2,1)S(1)} %reshape.308, f32[2304]{0:T(1024)S(1)} %get-tuple-element.151), kind=kOutput, calls=%fused_computation.21 | convolution fusion | flops 3628597248 | bytes 9839616 | tf_op jit(solution)/shard_map/dot_general | solution.py:269
  170.4 6.4 copy.58
  180.0 8.9 %copy.59 = bf16[4,8,384,192]{2,1,3,0:T(8,128)(2,1)} copy(bf16[4,8,384,192]{3,2,1,0:T(8,128)(2,1)} %bitcast.198) | data formatting | bytes 9437184 | tf_op jit(solution)/shard_map/reshape | solution.py:924
  188.9 5.8 copy.83
  198.2 22.9 %shard_map.171 = (bf16[1024,768]{1,0:T(8,128)(2,1)S(1)}, f32[6,8,256]{2,1,0:T(8,128)S(1)}) custom-call(s32[8]{0:T(128)S(1)} %get-tuple-element.125.first_ref, s32[8]{0:T(128)S(1)} %get-tuple-element.124.count_ref, bf16[1024,2304]{1,0:T(8,128)(2,1)S(1)} %bitcast.181, f32[1024,1024]{1,0:T(8,128)S(1)} %fusion.17.bias_ref), custom_call_target="tpu_custom_call" | custom-call | tf_op jit(solution)/shard_map/pallas_call | solution.py:155
  224.9 9.3 %multiply_convert_fusion.1 = (bf16[1024,3072]{1,0:T(8,128)(2,1)S(1)}, f32[1024,3072]{1,0:T(8,128)}) fusion(f32[3072]{0:T(1024)S(1)} %bitcast.245, bf16[768,3072]{1,0:T(8,128)(2,1)S(1)} %bitcast.202, f32[1024,768]{1,0:T(8,128)S(1)} %get-tuple-element.153, f32[768]{0:T(1024)S(1)} %copy-done.58, f32[768]{0:T(1024)S(1)} %copy-done.48, ...), kind=kOutput, calls=%fused_computation.16 | convolution fusion | flops 4854644736 | bytes 26765312 | tf_op jit(solution)/shard_map/dot_general | solution.py:276
  254.0 6.1 copy.99
  260.1 7.9 %reshape.316 = bf16[768,2304]{1,0:T(8,128)(2,1)} reshape(bf16[8,96,4,576]{3,2,1,0:T(4,128)(2,1)} %bitcast.192) | data formatting | bytes 7077888 | tf_op jit(solution)/shard_map/reshape | solution.py:922
  268.0 6.7 add_convert_fusion.qkv_ref
  274.7 22.9 %shard_map.172 = (bf16[1024,768]{1,0:T(8,128)(2,1)S(1)}, f32[6,8,256]{2,1,0:T(8,128)S(1)}) custom-call(s32[8]{0:T(128)S(1)} %get-tuple-element.125.first_ref, s32[8]{0:T(128)S(1)} %get-tuple-element.124.count_ref, bf16[1024,2304]{1,0:T(8,128)(2,1)S(1)} %add_convert_fusion.qkv_ref, f32[1024,1024]{1,0:T(8,128)S(1)} %copy-done.1), custom_call_target="tpu_custom_call" | custom-call | tf_op jit(solution)/shard_map/pallas_call | solution.py:155
  301.8 6.0 copy.62
  319.4 9.4 %multiply_convert_fusion = (bf16[1024,3072]{1,0:T(8,128)(2,1)S(1)}, f32[1024,3072]{1,0:T(8,128)}) fusion(f32[3072]{0:T(1024)S(1)} %bitcast.247, bf16[768,3072]{1,0:T(8,128)(2,1)S(1)} %bitcast.210, f32[1024,768]{1,0:T(8,128)S(1)} %copy-done.13, f32[768]{0:T(1024)S(1)} %copy-done.60, f32[768]{0:T(1024)S(1)} %copy-done.50, f32[1024]{0:T(1024)S(1)} %add_rsqrt_fusion.1, ...), kind=kOutput, calls=%fused_computation.14 | convolution fusion | flops 4854644736 | bytes 26765312 | tf_op jit(solution)/shard_map/dot_general | solution.py:276
  341.3 14.3 %convert_reduce_fusion = (f32[3072]{0:T(1024)S(1)}, bf16[1024,3072]{1,0:T(8,128)(2,1)}) fusion(f32[1024,3072]{1,0:T(8,128)} %get-tuple-element.161, f32[3072]{0:T(1024)S(1)} %bitcast.248, bf16[3072,768]{0,1:T(8,128)(2,1)S(1)} %bitcast.213, f32[1024,768]{1,0:T(8,128)S(1)} %get-tuple-element.121), kind=kOutput, calls=%fused_computation.12 | convolution fusion | flops 4873516032 | bytes 26763264 | tf_op jit(solution)/shard_map/td,fd->tf/dot_general | solution.py:301
  355.5 8.3 %multiply_reduce_fusion = (f32[768]{0:T(1024)S(1)}, f32[1024]{0:T(1024)S(1)}, f32[1024]{0:T(1024)S(1)}, f32[768]{0:T(1024)S(1)}, f32[1024,768]{1,0:T(8,128)S(1)}) fusion(f32[1024,768]{1,0:T(8,128)S(1)} %copy-done.13, f32[1024]{0:T(1024)S(1)} %add_rsqrt_fusion.1, f32[1024]{0:T(1024)S(1)} %broadcast_multiply_fusion.9, f32[768]{0:T(1024)S(1)} %copy-done.50, ...), kind=kOutput, calls=%fused_computation.53 | convolution fusion | flops 4839698432 | bytes 20472832 | tf_op jit(solution)/shard_map/tf,df->td/dot_general | solution.py:305
  372.8 29.0 %shard_map.173 = bf16[1024,2304]{1,0:T(8,128)(2,1)} custom-call(s32[8]{0:T(128)S(1)} %get-tuple-element.125.first_ref, s32[8]{0:T(128)S(1)} %get-tuple-element.124.count_ref, bf16[1024,2304]{1,0:T(8,128)(2,1)} %copy-done.4, bf16[1024,768]{1,0:T(8,128)(2,1)S(1)} %convolution_convert_fusion.7.grad_ref, f32[1024,1024]{1,0:T(8,128)S(1)} %copy-done.2, ...), custom_call_target="tpu_custom_call" | custom-call | tf_op jit(solution)/shard_map/pallas_call | solution.py:171
  401.7 8.0 %convolution_convert_fusion.4 = bf16[768,2304]{1,0:T(8,128)(2,1)} fusion(bf16[1024,2304]{1,0:T(8,128)(2,1)} %shard_map.173, f32[1024,768]{1,0:T(8,128)S(1)} %copy-done.11, f32[768]{0:T(1024)S(1)} %copy-done.61, f32[768]{0:T(1024)S(1)} %copy-done.49, f32[1024]{0:T(1024)S(1)} %add_rsqrt_fusion.2, f32[1024]{0:T(1024)S(1)} %broadcast_multiply_fusion.10), kind=kOutput, calls=%fused_computation.27 | convolution fusion | flops 3629580288 | bytes 11417600 | tf_op jit(solution)/shard_map/td,te->de/dot_general | solution.py:314
  409.8 10.7 %multiply_reduce_fusion.1 = (f32[768]{0:T(1024)S(1)}, f32[1024]{0:T(1024)S(1)}, f32[1024]{0:T(1024)S(1)}, f32[768]{0:T(1024)S(1)}, f32[1024,768]{1,0:T(8,128)}) fusion(f32[1024,768]{1,0:T(8,128)S(1)} %copy-done.11, f32[1024]{0:T(1024)S(1)} %add_rsqrt_fusion.2, f32[1024]{0:T(1024)S(1)} %broadcast_multiply_fusion.10, f32[768]{0:T(1024)S(1)} %copy-done.49, ...), kind=kOutput, calls=%fused_computation.56 | convolution fusion | flops 3631739392 | bytes 17720320 | tf_op jit(solution)/shard_map/te,de->td/dot_general | solution.py:315
  420.5 10.5 %convolution_convert_fusion.1 = bf16[768,3072]{1,0:T(8,128)(2,1)} fusion(bf16[1024,3072]{1,0:T(8,128)(2,1)} %get-tuple-element.168, f32[1024,768]{1,0:T(8,128)S(1)} %copy-done.14, f32[768]{0:T(1024)S(1)} %copy-done.60, f32[768]{0:T(1024)S(1)} %copy-done.50, f32[1024]{0:T(1024)S(1)} %add_rsqrt_fusion.1, f32[1024]{0:T(1024)S(1)} %broadcast_multiply_fusion.9), kind=kOutput, calls=%fused_computation.24 | convolution fusion | flops 4838129664 | bytes 14170112 | tf_op jit(solution)/shard_map/td,tf->df/dot_general | solution.py:304
  434.0 14.8 %convert_reduce_fusion.1 = (f32[3072]{0:T(1024)S(1)}, bf16[1024,3072]{1,0:T(8,128)(2,1)}) fusion(f32[1024,3072]{1,0:T(8,128)} %get-tuple-element.155, f32[3072]{0:T(1024)S(1)} %bitcast.246, bf16[3072,768]{0,1:T(8,128)(2,1)} %bitcast.203, f32[1024,768]{1,0:T(8,128)S(1)} %get-tuple-element.117), kind=kOutput, calls=%fused_computation.13 | convolution fusion | flops 4873516032 | bytes 26763264 | tf_op jit(solution)/shard_map/td,fd->tf/dot_general | solution.py:301
  449.0 11.5 %multiply_reduce_fusion.2 = (f32[768]{0:T(1024)S(1)}, f32[1024]{0:T(1024)S(1)}, f32[1024]{0:T(1024)S(1)}, f32[768]{0:T(1024)S(1)}, f32[1024,768]{1,0:T(8,128)}) fusion(f32[1024,768]{1,0:T(8,128)S(1)} %copy-done.8, f32[1024]{0:T(1024)S(1)} %add_rsqrt_fusion.3, f32[1024]{0:T(1024)S(1)} %broadcast_multiply_fusion.11, f32[768]{0:T(1024)S(1)} %copy-done.48, ...), kind=kOutput, calls=%fused_computation.57 | convolution fusion | flops 4839698432 | bytes 20472832 | tf_op jit(solution)/shard_map/tf,df->td/dot_general | solution.py:305
  460.6 8.0 %convolution_convert_fusion.3 = bf16[768,3072]{1,0:T(8,128)(2,1)} fusion(bf16[1024,3072]{1,0:T(8,128)(2,1)S(1)} %copy-done.67, f32[1024,768]{1,0:T(8,128)S(1)} %copy-done.8, f32[768]{0:T(1024)S(1)} %copy-done.59, f32[768]{0:T(1024)S(1)} %copy-done.48, f32[1024]{0:T(1024)S(1)} %add_rsqrt_fusion.3, f32[1024]{0:T(1024)S(1)} %broadcast_multiply_fusion.11), kind=kOutput, calls=%fused_computation.26 | convolution fusion | flops 4838129664 | bytes 14170112 | tf_op jit(solution)/shard_map/td,tf->df/dot_general | solution.py:304
  468.6 10.3 %convolution_convert_fusion = bf16[3072,768]{1,0:T(8,128)(2,1)} fusion(bf16[1024,3072]{1,0:T(8,128)(2,1)} %copy-done.69, f32[1024,768]{1,0:T(8,128)S(1)} %copy-done.22), kind=kOutput, calls=%fused_computation.23 | convolution fusion | flops 4834983936 | bytes 14155776 | tf_op jit(solution)/shard_map/tf,td->fd/dot_general | solution.py:300
  482.5 10.3 %reshape.324 = bf16[4,2,96,4,768]{4,3,2,1,0:T(4,128)(2,1)} reshape(bf16[768,3072]{1,0:T(8,128)(2,1)} %convolution_convert_fusion.3) | data formatting | bytes 9437184 | tf_op jit(solution)/shard_map/reshape | solution.py:945
  513.2 28.9 %shard_map.174 = bf16[1024,2304]{1,0:T(8,128)(2,1)} custom-call(s32[8]{0:T(128)S(1)} %get-tuple-element.125.first_ref, s32[8]{0:T(128)S(1)} %get-tuple-element.124.count_ref, bf16[1024,2304]{1,0:T(8,128)(2,1)} %add_convert_fusion.1.qkv_ref, bf16[1024,768]{1,0:T(8,128)(2,1)S(1)} %convolution_convert_fusion.6.grad_ref, f32[1024,1024]{1,0:T(8,128)S(1)} %copy-done.3, ...), custom_call_target="tpu_custom_call" | custom-call | tf_op jit(solution)/shard_map/pallas_call | solution.py:171
  546.7 6.7 convolution_convert_fusion.5
  566.1 9.8 %convolution_convert_fusion.2 = bf16[3072,768]{1,0:T(8,128)(2,1)} fusion(bf16[1024,3072]{1,0:T(8,128)(2,1)} %copy-done.68, f32[1024,768]{1,0:T(8,128)S(1)} %copy-done.24), kind=kOutput, calls=%fused_computation.25 | convolution fusion | flops 4834983936 | bytes 14155776 | tf_op jit(solution)/shard_map/tf,td->fd/dot_general | solution.py:300
  575.9 13.1 %reshape.340 = bf16[4,2,384,4,192]{4,3,2,1,0:T(4,128)(2,1)} reshape(bf16[3072,768]{1,0:T(8,128)(2,1)} %convolution_convert_fusion.2) | data formatting | bytes 9437184 | tf_op jit(solution)/shard_map/reshape | solution.py:945
  589.0 7.2 copy.96
  613.7 108.5 %shard_map.175 = (f32[96,576]{1,0:T(8,128)}, f32[96,192]{1,0:T(8,128)}, f32[96,768]{1,0:T(8,128)}, f32[384,192]{1,0:T(8,128)}, f32[96,576]{1,0:T(8,128)}, /*inde...) custom-call(bf16[4,4,2,96,576]{4,3,2,1,0:T(8,128)(2,1)} %bitcast.190,, ...), custom_call_target="tpu_custom_call" | custom-call | tf_op jit(solution)/shard_map/pallas_call | solution.py:879
  (326 shorter events, 178.8 us)
Async XLA Ops:
  7.2 240.2 %all-gather.11.cloned.1.call-start = ((), (), s32[]{:S(2)}) async-start(), calls=%async_computation.9 | async-start | bytes 1769472 | tf_op jit(solution)/shard_map/all_gather | solution.py:926
  11.7 114.3 %copy-start.30 = (bf16[2,512,768]{2,1,0:T(8,128)(2,1)S(1)}, bf16[2,512,768]{2,1,0:T(8,128)(2,1)}, u32[]{:S(2)}) copy-start(bf16[2,512,768]{2,1,0:T(8,128)(2,1)} %param.21) | copy-start | bytes 4718596
  124.5 129.5 %all-gather.9.cloned.1.call-start = ((), (), s32[]{:S(2)}) async-start(), calls=%async_computation.8 | async-start | bytes 4423680 | tf_op jit(solution)/shard_map/all_gather | solution.py:926
  125.2 176.6 %all-gather.13.cloned.1.call-start = ((), (), s32[]{:S(2)}) async-start(), calls=%async_computation.10 | async-start | bytes 5308416 | tf_op jit(solution)/shard_map/all_gather | solution.py:926
  126.0 185.0 %all-gather.15.cloned.1.call-start = ((), (), s32[]{:S(2)}) async-start(), calls=%async_computation.11 | async-start | bytes 5308416 | tf_op jit(solution)/shard_map/all_gather | solution.py:926
  127.0 116.1 %collective-permute-start.1 = (bf16[512,768]{1,0:T(8,128)(2,1)}, bf16[512,768]{1,0:T(8,128)(2,1)}, u32[]{:S(2)}, u32[]{:S(2)}) collective-permute-start(bf16[512,768]{1,0:T(8,128)(2,1)} %dynamic-slice_bitcast_fusion), channel_id=1, source_target_pairs={{0,1},{1,0},{2,3},{3,2},{4,5},{5,4},{6,7},{7,6},{8,9},{9,8},{10,11... | collective-permute-start | bytes 2359304 | tf_op jit(solution)/shard_map/ppermute | solution.py:219
  128.1 477.0 %reduce-scatter.7.cloned.1.call-start = ((), (), s32[]{:S(2)}) async-start(), calls=%async_computation.5 | async-start | bytes 1327104 | tf_op jit(solution)/shard_map/reduce_scatter | solution.py:949
  146.5 19.0 %copy-start.19 = (bf16[768,2304]{1,0:T(8,128)(2,1)}, bf16[768,2304]{1,0:T(8,128)(2,1)S(1)}, u32[]{:S(2)}) copy-start(bf16[768,2304]{1,0:T(8,128)(2,1)S(1)} %reshape.308) | copy-start | bytes 10616836
  170.4 50.7 %copy-start.32 = (bf16[768,768]{0,1:T(8,128)(2,1)}, bf16[768,768]{0,1:T(8,128)(2,1)S(1)}, u32[]{:S(2)}) copy-start(bf16[768,768]{0,1:T(8,128)(2,1)S(1)} %reshape.311) | copy-start | bytes 3538948
  198.1 23.0 %copy-start = (f32[1024,1024]{1,0:T(8,128)}, f32[1024,1024]{1,0:T(8,128)S(1)}, u32[]{:S(2)}) copy-start(f32[1024,1024]{1,0:T(8,128)S(1)} %fusion.17.bias_ref) | copy-start | bytes 12582916
  198.1 23.0 %copy-start.65 = (f32[768]{0:T(1024)S(1)}, f32[768]{0:T(1024)}, u32[]{:S(2)}) copy-start(f32[768]{0:T(1024)} %get-tuple-element.111) | copy-start | bytes 9220
  198.2 23.0 %copy-start.66 = (bf16[2,512,768]{2,1,0:T(8,128)(2,1)S(1)}, bf16[2,512,768]{2,1,0:T(8,128)(2,1)}, u32[]{:S(2)}) copy-start(bf16[2,512,768]{2,1,0:T(8,128)(2,1)} %get-tuple-element.33) | copy-start | bytes 4718596
  222.7 11.5 %copy-start.7 = (f32[1024,768]{1,0:T(8,128)}, f32[1024,768]{1,0:T(8,128)S(1)}, u32[]{:S(2)}) copy-start(f32[1024,768]{1,0:T(8,128)S(1)} %get-tuple-element.153) | copy-start | bytes 9437188
  222.7 14.2 %slice-start.6 = ((s8[4718592]{0:T(1024)(128)(4,1)}), s8[4194304]{0:T(1024)(128)(4,1)S(1)}, s32[]{:S(2)}) async-start(s8[4718592]{0:T(1024)(128)(4,1)} %bitcast.204), calls=%async_computation.18 | async-start | bytes 8388608
  224.9 12.0 %slice-start.7 = ((s8[4718592]{0:T(1024)(128)(4,1)}), s8[524288]{0:T(1024)(128)(4,1)S(1)}, s32[]{:S(2)}) async-start(s8[4718592]{0:T(1024)(128)(4,1)} %bitcast.204), calls=%async_computation.19 | async-start | bytes 1048576
  224.9 12.0 %copy-start.64 = (f32[768]{0:T(1024)S(1)}, f32[768]{0:T(1024)}, u32[]{:S(2)}) copy-start(f32[768]{0:T(1024)} %get-tuple-element.108) | copy-start | bytes 9220
  242.4 25.5 %copy-start.9 = (f32[1024,768]{1,0:T(8,128)}, f32[1024,768]{1,0:T(8,128)S(1)}, u32[]{:S(2)}) copy-start(f32[1024,768]{1,0:T(8,128)S(1)} %get-tuple-element.157) | copy-start | bytes 9437188
  274.7 22.9 %copy-start.4 = (bf16[1024,2304]{1,0:T(8,128)(2,1)}, bf16[1024,2304]{1,0:T(8,128)(2,1)S(1)}, u32[]{:S(2)}) copy-start(bf16[1024,2304]{1,0:T(8,128)(2,1)S(1)} %add_convert_fusion.qkv_ref) | copy-start | bytes 14155780
  274.7 22.9 %copy-start.10 = (f32[1024,768]{1,0:T(8,128)S(1)}, f32[1024,768]{1,0:T(8,128)}, u32[]{:S(2)}) copy-start(f32[1024,768]{1,0:T(8,128)} %copy-done.9) | copy-start | bytes 9437188
  274.7 22.9 %copy-start.34 = (bf16[768,768]{0,1:T(8,128)(2,1)S(1)}, bf16[768,768]{0,1:T(8,128)(2,1)}, u32[]{:S(2)}) copy-start(bf16[768,768]{0,1:T(8,128)(2,1)} %reshape.317) | copy-start | bytes 3538948
  274.7 22.9 %copy-start.63 = (f32[768]{0:T(1024)S(1)}, f32[768]{0:T(1024)}, u32[]{:S(2)}) copy-start(f32[768]{0:T(1024)} %get-tuple-element.103) | copy-start | bytes 9220
  341.3 14.3 %copy-start.21 = (f32[1024,768]{1,0:T(8,128)}, f32[1024,768]{1,0:T(8,128)S(1)}, u32[]{:S(2)}) copy-start(f32[1024,768]{1,0:T(8,128)S(1)} %get-tuple-element.121) | copy-start | bytes 9437188
  369.2 237.7 %reduce-scatter.5.cloned.1.call-start = ((), (), s32[]{:S(2)}) async-start(), calls=%async_computation.4 | async-start | bytes 3981312 | tf_op jit(solution)/shard_map/reduce_scatter | solution.py:949
  372.7 29.0 %copy-start.11 = (f32[1024,768]{1,0:T(8,128)S(1)}, f32[1024,768]{1,0:T(8,128)}, u32[]{:S(2)}) copy-start(f32[1024,768]{1,0:T(8,128)} %copy-done.9) | copy-start | bytes 9437188
  409.7 199.5 %reduce-scatter.9.cloned.1.call-start = ((), (), s32[]{:S(2)}) async-start(), calls=%async_computation.6 | async-start | bytes 5308416 | tf_op jit(solution)/shard_map/reduce_scatter | solution.py:949
  431.0 180.2 %reduce-scatter.11.cloned.1.call-start = ((), (), s32[]{:S(2)}) async-start(), calls=%async_computation.7 | async-start | bytes 5308416 | tf_op jit(solution)/shard_map/reduce_scatter | solution.py:949
  434.0 14.8 %copy-start.23 = (f32[1024,768]{1,0:T(8,128)}, f32[1024,768]{1,0:T(8,128)S(1)}, u32[]{:S(2)}) copy-start(f32[1024,768]{1,0:T(8,128)S(1)} %get-tuple-element.117) | copy-start | bytes 9437188
  434.0 15.0 %copy-start.8 = (f32[1024,768]{1,0:T(8,128)S(1)}, f32[1024,768]{1,0:T(8,128)}, u32[]{:S(2)}) copy-start(f32[1024,768]{1,0:T(8,128)} %copy-done.7) | copy-start | bytes 9437188
  449.0 11.6 %copy-start.59 = (f32[768]{0:T(1024)S(1)}, f32[768]{0:T(1024)}, u32[]{:S(2)}) copy-start(f32[768]{0:T(1024)} %get-tuple-element.109) | copy-start | bytes 9220
  449.0 11.6 %copy-start.67 = (bf16[1024,3072]{1,0:T(8,128)(2,1)S(1)}, bf16[1024,3072]{1,0:T(8,128)(2,1)}, u32[]{:S(2)}) copy-start(bf16[1024,3072]{1,0:T(8,128)(2,1)} %get-tuple-element.170) | copy-start | bytes 18874372
  563.9 38.2 %collective-permute-start = (bf16[512,768]{1,0:T(8,128)(2,1)S(1)}, bf16[512,768]{1,0:T(8,128)(2,1)}, u32[]{:S(2)}, u32[]{:S(2)}) collective-permute-start(bf16[512,768]{1,0:T(8,128)(2,1)S(1)} %dynamic-slice_bitcast_fusion.1), channel_id=1, source_target_pairs={{0,1},{1,0},{2,3},{3,2},{4,5},{5,4},{6,7},{7,6},{8,9},{9,8},{10,11... | collective-permute-start | bytes 2359304 | tf_op jit(solution)/shard_map/ppermute | solution.py:219
  575.9 21.1 %slice-start.2 = ((s8[4718592]{0:T(1024)(128)(4,1)}), s8[524288]{0:T(1024)(128)(4,1)S(1)}, s32[]{:S(2)}) async-start(s8[4718592]{0:T(1024)(128)(4,1)} %bitcast.183), calls=%async_computation.14 | async-start | bytes 1048576
  (56 other events, 264.4 us)
Sparse Core Ops, SparseCore 0:
  124.6 26.1 all-gather.10
  152.6 35.6 all-gather.8
  190.2 38.9 all-gather.12
  231.5 38.8 all-gather.14
  369.3 37.7 reduce-scatter.6
  410.8 48.1 reduce-scatter.4
  462.9 53.8 reduce-scatter.8
  520.2 53.8 reduce-scatter.10

commit v3 on v2

--- a/solution.py
+++ b/solution.py
@@ -420,23 +420,42 @@
             pl.when(valid)(lambda copy=copy: copy().wait_send())
 
 
-def gather_item(place, own, whole, local_sem, line_sems, chip_sems, core_sems):
+def cut(begin, size):
+    first = size // 32 * 16
+    return ((begin, first), (begin + first, size - first))
+
+
+def place_side_by_side(slots, rows, out):
+    width = slots.shape[2]
+    for col in range(slots.shape[0]):
+        out[rows, col * width : (col + 1) * width] = slots[col, rows, :]
+
+
+def take_apart(whole, rows, slots):
+    width = slots.shape[2]
+    for col in range(slots.shape[0]):
+        slots[col, rows, :] = whole[rows, col * width : (col + 1) * width]
+
+
+def gather_item(place, own, slots, wide, whole, piece, local_sems, line_sems, chip_sems, core_sems):
     hops = place.cols - 1
-    row_slot = lambda col: whole.at[col, place.row // 2, place.core]
-    line = LineGather(place, own, row_slot, line_sems)
-    mine = lambda: pltpu.make_async_copy(own, row_slot(place.col), local_sem)
-    half = place.cols // 2
+    rows = pl.ds(*piece)
+    line = LineGather(place, own.at[rows], lambda col: slots.at[col, rows], line_sems)
+    mine = lambda: pltpu.make_async_copy(own.at[rows], slots.at[place.col, rows], local_sems.at[0])
+    home = lambda: pltpu.make_async_copy(
+        wide.at[rows], whole.at[place.row // 2, place.core, rows], local_sems.at[1]
+    )
 
     def chip_copies(phase, receiving):
-        for part in range(2):
+        for part, span in enumerate(cut(*piece)):
             order = place.orders[part]
             bit = order[phase]
             for index, row in enumerate(place.others(order[:phase])):
                 if receiving:
                     row = place.flipped(row, bit)
-                ref = whole.at[pl.ds(part * half, half), row // 2, row % 2]
+                ref = whole.at[row // 2, row % 2, pl.ds(*span)]
                 yield remote(
-                    ref,
+                    wide.at[pl.ds(*span)] if index == 0 else ref,
                     ref,
                     chip_sems.at[0, phase, part, index],
                     chip_sems.at[1, phase, part, index],
@@ -444,7 +463,7 @@
                 )
 
     def core_copy(receiving):
-        ref = whole.at[:, :, 1 - place.core if receiving else place.core]
+        ref = whole.at[:, 1 - place.core if receiving else place.core, rows]
         return remote(ref, ref, core_sems.at[0], core_sems.at[1], place.partner(0))
 
     phases = len(place.bits)
@@ -461,15 +480,19 @@
         if phase == 0:
             line.wait_recv(hops - 1)
             mine().wait()
+            place_side_by_side(slots, rows, wide)
         else:
             for copy in chip_copies(phase - 1, True):
                 copy.wait_recv()
         for copy in chip_copies(phase, False):
             copy.start()
+        if phase == 0:
+            home().start()
 
     def core_stage():
         for copy in chip_copies(phases - 1, True):
             copy.wait_recv()
+        home().wait()
         core_copy(False).start()
 
     def last():
@@ -489,10 +512,10 @@
     )
 
 
-def gather_small_item(place, own, whole, local_sem, line_sems):
+def gather_line_item(place, own, slots, wide, local_sem, line_sems):
     hops = place.cols - 1
-    line = LineGather(place, own, lambda col: whole.at[col], line_sems)
-    mine = lambda: pltpu.make_async_copy(own, whole.at[place.col], local_sem)
+    line = LineGather(place, own, lambda col: slots.at[col], line_sems)
+    mine = lambda: pltpu.make_async_copy(own, slots.at[place.col], local_sem)
 
     def first():
         mine().start()
@@ -505,6 +528,8 @@
     def last():
         line.wait_recv(hops - 1)
         mine().wait()
+        if wide is not None:
+            place_side_by_side(slots, slice(None), wide)
         for hop in range(hops):
             line.wait_send(hop)
 
@@ -548,20 +573,24 @@
 def gather_kernel(rows, cols, *refs):
     (full, lined), (small, tokens, marks) = (refs[:4], refs[4:8]), refs[8:11]
     (full_out, lined_out), (small_out, hidden, marks_out) = (refs[11:15], refs[15:19]), refs[19:22]
-    local_sems, line_sems, chip_sems, core_sems, exchange_sems = refs[22:]
+    slots, wide, lined_slots = refs[22:26], refs[26:30], refs[30:34]
+    local_sems, line_sems, chip_sems, core_sems, exchange_sems = refs[34:]
     place = Place(rows, cols)
     place.greet()
     items = [
         (0, exchange_item(place, marks, marks_out, exchange_sems.at[1], 16)),
-        (0, gather_small_item(place, small, small_out, local_sems.at[0], line_sems.at[0])),
+        (0, gather_line_item(place, small, small_out, None, local_sems.at[0, 0], line_sems.at[0])),
     ]
     number = 0
-    for own, whole in zip(full, full_out):
-        for begin, size in row_pieces(own.shape[0]):
+    for index in range(4):
+        for piece in row_pieces(full[index].shape[0]):
             stages = gather_item(
                 place,
-                own.at[pl.ds(begin, size)],
-                whole.at[:, :, :, pl.ds(begin, size)],
+                full[index],
+                slots[index],
+                wide[index],
+                full_out[index],
+                piece,
                 local_sems.at[number + 1],
                 line_sems.at[number + 1],
                 chip_sems.at[number],
@@ -570,11 +599,17 @@
             items.append((number, stages))
             number += 1
     items.append((number, exchange_item(place, tokens, hidden, exchange_sems.at[0], 16)))
-    for index, (own, whole) in enumerate(zip(lined, lined_out)):
+    for index in range(4):
         at = number + index
-        items.append(
-            (at, gather_small_item(place, own, whole, local_sems.at[at + 1], line_sems.at[at + 1]))
+        stages = gather_line_item(
+            place,
+            lined[index],
+            lined_slots[index],
+            lined_out[index],
+            local_sems.at[at + 1, 0],
+            line_sems.at[at + 1],
         )
+        items.append((at, stages))
     run_stages(items)
 
 
@@ -582,21 +617,28 @@
     number = sum(len(row_pieces(x.shape[0])) for x in full)
     phases = rows.bit_length() - 2
     like = lambda x, lead=(): jax.ShapeDtypeStruct(lead + x.shape, x.dtype)
-    outs = [like(x, (cols, rows // 2, 2)) for x in full] + [like(x, (cols,)) for x in lined]
+    wide = [(x.shape[0], cols * x.shape[1]) for x in full]
+    outs = [jax.ShapeDtypeStruct((rows // 2, 2) + shape, BF16) for shape in wide]
+    outs += [jax.ShapeDtypeStruct(shape, BF16) for shape in wide]
     outs += [like(small, (cols,)), like(tokens), like(marks)]
     return pl.pallas_call(
         functools.partial(gather_kernel, rows, cols),
         out_shape=tuple(outs),
         in_specs=[ANY_SPEC] * 11,
-        out_specs=(ANY_SPEC,) * 11,
-        scratch_shapes=[
-            DMA((number + len(lined) + 1,)),
+        out_specs=(ANY_SPEC,) * 4 + (VMEM_SPEC,) * 4 + (ANY_SPEC,) * 3,
+        scratch_shapes=[pltpu.VMEM((cols,) + x.shape, BF16) for x in full]
+        + [pltpu.VMEM(shape, BF16) for shape in wide]
+        + [pltpu.VMEM((cols,) + x.shape, BF16) for x in lined]
+        + [
+            DMA((number + len(lined) + 1, 2)),
             DMA((number + len(lined) + 1, 2, 2, cols - 1)),
             DMA((number, 2, phases, 2, 2 ** (phases - 1))),
             DMA((number, 2)),
             DMA((2, 3)),
         ],
-        compiler_params=pltpu.CompilerParams(collective_id=0, has_side_effects=True),
+        compiler_params=pltpu.CompilerParams(
+            collective_id=0, has_side_effects=True, vmem_limit_bytes=50 << 20
+        ),
     )(*full, *lined, small, tokens, marks)
 
 
@@ -676,47 +718,48 @@
     )
 
 
-def reduce_item(place, partial, out, sums, from_core, from_chips, from_line, sems):
+def reduce_item(place, partial, out, sums, from_core, from_chips, slots, from_line, piece, sems):
     local_sem, core_sems, chip_sems, line_sems = sems
-    half = place.cols // 2
     phases = len(place.bits)
+    rows = pl.ds(*piece)
     core_copy = lambda: remote(
-        partial.at[:, :, 1 - place.core], from_core, core_sems.at[0], core_sems.at[1], place.partner(0)
-    )
-    load = lambda: pltpu.make_async_copy(partial.at[:, :, place.core], sums, local_sem)
+        partial.at[:, 1 - place.core, rows],
+        from_core.at[:, rows],
+        core_sems.at[0],
+        core_sems.at[1],
+        place.partner(0),
+    )
+    load = lambda: pltpu.make_async_copy(
+        partial.at[:, place.core, rows], sums.at[:, rows], local_sem
+    )
     line = LineReduce(
-        place, lambda col: sums.at[col, place.row // 2], from_line, line_sems
+        place, lambda col: slots.at[col, rows], from_line.at[:, :, rows], line_sems
     )
 
     def chip_parts(phase):
-        for part in range(2):
+        for part, span in enumerate(cut(*piece)):
             order = place.orders[part][::-1]
-            yield part, order[phase], order[phase + 1 :]
+            yield part, pl.ds(*span), order[phase], order[phase + 1 :]
 
     def chip_copies(phase):
-        for part, bit, rest in chip_parts(phase):
+        for part, span, bit, rest in chip_parts(phase):
             for index, row in enumerate(place.others(rest)):
                 row = place.flipped(row, bit)
                 yield remote(
-                    sums.at[pl.ds(part * half, half), row // 2],
-                    from_chips[phase].at[part, index],
+                    sums.at[row // 2, span],
+                    from_chips[phase].at[index, span],
                     chip_sems.at[0, phase, part, index],
                     chip_sems.at[1, phase, part, index],
                     place.partner(bit),
                 )
 
     def chip_take(phase):
-        for part, _, rest in chip_parts(phase):
+        for part, span, _, rest in chip_parts(phase):
             for index, row in enumerate(place.others(rest)):
-                arrived = from_chips[phase].at[part, index]
+                arrived = from_chips[phase].at[index, span]
                 pltpu.make_async_copy(arrived, arrived, chip_sems.at[1, phase, part, index]).wait()
-
-                def add(col, carry, part=part, index=index, row=row):
-                    ref = sums.at[part * half + col, row // 2]
-                    ref[...] = ref[...] + from_chips[phase].at[part, index, col][...]
-                    return carry
-
-                lax.fori_loop(0, half, add, 0)
+                ref = sums.at[row // 2, span]
+                ref[...] = ref[...] + arrived[...]
 
     def first():
         core_copy().start()
@@ -727,17 +770,20 @@
             load().wait()
             core_copy().wait_recv()
 
-            def add(slot, carry):
-                col, pair = slot // (place.rows // 2), slot % (place.rows // 2)
-                ref = sums.at[col, pair]
-                ref[...] = ref[...] + from_core.at[col, pair][...]
+            def add(pair, carry):
+                ref = sums.at[pair, rows]
+                ref[...] = ref[...] + from_core.at[pair, rows][...]
                 return carry
 
-            lax.fori_loop(0, place.cols * (place.rows // 2), add, 0)
+            lax.fori_loop(0, place.rows // 2, add, 0)
         else:
             chip_take(phase - 1)
         for copy in chip_copies(phase):
             copy.start()
+
+    def to_slots():
+        chip_take(phases - 1)
+        take_apart(sums.at[place.row // 2], rows, slots)
 
     def last():
         core_copy().wait_send()
@@ -748,15 +794,14 @@
     return (
         [first]
         + [functools.partial(chip_stage, phase) for phase in range(phases)]
-        + line_stages(line, out, lambda: chip_take(phases - 1))
+        + line_stages(line, out.at[rows], to_slots)
         + [last]
     )
 
 
-def reduce_line_item(place, partial, out, sums, from_line, local_sem, line_sems):
-    load = lambda: pltpu.make_async_copy(partial, sums, local_sem)
-    line = LineReduce(place, lambda col: sums.at[col], from_line, line_sems)
-    return [lambda: load().start()] + line_stages(line, out, lambda: load().wait())
+def reduce_line_item(place, partial, out, slots, from_line, line_sems):
+    line = LineReduce(place, lambda col: slots.at[col], from_line, line_sems)
+    return line_stages(line, out, lambda: take_apart(partial, slice(None), slots))
 
 
 def reduce_small_item(place, partial, out, sums, arrived, from_line, sems, line_sems):
@@ -804,29 +849,28 @@
     )
     time = 0
     for index in range(full):
-        sums, from_core, from_line = take(3)
+        sums, from_core, slots, from_line = take(4)
         from_chips = take(phases)
         local_sems, core_sems, chip_sems, line_sems = take(4)
-        for piece, (begin, size) in enumerate(row_pieces(full_in[index].shape[-2])):
-            rows_of = lambda ref, begin=begin, size=size: ref.at[
-                (slice(None),) * (len(ref.shape) - 2) + (pl.ds(begin, size),)
-            ]
+        for number, piece in enumerate(row_pieces(full_in[index].shape[2])):
             stages = reduce_item(
                 place,
-                rows_of(full_in[index]),
-                rows_of(full_out[index]),
-                rows_of(sums),
-                rows_of(from_core),
-                [rows_of(ref) for ref in from_chips],
-                rows_of(from_line),
-                (local_sems.at[piece], core_sems.at[piece], chip_sems.at[piece], line_sems.at[piece]),
+                full_in[index],
+                full_out[index],
+                sums,
+                from_core,
+                from_chips,
+                slots,
+                from_line,
+                piece,
+                (local_sems.at[number], core_sems.at[number], chip_sems.at[number], line_sems.at[number]),
             )
             items.append((time, stages))
             time += 1
     for index in range(lined):
-        sums, from_line, local_sem, line_sems = take(4)
+        slots, from_line, line_sems = take(3)
         items.append(
-            (index, reduce_line_item(place, line_in[index], line_out[index], sums, from_line, local_sem.at[0], line_sems))
+            (index, reduce_line_item(place, line_in[index], line_out[index], slots, from_line, line_sems))
         )
     items.append(
         (1, reduce_small_item(place, small_in, small_out, small_sums, small_arrived, small_line, small_sems, small_line_sems))
@@ -840,28 +884,29 @@
 def reduce_all(rows, cols, full, lined, small, tokens):
     phases = rows.bit_length() - 2
     hops = cols - 1
-    shard = lambda x: x.shape[-2:]
-    outs = [jax.ShapeDtypeStruct(shard(x), F32) for x in (*full, *lined, small)]
+    shard = lambda x: (x.shape[-2], x.shape[-1] // cols)
+    outs = [jax.ShapeDtypeStruct(shard(x), F32) for x in (*full, *lined)]
+    outs.append(jax.ShapeDtypeStruct(small.shape[1:], F32))
     outs.append(jax.ShapeDtypeStruct(tokens.shape, tokens.dtype))
     scratch = [
         pltpu.VMEM(small.shape, F32),
         pltpu.VMEM((phases + 1,) + small.shape, F32),
-        pltpu.VMEM((2, hops) + shard(small), F32),
+        pltpu.VMEM((2, hops) + small.shape[1:], F32),
         DMA((2, phases + 1)),
         DMA((2, 2, hops)),
         DMA((2,)),
     ]
     for x in full:
+        count = len(row_pieces(x.shape[2]))
         scratch += [
-            pltpu.VMEM((cols, rows // 2) + shard(x), BF16),
-            pltpu.VMEM((cols, rows // 2) + shard(x), BF16),
+            pltpu.VMEM((rows // 2,) + x.shape[2:], BF16),
+            pltpu.VMEM((rows // 2,) + x.shape[2:], BF16),
+            pltpu.VMEM((cols,) + shard(x), BF16),
             pltpu.VMEM((2, hops) + shard(x), BF16),
         ]
         scratch += [
-            pltpu.VMEM((2, 2 ** (phases - 1 - phase), cols // 2) + shard(x), BF16)
-            for phase in range(phases)
+            pltpu.VMEM((2 ** (phases - 1 - phase),) + x.shape[2:], BF16) for phase in range(phases)
         ]
-        count = len(row_pieces(x.shape[-2]))
         scratch += [
             DMA((count,)),
             DMA((count, 2)),
@@ -872,18 +917,16 @@
         scratch += [
             pltpu.VMEM((cols,) + shard(x), BF16),
             pltpu.VMEM((2, hops) + shard(x), BF16),
-            DMA((1,)),
             DMA((2, 2, hops)),
         ]
-    many = len(full) + len(lined)
     return pl.pallas_call(
         functools.partial(reduce_kernel, rows, cols, len(full), len(lined)),
         out_shape=tuple(outs),
-        in_specs=[ANY_SPEC] * many + [VMEM_SPEC, ANY_SPEC],
-        out_specs=(VMEM_SPEC,) * (many + 1) + (ANY_SPEC,),
+        in_specs=[ANY_SPEC] * len(full) + [VMEM_SPEC] * (len(lined) + 1) + [ANY_SPEC],
+        out_specs=(VMEM_SPEC,) * (len(full) + len(lined) + 1) + (ANY_SPEC,),
         scratch_shapes=scratch,
         compiler_params=pltpu.CompilerParams(
-            collective_id=1, has_side_effects=True, vmem_limit_bytes=62 << 20
+            collective_id=1, has_side_effects=True, vmem_limit_bytes=60 << 20
         ),
     )(*full, *lined, small, tokens)
 
@@ -918,13 +961,8 @@
     rand = marks[:, 2 * lines, : half // BLOCK * rand_blocks.shape[2]]
     pattern = key_pattern(seg, pad, rand.reshape(-1, rand_blocks.shape[2]))
 
-    def assembled(slots):
-        return slots.transpose(1, 2, 0, 3).reshape(rows * slots.shape[2], -1)
-
-    first_mats = [assembled(g.reshape((cols, rows) + g.shape[3:])) for g in got[:4]]
-    second_mats = [
-        assembled(lax.all_gather(g, "row", axis=0).transpose(1, 0, 2, 3)) for g in got[4:8]
-    ]
+    first_mats = [g.reshape(-1, g.shape[3]) for g in got[:4]]
+    second_mats = [lax.all_gather(g, "row", axis=0, tiled=True) for g in got[4:8]]
     weights = [
         (*layer_mats, vectors[layer], up_biases[layer])
         for layer, layer_mats in enumerate((first_mats, second_mats))
@@ -940,14 +978,13 @@
         flow, grads[layer], vec_grads[layer], up_grads[layer] = layer_backward(
             flow, weights[layer], kept[layer], pattern
         )
-    full = []
-    for mat in grads[0]:
-        mat = mat.astype(BF16).reshape(rows // 2, 2, mat.shape[0] // rows, cols, -1)
-        full.append(mat.transpose(3, 0, 1, 2, 4))
-    lined = []
-    for mat in grads[1]:
-        mat = lax.psum_scatter(mat.astype(BF16), "row", scatter_dimension=0, tiled=True)
-        lined.append(mat.reshape(mat.shape[0], cols, -1).transpose(1, 0, 2))
+    full = [
+        mat.astype(BF16).reshape(rows // 2, 2, -1, mat.shape[1]) for mat in grads[0]
+    ]
+    lined = [
+        lax.psum_scatter(mat.astype(BF16), "row", scatter_dimension=0, tiled=True)
+        for mat in grads[1]
+    ]
     small = jnp.concatenate(
         [
             jnp.stack(vec_grads).reshape(layers * 8, cols, part).transpose(1, 0, 2),

time: 751 us -> 645 us (0.86)
  local copies, waits for them, and re-layouts: 186 us -> 33.8 us
  waiting for transfers between devices: 1.51 us -> 46.9 us
  other arithmetic: 46.6 us -> 38.1 us
    reshape x22 -> x0, local copies, waits for them, and re-layouts: 103 us -> none  [the longest x8 51.5 us: shards(): mat = mat.astype(BF16).reshape(rows // 2, 2, mat.shape[0] // rows, cols, -1)]
    reduce_scatter x4, waiting for transfers between devices: 0.01 us -> 25.8 us  [shards(): lax.psum_scatter(mat.astype(BF16), 'row', scatter_dimension=0, tiled=True)]
    all_gather x4 -> x0, local copies, waits for them, and re-layouts: 20 us -> none  [shards(): lax.all_gather(g, 'row', axis=0).transpose(1, 0, 2, 3)]
    all_gather x4, waiting for transfers between devices: 0.03 us -> 19.7 us  [shards(): lax.all_gather(g, 'row', axis=0, tiled=True)]
    unnamed x164 -> x116, local copies, waits for them, and re-layouts: 33 us -> 20.5 us
  transfers between devices with their start and end apart: 10 -> 10, of which waited for: 0 -> 2; matrix products, arithmetic and copies ran while one was open for 42% -> 28% of each run, Pallas kernels for 14% -> 16%
where the time goes in v3:
time: 645 us; the launch traced here: 636 us
  Pallas kernels  320 us (50%)
  matrix products  180 us (28%)
  waiting for transfers between devices  46.9 us (7%)
  other arithmetic  38.1 us (6%)
  local copies, waits for them, and re-layouts  33.8 us (5%)
  between operations  15.4 us (2%)
    pallas_call x1, Pallas kernels, reduce_all(): pl.pallas_call(functools.partial(reduce_kernel, rows, cols, len(full), le...  110 us
    pallas_call x1, Pallas kernels, gather_all(): pl.pallas_call(functools.partial(gather_kernel, rows, cols), out_shape=tu...  107 us
    pallas_call x2, Pallas kernels, attend_back(): pl.pallas_call(attend_back_kernel, out_shape=jax.ShapeDtypeStruct((length...  58.4 us
    pallas_call x2, Pallas kernels, attend(): pl.pallas_call(attend_kernel, out_shape=(jax.ShapeDtypeStruct((length, mo...  45.7 us
    dot_general x2, matrix products, layer_backward(): jnp.einsum('td,fd->tf', grad_down_low, mat_down, preferred_element_type=F32)  28.2 us
    reduce_scatter x4, waiting for transfers between devices, shards(): lax.psum_scatter(mat.astype(BF16), 'row', scatter_dimension=0, tiled=True)  25.8 us
    dot_general x2, matrix products, layer_forward(): pre_act = jnp.dot(first_out, mat_up, preferred_element_type=F32) + up_bias  24.4 us
    unnamed x116, local copies, waits for them, and re-layouts  20.5 us
  transfers between devices with their start and end apart: 10, of which 2 were waited for; matrix products, arithmetic and copies ran while one was open for 28% of the time, Pallas kernels for 16%

profile of v3, /device:TPU:0, one launch (start us, length us, event | category | flops | bytes accessed | tf_op | source)
XLA Modules:
  0.0 636.2 jit_solution(3046424320832298161)
XLA Ops:
  15.1 106.7 %shard_map.170 = (bf16[4,2,96,2304]{3,2,1,0:T(8,128)(2,1)}, bf16[4,2,96,768]{3,2,1,0:T(8,128)(2,1)S(1)}, bf16[4,2,96,3072]{3,2,1,0:T(8,128)(2,1)}, bf16[4,2,384,...) custom-call(bf16[96,576]{1,0:T(8,128)(2,1)S(1)} %get-tuple-element.1, ...), custom_call_target="tpu_custom_call" | custom-call | tf_op jit(solution)/shard_map/pallas_call | solution.py:624
  127.5 6.2 add_convert_fusion.1.qkv_ref
  133.8 3.3 fusion.17.bias_ref
  137.1 22.7 %shard_map.171 = (bf16[1024,768]{1,0:T(8,128)(2,1)S(1)}, f32[6,8,256]{2,1,0:T(8,128)S(1)}) custom-call(s32[8]{0:T(128)S(1)} %get-tuple-element.117.first_ref, s32[8]{0:T(128)S(1)} %get-tuple-element.116.count_ref, bf16[1024,2304]{1,0:T(8,128)(2,1)S(1)} %add_convert_fusion.1.qkv_ref, f32[1024,1024]{1,0:T(8,128)S(1)} %fusion.17.bias_ref), custom_call_target="tpu_custom_call" | custom-call | tf_op jit(solution)/shard_map/pallas_call | solution.py:155
  163.8 11.7 %multiply_convert_fusion.1 = (bf16[1024,3072]{1,0:T(8,128)(2,1)S(1)}, f32[1024,3072]{1,0:T(8,128)}) fusion(f32[3072]{0:T(1024)S(1)} %bitcast.148, bf16[768,3072]{1,0:T(8,128)(2,1)} %bitcast.155, f32[1024,768]{1,0:T(8,128)} %copy-done.10, f32[768]{0:T(1024)S(1)} %get-tuple-element.101, f32[768]{0:T(1024)S(1)} %get-tuple-element.102, ...), kind=kOutput, calls=%fused_computation.16 | convolution fusion | flops 4854644736 | bytes 26765312 | tf_op jit(solution)/shard_map/dot_general | solution.py:276
  178.1 7.8 %fusion.51 = (f32[1024]{0:T(1024)S(1)}, f32[1024,768]{1,0:T(8,128)S(1)}) fusion(f32[768]{0:T(1024)S(1)} %get-tuple-element.100, bf16[1024,3072]{1,0:T(8,128)(2,1)S(1)} %get-tuple-element.146, bf16[3072,768]{1,0:T(8,128)(2,1)} %bitcast.157, f32[768]{0:T(1024)S(1)} %get-tuple-element.101, f32[768]{0:T(1024)S(1)} %get-tuple-element.102, ...), kind=kOutput, calls=%fused_computation.195 | convolution fusion | flops 4838915072 | bytes 17323008 | tf_op jit(solution)/shard_map/dot_general | solution.py:278
  191.0 6.6 %add_convert_fusion.qkv_ref = bf16[1024,2304]{1,0:T(8,128)(2,1)S(1)} fusion(bf16[768,2304]{1,0:T(8,128)(2,1)} %all-gather.5.cloned.1.call-done, f32[2304]{0:T(1024)S(1)} %get-tuple-element.142, f32[1024,768]{1,0:T(8,128)S(1)} %get-tuple-element.149, f32[768]{0:T(1024)S(1)} %get-tuple-element.98, f32[768]{0:T(1024)S(1)} %get-tuple-element.99, ...), kind=kOutput, calls=%fused_computation.20 | convolution fusion | flops 3632529408 | bytes 11426816 | tf_op jit(solution)/shard_map/dot_general | solution.py:269
  197.7 23.0 %shard_map.172 = (bf16[1024,768]{1,0:T(8,128)(2,1)S(1)}, f32[6,8,256]{2,1,0:T(8,128)S(1)}) custom-call(s32[8]{0:T(128)S(1)} %get-tuple-element.117.first_ref, s32[8]{0:T(128)S(1)} %get-tuple-element.116.count_ref, bf16[1024,2304]{1,0:T(8,128)(2,1)S(1)} %add_convert_fusion.qkv_ref, f32[1024,1024]{1,0:T(8,128)S(1)} %copy-done.1), custom_call_target="tpu_custom_call" | custom-call | tf_op jit(solution)/shard_map/pallas_call | solution.py:155
  222.8 4.1 fusion.52
  229.3 12.7 %multiply_convert_fusion = (bf16[1024,3072]{1,0:T(8,128)(2,1)}, f32[1024,3072]{1,0:T(8,128)}) fusion(f32[3072]{0:T(1024)S(1)} %bitcast.150, bf16[768,3072]{1,0:T(8,128)(2,1)} %all-gather.9.cloned.1.call-done, f32[1024,768]{1,0:T(8,128)} %copy-done.14, f32[768]{0:T(1024)S(1)} %get-tuple-element.93, f32[768]{0:T(1024)S(1)} %get-tuple-element.94, ...), kind=kOutput, calls=%fused_computation.14 | convolution fusion | flops 4854644736 | bytes 26765312 | tf_op jit(solution)/shard_map/dot_general | solution.py:276
  242.0 19.6 %all-gather.11.cloned.1.call-done = bf16[3072,768]{1,0:T(8,128)(2,1)} async-done(((bf16[384,768]{1,0:T(8,128)(2,1)}), bf16[3072,768]{1,0:T(8,128)(2,1)}) %all-gather.11.cloned.1.call-update) | async-done | bytes 4718608 | tf_op jit(solution)/shard_map/all_gather | solution.py:965
  261.6 9.3 %fusion.53 = (f32[1024]{0:T(1024)S(1)}, f32[1024,768]{1,0:T(8,128)S(1)}) fusion(f32[768]{0:T(1024)S(1)} %get-tuple-element.92, bf16[1024,3072]{1,0:T(8,128)(2,1)} %get-tuple-element.152, bf16[3072,768]{1,0:T(8,128)(2,1)} %all-gather.11.cloned.1.call-done, f32[768]{0:T(1024)S(1)} %get-tuple-element.93, f32[768]{0:T(1024)S(1)} %get-tuple-element.94, ...), kind=kOutput, calls=%fused_computation.197 | convolution fusion | flops 4838915072 | bytes 17323008 | tf_op jit(solution)/shard_map/dot_general | solution.py:278
  277.9 13.2 %convert_reduce_fusion = (f32[3072]{0:T(1024)S(1)}, bf16[1024,3072]{1,0:T(8,128)(2,1)S(1)}) fusion(f32[1024,3072]{1,0:T(8,128)} %get-tuple-element.153, f32[3072]{0:T(1024)S(1)} %bitcast.151, bf16[3072,768]{1,0:T(8,128)(2,1)S(1)} %copy-done.40, f32[1024,768]{1,0:T(8,128)S(1)} %get-tuple-element.113), kind=kOutput, calls=%fused_computation.12 | convolution fusion | flops 4873516032 | bytes 26763264 | tf_op jit(solution)/shard_map/td,fd->tf/dot_general | solution.py:301
  291.2 6.0 multiply_reduce_fusion
  302.7 3.5 convolution_convert_fusion.7.grad_ref
  306.2 29.0 %shard_map.173 = bf16[1024,2304]{1,0:T(8,128)(2,1)} custom-call(s32[8]{0:T(128)S(1)} %get-tuple-element.117.first_ref, s32[8]{0:T(128)S(1)} %get-tuple-element.116.count_ref, bf16[1024,2304]{1,0:T(8,128)(2,1)} %copy-done.5, bf16[1024,768]{1,0:T(8,128)(2,1)S(1)} %convolution_convert_fusion.7.grad_ref, f32[1024,1024]{1,0:T(8,128)S(1)} %copy-done.2, ...), custom_call_target="tpu_custom_call" | custom-call | tf_op jit(solution)/shard_map/pallas_call | solution.py:171
  335.2 8.0 %convolution_convert_fusion.4 = bf16[768,2304]{1,0:T(8,128)(2,1)} fusion(bf16[1024,2304]{1,0:T(8,128)(2,1)} %shard_map.173, f32[1024,768]{1,0:T(8,128)S(1)} %copy-done.18, f32[768]{0:T(1024)S(1)} %get-tuple-element.98, f32[768]{0:T(1024)S(1)} %get-tuple-element.99, f32[1024]{0:T(1024)S(1)} %add_rsqrt_fusion.2, f32[1024]{0:T(1024)S(1)} %broadcast_multiply_fusion.10), kind=kOutput, calls=%fused_computation.26 | convolution fusion | flops 3629580288 | bytes 11417600 | tf_op jit(solution)/shard_map/td,te->de/dot_general | solution.py:314
  343.3 10.6 %multiply_reduce_fusion.1 = (f32[768]{0:T(1024)S(1)}, f32[1024]{0:T(1024)S(1)}, f32[1024]{0:T(1024)S(1)}, f32[768]{0:T(1024)S(1)}, f32[1024,768]{1,0:T(8,128)}) fusion(f32[1024,768]{1,0:T(8,128)S(1)} %copy-done.18, f32[1024]{0:T(1024)S(1)} %add_rsqrt_fusion.2, f32[1024]{0:T(1024)S(1)} %broadcast_multiply_fusion.10, f32[768]{0:T(1024)S(1)} %get-tuple-element.99, ...), kind=kOutput, calls=%fused_computation.51 | convolution fusion | flops 3631739392 | bytes 17720320 | tf_op jit(solution)/shard_map/te,de->td/dot_general | solution.py:315
  353.9 10.2 %convolution_convert_fusion = bf16[3072,768]{1,0:T(8,128)(2,1)} fusion(bf16[1024,3072]{1,0:T(8,128)(2,1)} %get-tuple-element.152, f32[1024,768]{1,0:T(8,128)S(1)} %copy-done.23), kind=kOutput, calls=%fused_computation.22 | convolution fusion | flops 4834983936 | bytes 14155776 | tf_op jit(solution)/shard_map/tf,td->fd/dot_general | solution.py:300
  364.2 3.0 convert_reduce_fusion.9
  367.3 15.0 %convert_reduce_fusion.1 = (f32[3072]{0:T(1024)S(1)}, bf16[1024,3072]{1,0:T(8,128)(2,1)}) fusion(f32[1024,3072]{1,0:T(8,128)} %get-tuple-element.147, f32[3072]{0:T(1024)S(1)} %bitcast.149, bf16[3072,768]{1,0:T(8,128)(2,1)} %bitcast.158, f32[1024,768]{1,0:T(8,128)S(1)} %get-tuple-element.109), kind=kOutput, calls=%fused_computation.13 | convolution fusion | flops 4873516032 | bytes 26763264 | tf_op jit(solution)/shard_map/td,fd->tf/dot_general | solution.py:301
  382.4 10.4 %multiply_reduce_fusion.2 = (f32[768]{0:T(1024)S(1)}, f32[1024]{0:T(1024)S(1)}, f32[1024]{0:T(1024)S(1)}, f32[768]{0:T(1024)S(1)}, f32[1024,768]{1,0:T(8,128)S(1)}) fusion(f32[1024,768]{1,0:T(8,128)S(1)} %copy-done.12, f32[1024]{0:T(1024)S(1)} %add_rsqrt_fusion.3, f32[1024]{0:T(1024)S(1)} %broadcast_multiply_fusion.11, f32[768]{0:T(1024)S(1)} %get-tuple-element.102, ...), kind=kOutput, calls=%fused_computation.52 | convolution fusion | flops 4839698432 | bytes 20472832 | tf_op jit(solution)/shard_map/tf,df->td/dot_general | solution.py:305
  395.2 3.2 convert_reduce_fusion.2
  401.2 29.4 %shard_map.174 = bf16[1024,2304]{1,0:T(8,128)(2,1)} custom-call(s32[8]{0:T(128)S(1)} %get-tuple-element.117.first_ref, s32[8]{0:T(128)S(1)} %get-tuple-element.116.count_ref, bf16[1024,2304]{1,0:T(8,128)(2,1)} %copy-done.4, bf16[1024,768]{1,0:T(8,128)(2,1)S(1)} %convolution_convert_fusion.6.grad_ref, f32[1024,1024]{1,0:T(8,128)S(1)} %copy-done.3, ...), custom_call_target="tpu_custom_call" | custom-call | tf_op jit(solution)/shard_map/pallas_call | solution.py:171
  430.6 3.2 convert_reduce_fusion.3
  434.0 7.9 %convolution_convert_fusion.1 = bf16[768,3072]{1,0:T(8,128)(2,1)} fusion(bf16[1024,3072]{1,0:T(8,128)(2,1)S(1)} %bitcast.167, f32[1024,768]{1,0:T(8,128)S(1)} %copy-done.16, f32[768]{0:T(1024)S(1)} %get-tuple-element.93, f32[768]{0:T(1024)S(1)} %get-tuple-element.94, f32[1024]{0:T(1024)S(1)} %add_rsqrt_fusion.1, f32[1024]{0:T(1024)S(1)} %broadcast_multiply_fusion.9), kind=kOutput, calls=%fused_computation.23 | convolution fusion | flops 4838129664 | bytes 14170112 | tf_op jit(solution)/shard_map/td,tf->df/dot_general | solution.py:304
  445.1 8.4 %convolution_add_fusion.2 = f32[1024,768]{1,0:T(8,128)S(1)} fusion(f32[1024,768]{1,0:T(8,128)} %get-tuple-element.111, bf16[1024,2304]{1,0:T(8,128)(2,1)} %shard_map.174, bf16[768,2304]{1,0:T(8,128)(2,1)} %bitcast.162), kind=kOutput, calls=%fused_computation.84 | convolution fusion | flops 3624665088 | bytes 14548992 | tf_op jit(solution)/shard_map/te,de->td/dot_general | solution.py:315
  458.8 7.9 %convolution_convert_fusion.3 = bf16[768,3072]{1,0:T(8,128)(2,1)} fusion(bf16[1024,3072]{1,0:T(8,128)(2,1)S(1)} %bitcast.169, f32[1024,768]{1,0:T(8,128)S(1)} %copy-done.13, f32[768]{0:T(1024)S(1)} %copy-done.39, f32[768]{0:T(1024)S(1)} %get-tuple-element.102, f32[1024]{0:T(1024)S(1)} %add_rsqrt_fusion.3, f32[1024]{0:T(1024)S(1)} %broadcast_multiply_fusion.11), kind=kOutput, calls=%fused_computation.25 | convolution fusion | flops 4838129664 | bytes 14170112 | tf_op jit(solution)/shard_map/td,tf->df/dot_general | solution.py:304
  466.7 7.3 %convolution_convert_fusion.2 = bf16[3072,768]{1,0:T(8,128)(2,1)} fusion(bf16[1024,3072]{1,0:T(8,128)(2,1)S(1)} %bitcast.171, f32[1024,768]{1,0:T(8,128)S(1)} %copy-done.25), kind=kOutput, calls=%fused_computation.24 | convolution fusion | flops 4834983936 | bytes 14155776 | tf_op jit(solution)/shard_map/tf,td->fd/dot_general | solution.py:300
  474.0 5.4 convolution_convert_fusion.5
  480.8 25.8 %reduce-scatter.9.cloned.1.call-done.refs_6_ = bf16[96,3072]{1,0:T(8,128)(2,1)} async-done(((bf16[768,3072]{1,0:T(8,128)(2,1)}), bf16[96,3072]{1,0:T(8,128)(2,1)}) %reduce-scatter.9.cloned.1.call-update) | async-done | bytes 589840 | tf_op jit(solution)/shard_map/reduce_scatter | solution.py:985
  506.6 109.5 %shard_map.175 = (f32[96,576]{1,0:T(8,128)}, f32[96,192]{1,0:T(8,128)}, f32[96,768]{1,0:T(8,128)}, f32[384,192]{1,0:T(8,128)}, f32[96,576]{1,0:T(8,128)}, /*inde...) custom-call(bf16[4,2,96,2304]{3,2,1,0:T(8,128)(2,1)} %bitcast.127, ...), custom_call_target="tpu_custom_call" | custom-call | tf_op jit(solution)/shard_map/pallas_call | solution.py:922
  (251 shorter events, 70.1 us)
Async XLA Ops:
  7.2 183.8 %all-gather.5.cloned.1.call-start = ((), (), s32[]{:S(2)}) async-start(), calls=%async_computation.4 | async-start | bytes 3981312 | tf_op jit(solution)/shard_map/all_gather | solution.py:965
  121.9 38.0 %copy-start.8 = (bf16[4,2,96,768]{3,2,1,0:T(8,128)(2,1)}, bf16[4,2,96,768]{3,2,1,0:T(8,128)(2,1)S(1)}, u32[]{:S(2)}) copy-start(bf16[4,2,96,768]{3,2,1,0:T(8,128)(2,1)S(1)} %get-tuple-element.38) | copy-start | bytes 3538948
  121.9 100.9 %all-gather.7.cloned.1.call-start = ((), (), s32[]{:S(2)}) async-start(), calls=%async_computation.5 | async-start | bytes 1327104 | tf_op jit(solution)/shard_map/all_gather | solution.py:965
  122.6 106.6 %all-gather.9.cloned.1.call-start = ((), (), s32[]{:S(2)}) async-start(), calls=%async_computation.6 | async-start | bytes 5308416 | tf_op jit(solution)/shard_map/all_gather | solution.py:965
  123.4 138.2 %all-gather.11.cloned.1.call-start = ((), (), s32[]{:S(2)}) async-start(), calls=%async_computation.7 | async-start | bytes 5308416 | tf_op jit(solution)/shard_map/all_gather | solution.py:965
  125.5 61.0 %collective-permute-start.1 = (bf16[512,768]{1,0:T(8,128)(2,1)}, bf16[512,768]{1,0:T(8,128)(2,1)}, u32[]{:S(2)}, u32[]{:S(2)}) collective-permute-start(bf16[512,768]{1,0:T(8,128)(2,1)} %dynamic-slice_bitcast_fusion), channel_id=1, source_target_pairs={{0,1},{1,0},{2,3},{3,2},{4,5},{5,4},{6,7},{7,6},{8,9},{9,8},{10,11... | collective-permute-start | bytes 2359304 | tf_op jit(solution)/shard_map/ppermute | solution.py:219
  125.5 355.3 %reduce-scatter.7.cloned.1.call-start = ((), (), s32[]{:S(2)}) async-start(), calls=%async_computation.9 | async-start | bytes 1327104 | tf_op jit(solution)/shard_map/reduce_scatter | solution.py:985
  127.5 48.0 %copy-start.38 = (f32[768]{0:T(1024)}, f32[768]{0:T(1024)S(1)}, u32[]{:S(2)}) copy-start(f32[768]{0:T(1024)S(1)} %get-tuple-element.101) | copy-start | bytes 9220
  133.8 26.1 %copy-start.4 = (bf16[1024,2304]{1,0:T(8,128)(2,1)}, bf16[1024,2304]{1,0:T(8,128)(2,1)S(1)}, u32[]{:S(2)}) copy-start(bf16[1024,2304]{1,0:T(8,128)(2,1)S(1)} %add_convert_fusion.1.qkv_ref) | copy-start | bytes 14155780
  137.1 22.7 %copy-start = (f32[1024,1024]{1,0:T(8,128)}, f32[1024,1024]{1,0:T(8,128)S(1)}, u32[]{:S(2)}) copy-start(f32[1024,1024]{1,0:T(8,128)S(1)} %fusion.17.bias_ref) | copy-start | bytes 12582916
  163.7 14.4 %copy-start.11 = (f32[1024,768]{1,0:T(8,128)S(1)}, f32[1024,768]{1,0:T(8,128)}, u32[]{:S(2)}) copy-start(f32[1024,768]{1,0:T(8,128)} %copy-done.10) | copy-start | bytes 9437188
  274.9 16.2 %slice-start.2 = ((s8[4718592]{0:T(1024)(128)(4,1)}), s8[4194304]{0:T(1024)(128)(4,1)S(1)}, s32[]{:S(2)}) async-start(s8[4718592]{0:T(1024)(128)(4,1)} %bitcast.159), calls=%async_computation.14 | async-start | bytes 8388608
  277.9 13.2 %copy-start.22 = (f32[1024,768]{1,0:T(8,128)}, f32[1024,768]{1,0:T(8,128)S(1)}, u32[]{:S(2)}) copy-start(f32[1024,768]{1,0:T(8,128)S(1)} %get-tuple-element.113) | copy-start | bytes 9437188
  277.9 13.2 %copy-start.15 = (f32[1024,768]{1,0:T(8,128)S(1)}, f32[1024,768]{1,0:T(8,128)}, u32[]{:S(2)}) copy-start(f32[1024,768]{1,0:T(8,128)} %copy-done.14) | copy-start | bytes 9437188
  277.9 13.3 %slice-start.3 = ((s8[4718592]{0:T(1024)(128)(4,1)}), s8[524288]{0:T(1024)(128)(4,1)S(1)}, s32[]{:S(2)}) async-start(s8[4718592]{0:T(1024)(128)(4,1)} %bitcast.159), calls=%async_computation.15 | async-start | bytes 1048576
  302.6 178.2 %reduce-scatter.5.cloned.1.call-start = ((), (), s32[]{:S(2)}) async-start(), calls=%async_computation.8 | async-start | bytes 3981312 | tf_op jit(solution)/shard_map/reduce_scatter | solution.py:985
  306.2 29.0 %copy-start.18 = (f32[1024,768]{1,0:T(8,128)S(1)}, f32[1024,768]{1,0:T(8,128)}, u32[]{:S(2)}) copy-start(f32[1024,768]{1,0:T(8,128)} %copy-done.17) | copy-start | bytes 9437188
  343.2 137.6 %reduce-scatter.11.cloned.1.call-start = ((), (), s32[]{:S(2)}) async-start(), calls=%async_computation.11 | async-start | bytes 5308416 | tf_op jit(solution)/shard_map/reduce_scatter | solution.py:985
  343.3 10.6 %copy-start.23 = (f32[1024,768]{1,0:T(8,128)S(1)}, f32[1024,768]{1,0:T(8,128)}, u32[]{:S(2)}) copy-start(f32[1024,768]{1,0:T(8,128)} %copy-done.22) | copy-start | bytes 9437188
  364.2 142.4 %reduce-scatter.9.cloned.1.call-start = ((), (), s32[]{:S(2)}) async-start(), calls=%async_computation.10 | async-start | bytes 5308416 | tf_op jit(solution)/shard_map/reduce_scatter | solution.py:985
  367.2 15.0 %copy-start.24 = (f32[1024,768]{1,0:T(8,128)}, f32[1024,768]{1,0:T(8,128)S(1)}, u32[]{:S(2)}) copy-start(f32[1024,768]{1,0:T(8,128)S(1)} %get-tuple-element.109) | copy-start | bytes 9437188
  367.3 15.2 %copy-start.12 = (f32[1024,768]{1,0:T(8,128)S(1)}, f32[1024,768]{1,0:T(8,128)}, u32[]{:S(2)}) copy-start(f32[1024,768]{1,0:T(8,128)} %copy-done.10) | copy-start | bytes 9437188
  398.8 35.1 %slice-start.4 = ((s8[6291456]{0:T(1024)(128)(4,1)}), s8[2097152]{0:T(1024)(128)(4,1)S(1)}, s32[]{:S(2)}) async-start(s8[6291456]{0:T(1024)(128)(4,1)} %bitcast.166), calls=%async_computation.16 | async-start | bytes 4194304
  401.2 32.6 %slice-start.5 = ((s8[6291456]{0:T(1024)(128)(4,1)}), s8[4194304]{0:T(1024)(128)(4,1)S(1)}, s32[]{:S(2)}) async-start(s8[6291456]{0:T(1024)(128)(4,1)} %bitcast.166), calls=%async_computation.17 | async-start | bytes 8388608
  443.3 15.4 %slice-start.6 = ((s8[6291456]{0:T(1024)(128)(4,1)}), s8[2097152]{0:T(1024)(128)(4,1)S(1)}, s32[]{:S(2)}) async-start(s8[6291456]{0:T(1024)(128)(4,1)} %bitcast.168), calls=%async_computation.18 | async-start | bytes 4194304
  443.3 36.1 %collective-permute-start = (bf16[512,768]{1,0:T(8,128)(2,1)S(1)}, bf16[512,768]{1,0:T(8,128)(2,1)S(1)}, u32[]{:S(2)}, u32[]{:S(2)}) collective-permute-start(bf16[512,768]{1,0:T(8,128)(2,1)S(1)} %dynamic-slice_bitcast_fusion.1), channel_id=1, source_target_pairs={{0,1},{1,0},{2,3},{3,2},{4,5},{5,4},{6,7},{7,6},{8,9},{9,8},{10,11... | collective-permute-start | bytes 2359304 | tf_op jit(solution)/shard_map/ppermute | solution.py:219
  445.1 11.1 %copy-start.7 = (bf16[1024,768]{1,0:T(8,128)(2,1)S(1)}, bf16[1024,768]{1,0:T(8,128)(2,1)}, u32[]{:S(2)}) copy-start(bf16[1024,768]{1,0:T(8,128)(2,1)} %copy-done.6) | copy-start | bytes 4718596
  445.1 11.1 %copy-start.27 = (f32[1024,768]{1,0:T(8,128)S(1)}, f32[1024,768]{1,0:T(8,128)}, u32[]{:S(2)}) copy-start(f32[1024,768]{1,0:T(8,128)} %get-tuple-element.111) | copy-start | bytes 9437188
  445.1 13.6 %slice-start.7 = ((s8[6291456]{0:T(1024)(128)(4,1)}), s8[4194304]{0:T(1024)(128)(4,1)S(1)}, s32[]{:S(2)}) async-start(s8[6291456]{0:T(1024)(128)(4,1)} %bitcast.168), calls=%async_computation.19 | async-start | bytes 8388608
  456.2 10.5 %slice-start.8 = ((s8[6291456]{0:T(1024)(128)(4,1)}), s8[4194304]{0:T(1024)(128)(4,1)S(1)}, s32[]{:S(2)}) async-start(s8[6291456]{0:T(1024)(128)(4,1)} %bitcast.170), calls=%async_computation.20 | async-start | bytes 8388608
  458.7 8.0 %copy-start.25 = (f32[1024,768]{1,0:T(8,128)S(1)}, f32[1024,768]{1,0:T(8,128)}, u32[]{:S(2)}) copy-start(f32[1024,768]{1,0:T(8,128)} %copy-done.24) | copy-start | bytes 9437188
  458.7 15.2 %slice-start = ((s8[4718592]{0:T(1024)(128)(4,1)}), s8[524288]{0:T(1024)(128)(4,1)S(1)}, s32[]{:S(2)}) async-start(s8[4718592]{0:T(1024)(128)(4,1)} %bitcast.121), calls=%async_computation.12 | async-start | bytes 1048576
  (34 other events, 113.4 us)
Sparse Core Ops, SparseCore 0:
  122.0 31.9 all-gather.4
  155.9 24.1 all-gather.6
  182.0 38.9 all-gather.8
  222.6 38.9 all-gather.10
  302.7 36.7 reduce-scatter.6
  343.3 48.0 reduce-scatter.4
  395.3 53.8 reduce-scatter.10
  452.7 53.8 reduce-scatter.8

commit v4 on v3

--- a/solution.py
+++ b/solution.py
@@ -204,14 +204,10 @@
     )
 
 
-def gelu_value(pre_act):
-    return 0.5 * pre_act * (1.0 + lax.erf(pre_act * ROOT_HALF))
-
-
-def gelu_slope(pre_act):
-    return 0.5 * (1.0 + lax.erf(pre_act * ROOT_HALF)) + pre_act * INV_ROOT_TAU * jnp.exp(
-        -0.5 * pre_act * pre_act
-    )
+def gelu_both(pre_act):
+    below = 0.5 * (1.0 + lax.erf(pre_act * ROOT_HALF))
+    density = INV_ROOT_TAU * jnp.exp(-0.5 * pre_act * pre_act)
+    return pre_act * below, below + pre_act * density
 
 
 def swapped(block):
@@ -234,8 +230,8 @@
     halves = whole.reshape((2, -1) + whole.shape[1:])
     own = pick(halves, parity)
     other = swapped(pick(halves, 1 - parity).astype(narrow)).astype(whole.dtype)
-    first = parity == 0
-    return jnp.stack([jnp.where(first, own, other), jnp.where(first, other, own)])
+    mine = jnp.arange(2)[:, None, None] == parity
+    return jnp.where(mine, own[None], other[None])
 
 
 def key_pattern(seg, pad, rand):
@@ -274,21 +270,22 @@
     )
     first_out = first_norm.astype(BF16)
     pre_act = jnp.dot(first_out, mat_up, preferred_element_type=F32) + up_bias
-    act_low = gelu_value(pre_act).astype(BF16)
+    act, slope = gelu_both(pre_act)
+    act_low, slope = act.astype(BF16), slope.astype(BF16)
     down_out = jnp.dot(act_low, mat_down, preferred_element_type=F32) + vectors[3]
     final_out, normed_two, inv_two = norm_forward(
         first_out.astype(F32) + down_out, vectors[6], vectors[7]
     )
     saved = (
-        hidden, qkv, lse, mixture, normed_one, inv_one, first_out, pre_act, act_low, normed_two, inv_two,
+        hidden, qkv, lse, mixture, normed_one, inv_one, first_out, slope, act_low, normed_two, inv_two,
     )
     return final_out.astype(BF16), saved
 
 
-def layer_backward(grad_y, weights, saved, pattern):
+def layer_backward(grad_y, weights, saved, pattern, settle, after):
     mat_qkv, mat_out, mat_up, mat_down, vectors, up_bias = weights
     (
-        hidden, qkv, lse, mixture, normed_one, inv_one, first_out, pre_act, act_low, normed_two, inv_two,
+        hidden, qkv, lse, mixture, normed_one, inv_one, first_out, slope, act_low, normed_two, inv_two,
     ) = saved
     bias, first, count = pattern
     width = hidden.shape[1]
@@ -297,21 +294,29 @@
     grad_two = norm_backward(grad_y, normed_two, inv_two, vectors[6])
     grad_down_low = grad_two.astype(BF16)
     grad_bias_down = jnp.sum(grad_down_low.astype(F32), axis=0)
-    grad_mat_down = jnp.einsum("tf,td->fd", act_low, grad_down_low, preferred_element_type=F32)
+    grad_mat_down, grad_down_low = settle(
+        jnp.einsum("tf,td->fd", act_low, grad_down_low, preferred_element_type=F32), grad_down_low
+    )
     grad_act = jnp.einsum("td,fd->tf", grad_down_low, mat_down, preferred_element_type=F32)
-    grad_pre = (grad_act * gelu_slope(pre_act)).astype(BF16)
+    grad_pre = (grad_act * slope.astype(F32)).astype(BF16)
     grad_bias_hidden = jnp.sum(grad_pre.astype(F32), axis=0)
-    grad_mat_up = jnp.einsum("td,tf->df", first_out, grad_pre, preferred_element_type=F32)
+    grad_mat_up, grad_pre = settle(
+        jnp.einsum("td,tf->df", first_out, grad_pre, preferred_element_type=F32), grad_pre
+    )
     grad_first = grad_two + jnp.einsum("tf,df->td", grad_pre, mat_up, preferred_element_type=F32)
     grad_gain_one = jnp.sum(grad_first * normed_one, axis=0)
     grad_shift_one = jnp.sum(grad_first, axis=0)
     grad_one = norm_backward(grad_first, normed_one, inv_one, vectors[4])
     grad_branch = grad_one.astype(BF16)
     grad_bias_out = jnp.sum(grad_branch.astype(F32), axis=0)
-    grad_mat_out = jnp.einsum("td,te->de", mixture, grad_branch, preferred_element_type=F32)
+    grad_mat_out, grad_branch = settle(
+        jnp.einsum("td,te->de", mixture, grad_branch, preferred_element_type=F32), grad_branch
+    )
     grad_mix = jnp.einsum("te,de->td", grad_branch, mat_out, preferred_element_type=F32)
-    grad_qkv = attend_back(first, count, qkv, grad_mix.astype(BF16), bias, lse)
-    grad_mat_qkv = jnp.einsum("td,te->de", hidden, grad_qkv, preferred_element_type=F32)
+    grad_qkv = after(attend_back(first, count, qkv, grad_mix.astype(BF16), bias, lse))
+    grad_mat_qkv, grad_qkv = settle(
+        jnp.einsum("td,te->de", hidden, grad_qkv, preferred_element_type=F32), grad_qkv
+    )
     grad_hidden = grad_one + jnp.einsum("te,de->td", grad_qkv, mat_qkv, preferred_element_type=F32)
     bias_qkv = jnp.sum(grad_qkv.astype(F32), axis=0)
     grad_rows = jnp.stack(
@@ -378,7 +383,7 @@
     plan = []
     for order, (time, stages) in enumerate(items):
         for index, stage in enumerate(stages):
-            plan.append((time + index, order, stage))
+            plan.append((time + index * GAP, order, stage))
     for _, _, stage in sorted(plan, key=lambda step: step[:2]):
         stage()
 
@@ -566,15 +571,27 @@
     return [first] + [lambda: None] * delay + [last]
 
 
+PIECE = 96
+GAP = 2
+
+
 def row_pieces(rs):
-    return [(0, rs // 2), (rs // 2, rs // 2)] if rs % 32 == 0 and rs > 32 else [(0, rs)]
-
-
-def gather_kernel(rows, cols, *refs):
-    (full, lined), (small, tokens, marks) = (refs[:4], refs[4:8]), refs[8:11]
-    (full_out, lined_out), (small_out, hidden, marks_out) = (refs[11:15], refs[15:19]), refs[19:22]
-    slots, wide, lined_slots = refs[22:26], refs[26:30], refs[30:34]
-    local_sems, line_sems, chip_sems, core_sems, exchange_sems = refs[34:]
+    return [(begin, min(PIECE, rs)) for begin in range(0, rs, PIECE)]
+
+
+def gather_kernel(rows, cols, full_count, lined_count, *refs):
+    refs = list(refs)
+
+    def take(number):
+        taken = refs[:number]
+        del refs[:number]
+        return taken
+
+    full, lined, (small, tokens, marks) = take(full_count), take(lined_count), take(3)
+    full_out, lined_out = take(full_count), take(lined_count)
+    small_out, hidden, marks_out = take(3)
+    slots, wide, lined_slots = take(full_count), take(full_count), take(lined_count)
+    local_sems, line_sems, chip_sems, core_sems, exchange_sems = refs
     place = Place(rows, cols)
     place.greet()
     items = [
@@ -582,7 +599,7 @@
         (0, gather_line_item(place, small, small_out, None, local_sems.at[0, 0], line_sems.at[0])),
     ]
     number = 0
-    for index in range(4):
+    for index in range(full_count):
         for piece in row_pieces(full[index].shape[0]):
             stages = gather_item(
                 place,
@@ -599,7 +616,7 @@
             items.append((number, stages))
             number += 1
     items.append((number, exchange_item(place, tokens, hidden, exchange_sems.at[0], 16)))
-    for index in range(4):
+    for index in range(lined_count):
         at = number + index
         stages = gather_line_item(
             place,
@@ -619,13 +636,13 @@
     like = lambda x, lead=(): jax.ShapeDtypeStruct(lead + x.shape, x.dtype)
     wide = [(x.shape[0], cols * x.shape[1]) for x in full]
     outs = [jax.ShapeDtypeStruct((rows // 2, 2) + shape, BF16) for shape in wide]
-    outs += [jax.ShapeDtypeStruct(shape, BF16) for shape in wide]
+    outs += [jax.ShapeDtypeStruct((x.shape[0], cols * x.shape[1]), BF16) for x in lined]
     outs += [like(small, (cols,)), like(tokens), like(marks)]
     return pl.pallas_call(
-        functools.partial(gather_kernel, rows, cols),
+        functools.partial(gather_kernel, rows, cols, len(full), len(lined)),
         out_shape=tuple(outs),
-        in_specs=[ANY_SPEC] * 11,
-        out_specs=(ANY_SPEC,) * 4 + (VMEM_SPEC,) * 4 + (ANY_SPEC,) * 3,
+        in_specs=[ANY_SPEC] * (len(full) + len(lined) + 3),
+        out_specs=(ANY_SPEC,) * len(full) + (VMEM_SPEC,) * len(lined) + (ANY_SPEC,) * 3,
         scratch_shapes=[pltpu.VMEM((cols,) + x.shape, BF16) for x in full]
         + [pltpu.VMEM(shape, BF16) for shape in wide]
         + [pltpu.VMEM((cols,) + x.shape, BF16) for x in lined]
@@ -837,7 +854,8 @@
         return taken
 
     full_in, line_in, (small_in, tokens) = take(full), take(lined), take(2)
-    full_out, line_out, (small_out, tokens_out) = take(full), take(lined), take(2)
+    mats_out, (small_out, tokens_out) = take(full), take(2)
+    full_out, line_out = [ref.at[0] for ref in mats_out], [ref.at[1] for ref in mats_out]
     place = Place(rows, cols)
     place.greet()
     items = []
@@ -885,7 +903,7 @@
     phases = rows.bit_length() - 2
     hops = cols - 1
     shard = lambda x: (x.shape[-2], x.shape[-1] // cols)
-    outs = [jax.ShapeDtypeStruct(shard(x), F32) for x in (*full, *lined)]
+    outs = [jax.ShapeDtypeStruct((2,) + shard(x), F32) for x in full]
     outs.append(jax.ShapeDtypeStruct(small.shape[1:], F32))
     outs.append(jax.ShapeDtypeStruct(tokens.shape, tokens.dtype))
     scratch = [
@@ -923,7 +941,7 @@
         functools.partial(reduce_kernel, rows, cols, len(full), len(lined)),
         out_shape=tuple(outs),
         in_specs=[ANY_SPEC] * len(full) + [VMEM_SPEC] * (len(lined) + 1) + [ANY_SPEC],
-        out_specs=(VMEM_SPEC,) * (len(full) + len(lined) + 1) + (ANY_SPEC,),
+        out_specs=(VMEM_SPEC,) * (len(full) + 1) + (ANY_SPEC,),
         scratch_shapes=scratch,
         compiler_params=pltpu.CompilerParams(
             collective_id=1, has_side_effects=True, vmem_limit_bytes=60 << 20
@@ -947,9 +965,14 @@
     small = jnp.concatenate([layer_vectors.reshape(-1, part), bias_up.reshape(-1, part)])
     small_rows = small.shape[0]
     small = jnp.pad(small, ((0, -small_rows % 16), (0, 0)))
-    mats = (w_qkv, w_out, w_up, w_down)
     got = gather_all(
-        rows, cols, [w[0] for w in mats], [w[1] for w in mats], small, tokens, marks
+        rows,
+        cols,
+        [w_qkv[0], w_out[0], w_up[0], w_down[0], w_out[1]],
+        [w_qkv[1], w_up[1], w_down[1]],
+        small,
+        tokens,
+        marks,
     )
     vectors = got[8][:, : layers * 8].transpose(1, 0, 2).reshape(layers, 8, -1).astype(F32)
     up_biases = got[8][:, layers * 8 : small_rows].reshape(cols, layers, -1).transpose(1, 0, 2)
@@ -961,8 +984,9 @@
     rand = marks[:, 2 * lines, : half // BLOCK * rand_blocks.shape[2]]
     pattern = key_pattern(seg, pad, rand.reshape(-1, rand_blocks.shape[2]))
 
-    first_mats = [g.reshape(-1, g.shape[3]) for g in got[:4]]
-    second_mats = [lax.all_gather(g, "row", axis=0, tiled=True) for g in got[4:8]]
+    whole = [g.reshape(-1, g.shape[3]) for g in got[:5]]
+    qkv, up, down = (lax.all_gather(g, "row", axis=0, tiled=True) for g in got[5:8])
+    first_mats, second_mats = whole[:4], (qkv, whole[4], up, down)
     weights = [
         (*layer_mats, vectors[layer], up_biases[layer])
         for layer, layer_mats in enumerate((first_mats, second_mats))
@@ -973,18 +997,33 @@
         kept.append(saved)
     output = from_sequence(hidden, parity, BF16)
     flow = to_sequence(d_out, parity).astype(F32)
+
+    def settle_none(mat, following):
+        return mat.astype(BF16), following
+
+    def settle_rows(mat, following):
+        mat, following = lax.optimization_barrier((mat.astype(BF16), following))
+        return lax.psum_scatter(mat, "row", scatter_dimension=0, tiled=True), following
+
     grads, vec_grads, up_grads = [None] * layers, [None] * layers, [None] * layers
-    for layer in reversed(range(layers)):
-        flow, grads[layer], vec_grads[layer], up_grads[layer] = layer_backward(
-            flow, weights[layer], kept[layer], pattern
-        )
-    full = [
-        mat.astype(BF16).reshape(rows // 2, 2, -1, mat.shape[1]) for mat in grads[0]
-    ]
-    lined = [
-        lax.psum_scatter(mat.astype(BF16), "row", scatter_dimension=0, tiled=True)
-        for mat in grads[1]
-    ]
+    flow, grads[1], vec_grads[1], up_grads[1] = layer_backward(
+        flow, weights[1], kept[1], pattern, settle_rows, lambda x: x
+    )
+    qkv, out, up, down = grads[1]
+    flow, down = lax.optimization_barrier((flow, down))
+    held = []
+
+    def after(x):
+        x, other = lax.optimization_barrier((x, up))
+        held.append(other)
+        return x
+
+    flow, grads[0], vec_grads[0], up_grads[0] = layer_backward(
+        flow, weights[0], kept[0], pattern, settle_none, after
+    )
+    grads[1] = (qkv, out, held[0], down)
+    full = [mat.reshape(rows // 2, 2, -1, mat.shape[1]) for mat in grads[0]]
+    lined = grads[1]
     small = jnp.concatenate(
         [
             jnp.stack(vec_grads).reshape(layers * 8, cols, part).transpose(1, 0, 2),
@@ -994,12 +1033,11 @@
     )
     halves = flow.reshape(2, half, -1)
     summed = reduce_all(rows, cols, full, lined, small, pick(halves, 1 - parity).astype(BF16))
-    own, other = pick(halves, parity), summed[9].astype(F32)
-    first = parity == 0
-    d_tokens = jnp.stack([jnp.where(first, own, other), jnp.where(first, other, own)])
-    mats = [jnp.stack([summed[i], summed[4 + i]]) for i in range(4)]
-    vec = summed[8][: layers * 8].reshape(layers, 8, part)
-    ups = summed[8][layers * 8 :].reshape(layers, -1)
+    mine = jnp.arange(2)[:, None, None] == parity
+    d_tokens = jnp.where(mine, pick(halves, parity)[None], summed[5].astype(F32)[None])
+    mats = summed[:4]
+    vec = summed[4][: layers * 8].reshape(layers, 8, part)
+    ups = summed[4][layers * 8 :].reshape(layers, -1)
     return output, d_tokens, *mats, vec, ups
 
 

time: 645 us -> 577 us (0.89)
  waiting for transfers between devices: 46.9 us -> 9.71 us
  Pallas kernels: 320 us -> 295 us
  local copies, waits for them, and re-layouts: 33.8 us -> 41.1 us
  matrix products: 180 us -> 173 us
    all_gather x4 -> x3, waiting for transfers between devices: 19.7 us -> 0.99 us  [shards(): lax.all_gather(g, 'row', axis=0, tiled=True)]
    reduce_scatter x4, waiting for transfers between devices: 25.8 us -> 7.92 us  [settle_rows(): lax.psum_scatter(mat, 'row', scatter_dimension=0, tiled=True)]
    pallas_call x1, Pallas kernels: 110 us -> 95.6 us  [reduce_all(): pl.pallas_call(functools.partial(reduce_kernel, rows, cols, len(full), le...]
    pallas_call x1, Pallas kernels: 107 us -> 95.7 us  [gather_all(): pl.pallas_call(functools.partial(gather_kernel, rows, cols, len(full), le...]
    another operation x8 -> x0, other arithmetic: 9.42 us -> none  [the longest x4 4.28 us: shards(): mats = [jnp.stack([summed[i], summed[4 + i]]) for i in range(4)]]
    unnamed x116 -> x115, local copies, waits for them, and re-layouts: 20.5 us -> 21.3 us
  transfers between devices with their start and end apart: 10 -> 9, of which waited for: 2 -> 2; matrix products, arithmetic and copies ran while one was open for 28% -> 34% of each run, Pallas kernels for 16% -> 18%
where the time goes in v4:
time: 577 us; the launch traced here: 569 us
  Pallas kernels  295 us (51%)
  matrix products  173 us (30%)
  local copies, waits for them, and re-layouts  41.1 us (7%)
  other arithmetic  32.8 us (6%)
  between operations  15.5 us (3%)
  waiting for transfers between devices  9.71 us (2%)
    pallas_call x1, Pallas kernels, gather_all(): pl.pallas_call(functools.partial(gather_kernel, rows, cols, len(full), le...  95.7 us
    pallas_call x1, Pallas kernels, reduce_all(): pl.pallas_call(functools.partial(reduce_kernel, rows, cols, len(full), le...  95.6 us
    pallas_call x2, Pallas kernels, attend_back(): pl.pallas_call(attend_back_kernel, out_shape=jax.ShapeDtypeStruct((length...  57.7 us
    pallas_call x2, Pallas kernels, attend(): pl.pallas_call(attend_kernel, out_shape=(jax.ShapeDtypeStruct((length, mo...  45.8 us
    dot_general x2, matrix products, layer_backward(): jnp.einsum('td,fd->tf', grad_down_low, mat_down, preferred_element_type=F32)  26.1 us
    dot_general x2, matrix products, layer_forward(): pre_act = jnp.dot(first_out, mat_up, preferred_element_type=F32) + up_bias  24.5 us
    unnamed x115, local copies, waits for them, and re-layouts  21.3 us
    dot_general x2, matrix products, layer_backward(): jnp.einsum('te,de->td', grad_qkv, mat_qkv, preferred_element_type=F32)  19.1 us
  transfers between devices with their start and end apart: 9, of which 2 were waited for; matrix products, arithmetic and copies ran while one was open for 34% of the time, Pallas kernels for 18%

profile of v4, /device:TPU:0, one launch (start us, length us, event | category | flops | bytes accessed | tf_op | source)
XLA Modules:
  0.0 568.8 jit_solution(664006609083262539)
XLA Ops:
  15.1 95.7 %shard_map.170 = (bf16[4,2,96,2304]{3,2,1,0:T(8,128)(2,1)}, bf16[4,2,96,768]{3,2,1,0:T(8,128)(2,1)S(1)}, bf16[4,2,96,3072]{3,2,1,0:T(8,128)(2,1)}, bf16[4,2,384,...) custom-call(bf16[96,576]{1,0:T(8,128)(2,1)S(1)} %get-tuple-element.1, ...), custom_call_target="tpu_custom_call" | custom-call | tf_op jit(solution)/shard_map/pallas_call | solution.py:641
  115.8 6.2 %add_convert_fusion.1.qkv_ref = bf16[1024,2304]{1,0:T(8,128)(2,1)S(1)} fusion(bf16[1024,768]{1,0:T(8,128)(2,1)S(1)} %bitcast.137, bf16[768,2304]{1,0:T(8,128)(2,1)} %bitcast.135, f32[2304]{0:T(1024)S(1)} %get-tuple-element.158), kind=kOutput, calls=%fused_computation.23 | convolution fusion | flops 3628597248 | bytes 9839616 | tf_op jit(solution)/shard_map/dot_general | solution.py:265
  122.0 3.3 fusion.17.bias_ref
  125.4 22.9 %shard_map.171 = (bf16[1024,768]{1,0:T(8,128)(2,1)S(1)}, f32[6,8,256]{2,1,0:T(8,128)S(1)}) custom-call(s32[8]{0:T(128)S(1)} %get-tuple-element.134.first_ref, s32[8]{0:T(128)S(1)} %get-tuple-element.133.count_ref, bf16[1024,2304]{1,0:T(8,128)(2,1)S(1)} %add_convert_fusion.1.qkv_ref, f32[1024,1024]{1,0:T(8,128)S(1)} %fusion.17.bias_ref), custom_call_target="tpu_custom_call" | custom-call | tf_op jit(solution)/shard_map/pallas_call | solution.py:155
  152.2 12.1 %multiply_convert_fusion.3 = (bf16[1024,3072]{1,0:T(8,128)(2,1)S(1)}, f32[1024,3072]{1,0:T(8,128)}) fusion(f32[3072]{0:T(1024)S(1)} %bitcast.122, bf16[768,3072]{1,0:T(8,128)(2,1)} %bitcast.129, f32[1024,768]{1,0:T(8,128)} %copy-done.16, f32[768]{0:T(1024)S(1)} %get-tuple-element.117, f32[768]{0:T(1024)S(1)} %get-tuple-element.118, ...), kind=kOutput, calls=%fused_computation.18 | convolution fusion | flops 4854644736 | bytes 26765312 | tf_op jit(solution)/shard_map/dot_general | solution.py:272
  167.1 7.8 %fusion.44 = (f32[1024]{0:T(1024)S(1)}, f32[1024,768]{1,0:T(8,128)S(1)}) fusion(f32[768]{0:T(1024)S(1)} %get-tuple-element.116, bf16[1024,3072]{1,0:T(8,128)(2,1)S(1)} %get-tuple-element.161, bf16[3072,768]{1,0:T(8,128)(2,1)} %bitcast.133, f32[768]{0:T(1024)S(1)} %get-tuple-element.117, f32[768]{0:T(1024)S(1)} %get-tuple-element.118, ...), kind=kOutput, calls=%fused_computation.185 | convolution fusion | flops 4838915072 | bytes 17323008 | tf_op jit(solution)/shard_map/dot_general | solution.py:275
  179.8 6.6 %add_convert_fusion.qkv_ref = bf16[1024,2304]{1,0:T(8,128)(2,1)S(1)} fusion(bf16[768,2304]{1,0:T(8,128)(2,1)} %all-gather.4.cloned.1.call-done, f32[2304]{0:T(1024)S(1)} %get-tuple-element.157, f32[1024,768]{1,0:T(8,128)S(1)} %get-tuple-element.164, f32[768]{0:T(1024)S(1)} %get-tuple-element.114, f32[768]{0:T(1024)S(1)} %get-tuple-element.115, ...), kind=kOutput, calls=%fused_computation.22 | convolution fusion | flops 3632529408 | bytes 11426816 | tf_op jit(solution)/shard_map/dot_general | solution.py:265
  186.5 22.9 %shard_map.172 = (bf16[1024,768]{1,0:T(8,128)(2,1)S(1)}, f32[6,8,256]{2,1,0:T(8,128)S(1)}) custom-call(s32[8]{0:T(128)S(1)} %get-tuple-element.134.first_ref, s32[8]{0:T(128)S(1)} %get-tuple-element.133.count_ref, bf16[1024,2304]{1,0:T(8,128)(2,1)S(1)} %add_convert_fusion.qkv_ref, f32[1024,1024]{1,0:T(8,128)S(1)} %copy-done.1), custom_call_target="tpu_custom_call" | custom-call | tf_op jit(solution)/shard_map/pallas_call | solution.py:155
  213.4 12.4 %multiply_convert_fusion.2 = (bf16[1024,3072]{1,0:T(8,128)(2,1)}, f32[1024,3072]{1,0:T(8,128)}) fusion(f32[3072]{0:T(1024)S(1)} %bitcast.124, bf16[768,3072]{1,0:T(8,128)(2,1)} %all-gather.6.cloned.1.call-done, f32[1024,768]{1,0:T(8,128)} %copy-done.20, f32[768]{0:T(1024)S(1)} %get-tuple-element.109, f32[768]{0:T(1024)S(1)} %get-tuple-element.110, ...), kind=kOutput, calls=%fused_computation.16 | convolution fusion | flops 4854644736 | bytes 26765312 | tf_op jit(solution)/shard_map/dot_general | solution.py:272
  226.8 9.3 %fusion.46 = (f32[1024]{0:T(1024)S(1)}, f32[1024,768]{1,0:T(8,128)S(1)}) fusion(f32[768]{0:T(1024)S(1)} %get-tuple-element.108, bf16[1024,3072]{1,0:T(8,128)(2,1)} %get-tuple-element.167, bf16[3072,768]{1,0:T(8,128)(2,1)} %all-gather.8.cloned.1.call-done, f32[768]{0:T(1024)S(1)} %get-tuple-element.109, f32[768]{0:T(1024)S(1)} %get-tuple-element.110, ...), kind=kOutput, calls=%fused_computation.187 | convolution fusion | flops 4838915072 | bytes 17323008 | tf_op jit(solution)/shard_map/dot_general | solution.py:275
  241.3 2.8 convert_reduce_fusion.7
  245.3 6.9 %convolution_convert_fusion.3 = bf16[3072,768]{1,0:T(8,128)(2,1)} fusion(bf16[1024,3072]{1,0:T(8,128)(2,1)S(1)} %bitcast.147, bf16[1024,768]{1,0:T(8,128)(2,1)S(1)} %get-tuple-element.54), kind=kOutput, calls=%fused_computation.27 | convolution fusion | flops 4834197504 | bytes 12582912 | tf_op jit(solution)/shard_map/tf,td->fd/dot_general | solution.py:298
  252.3 12.9 %convert_reduce_fusion = (f32[3072]{0:T(1024)S(1)}, bf16[1024,3072]{1,0:T(8,128)(2,1)S(1)}) fusion(f32[1024,3072]{1,0:T(8,128)} %get-tuple-element.168, f32[3072]{0:T(1024)S(1)} %bitcast.125, bf16[1024,768]{1,0:T(8,128)(2,1)} %copy-done.32, bf16[3072,768]{1,0:T(8,128)(2,1)} %all-gather.8.cloned.1.call-done), kind=kOutput, calls=%fused_computation.12 | convolution fusion | flops 4879021056 | bytes 25190400 | tf_op jit(solution)/shard_map/td,fd->tf/dot_general | solution.py:300
  267.8 7.9 %convolution_convert_fusion.2 = bf16[768,3072]{1,0:T(8,128)(2,1)} fusion(bf16[1024,3072]{1,0:T(8,128)(2,1)S(1)} %get-tuple-element.55, f32[1024,768]{1,0:T(8,128)S(1)} %copy-done.21, f32[768]{0:T(1024)S(1)} %get-tuple-element.109, f32[768]{0:T(1024)S(1)} %get-tuple-element.110, f32[1024]{0:T(1024)S(1)} %add_rsqrt_fusion.1, ...), kind=kOutput, calls=%fused_computation.26 | convolution fusion | flops 4838129664 | bytes 14170112 | tf_op jit(solution)/shard_map/td,tf->df/dot_general | solution.py:304
  275.9 2.8 dynamic-slice_bitcast_fusion.3
  280.2 11.4 %multiply_reduce_fusion = (f32[768]{0:T(1024)S(1)}, f32[1024]{0:T(1024)S(1)}, f32[1024]{0:T(1024)S(1)}, f32[768]{0:T(1024)S(1)}, f32[1024,768]{1,0:T(8,128)S(1)}) fusion(f32[1024,768]{1,0:T(8,128)} %copy-done.20, f32[1024]{0:T(1024)S(1)} %add_rsqrt_fusion.1, f32[1024]{0:T(1024)S(1)} %broadcast_multiply_fusion.9, f32[768]{0:T(1024)S(1)} %get-tuple-element.110, ...), kind=kOutput, calls=%fused_computation.49 | convolution fusion | flops 4848349184 | bytes 22065152 | tf_op jit(solution)/shard_map/tf,df->td/dot_general | solution.py:306
  296.6 2.9 convolution_convert_fusion.7.grad_ref
  299.4 28.9 %shard_map.173 = bf16[1024,2304]{1,0:T(8,128)(2,1)} custom-call(s32[8]{0:T(128)S(1)} %get-tuple-element.134.first_ref, s32[8]{0:T(128)S(1)} %get-tuple-element.133.count_ref, bf16[1024,2304]{1,0:T(8,128)(2,1)} %copy-done.5, bf16[1024,768]{1,0:T(8,128)(2,1)S(1)} %convolution_convert_fusion.7.grad_ref, f32[1024,1024]{1,0:T(8,128)S(1)} %copy-done.2, ...), custom_call_target="tpu_custom_call" | custom-call | tf_op jit(solution)/shard_map/pallas_call | solution.py:171
  328.4 8.0 %convolution_convert_fusion.5 = bf16[768,2304]{1,0:T(8,128)(2,1)} fusion(bf16[1024,2304]{1,0:T(8,128)(2,1)} %shard_map.173, f32[1024,768]{1,0:T(8,128)S(1)} %copy-done.14, f32[768]{0:T(1024)S(1)} %get-tuple-element.114, f32[768]{0:T(1024)S(1)} %get-tuple-element.115, f32[1024]{0:T(1024)S(1)} %add_rsqrt_fusion.2, f32[1024]{0:T(1024)S(1)} %broadcast_multiply_fusion.10), kind=kOutput, calls=%fused_computation.29 | convolution fusion | flops 3629580288 | bytes 11417600 | tf_op jit(solution)/shard_map/td,te->de/dot_general | solution.py:318
  336.3 3.0 convert_reduce_fusion.2
  339.5 10.0 %convolution_add_fusion.3 = f32[1024,768]{1,0:T(8,128)} fusion(f32[1024,768]{1,0:T(8,128)} %get-tuple-element.132, bf16[1024,2304]{1,0:T(8,128)(2,1)} %shard_map.173, bf16[768,2304]{1,0:T(8,128)(2,1)} %all-gather.4.cloned.1.call-done), kind=kOutput, calls=%fused_computation.84 | convolution fusion | flops 3624665088 | bytes 14548992 | tf_op jit(solution)/shard_map/te,de->td/dot_general | solution.py:320
  352.0 3.2 multiply_reduce_fusion.1
  356.4 13.2 %convert_reduce_fusion.1 = (f32[3072]{0:T(1024)S(1)}, bf16[1024,3072]{1,0:T(8,128)(2,1)S(1)}) fusion(f32[1024,3072]{1,0:T(8,128)} %get-tuple-element.162, f32[3072]{0:T(1024)S(1)} %bitcast.123, bf16[3072,768]{1,0:T(8,128)(2,1)} %bitcast.134, f32[1024,768]{1,0:T(8,128)S(1)} %get-tuple-element.125), kind=kOutput, calls=%fused_computation.13 | convolution fusion | flops 4879807488 | bytes 26763264 | tf_op jit(solution)/shard_map/td,fd->tf/dot_general | solution.py:300
  369.6 6.0 %multiply_reduce_fusion.2 = (f32[768]{0:T(1024)S(1)}, f32[1024]{0:T(1024)S(1)}, f32[1024]{0:T(1024)S(1)}, f32[768]{0:T(1024)S(1)}, f32[1024,768]{1,0:T(8,128)S(1)}) fusion(f32[1024,768]{1,0:T(8,128)S(1)} %copy-done.18, f32[1024]{0:T(1024)S(1)} %add_rsqrt_fusion.3, f32[1024]{0:T(1024)S(1)} %broadcast_multiply_fusion.11, f32[768]{0:T(1024)S(1)} %get-tuple-element.118, ...), kind=kOutput, calls=%fused_computation.53 | convolution fusion | flops 4839698432 | bytes 20472832 | tf_op jit(solution)/shard_map/tf,df->td/dot_general | solution.py:306
  380.2 28.8 %shard_map.174 = bf16[1024,2304]{1,0:T(8,128)(2,1)} custom-call(s32[8]{0:T(128)S(1)} %get-tuple-element.134.first_ref, s32[8]{0:T(128)S(1)} %get-tuple-element.133.count_ref, bf16[1024,2304]{1,0:T(8,128)(2,1)} %copy-done.4, bf16[1024,768]{1,0:T(8,128)(2,1)S(1)} %convolution_convert_fusion.6.grad_ref, f32[1024,1024]{1,0:T(8,128)S(1)} %copy-done.3, ...), custom_call_target="tpu_custom_call" | custom-call | tf_op jit(solution)/shard_map/pallas_call | solution.py:171
  409.1 9.1 %convolution_add_fusion.2 = f32[1024,768]{1,0:T(8,128)} fusion(f32[1024,768]{1,0:T(8,128)S(1)} %get-tuple-element.127, bf16[1024,2304]{1,0:T(8,128)(2,1)} %shard_map.174, bf16[768,2304]{1,0:T(8,128)(2,1)} %bitcast.136), kind=kOutput, calls=%fused_computation.83 | convolution fusion | flops 3624665088 | bytes 14548992 | tf_op jit(solution)/shard_map/te,de->td/dot_general | solution.py:320
  420.0 3.1 fusion.22.refs_9_
  427.3 5.3 convolution_convert_fusion.4
  432.7 7.8 %convolution_convert_fusion.1 = bf16[768,3072]{1,0:T(8,128)(2,1)} fusion(bf16[1024,3072]{1,0:T(8,128)(2,1)S(1)} %bitcast.143, f32[1024,768]{1,0:T(8,128)S(1)} %copy-done.19, f32[768]{0:T(1024)S(1)} %copy-done.37, f32[768]{0:T(1024)S(1)} %get-tuple-element.118, f32[1024]{0:T(1024)S(1)} %add_rsqrt_fusion.3, f32[1024]{0:T(1024)S(1)} %broadcast_multiply_fusion.11), kind=kOutput, calls=%fused_computation.25 | convolution fusion | flops 4838129664 | bytes 14170112 | tf_op jit(solution)/shard_map/td,tf->df/dot_general | solution.py:304
  440.6 7.3 %convolution_convert_fusion = bf16[3072,768]{1,0:T(8,128)(2,1)} fusion(bf16[1024,3072]{1,0:T(8,128)(2,1)S(1)} %bitcast.145, f32[1024,768]{1,0:T(8,128)S(1)} %copy-done.27), kind=kOutput, calls=%fused_computation.24 | convolution fusion | flops 4834983936 | bytes 14155776 | tf_op jit(solution)/shard_map/tf,td->fd/dot_general | solution.py:298
  447.8 7.9 %reduce-scatter.9.cloned.1.call-done.refs_4_ = bf16[96,2304]{1,0:T(8,128)(2,1)} async-done(((bf16[768,2304]{1,0:T(8,128)(2,1)}), bf16[96,2304]{1,0:T(8,128)(2,1)}) %reduce-scatter.9.cloned.1.call-update) | async-done | bytes 442384 | tf_op jit(solution)/shard_map/reduce_scatter | solution.py:1006
  455.7 95.6 %shard_map.175 = (f32[2,96,576]{2,1,0:T(8,128)}, f32[2,96,192]{2,1,0:T(8,128)}, f32[2,96,768]{2,1,0:T(8,128)}, f32[2,384,192]{2,1,0:T(8,128)}, f32[24,192]{1,0:T(8,128)}, /*index=5*/bf16[512,768]{1,0:T(8,128)(2,1)}) custom-call(bf16[4,2,96,2304]{3,2,1,0:T(8,128)(2,1)} %bitcast.109, bf16[4,2,96,768]{3,2,1,0:T(8,128)(2,1)} %bitcast.112, ...), custom_call_target="tpu_custom_call" | custom-call | tf_op jit(solution)/shard_map/pallas_call | solution.py:940
  (245 shorter events, 69.1 us)
Async XLA Ops:
  7.2 172.6 %all-gather.4.cloned.1.call-start = ((), (), s32[]{:S(2)}) async-start(), calls=%async_computation.4 | async-start | bytes 3981312 | tf_op jit(solution)/shard_map/all_gather | solution.py:988
  110.8 37.5 %copy-start.8 = (bf16[4,2,96,768]{3,2,1,0:T(8,128)(2,1)}, bf16[4,2,96,768]{3,2,1,0:T(8,128)(2,1)S(1)}, u32[]{:S(2)}) copy-start(bf16[4,2,96,768]{3,2,1,0:T(8,128)(2,1)S(1)} %get-tuple-element.46) | copy-start | bytes 3538948
  110.9 102.5 %all-gather.6.cloned.1.call-start = ((), (), s32[]{:S(2)}) async-start(), calls=%async_computation.5 | async-start | bytes 5308416 | tf_op jit(solution)/shard_map/all_gather | solution.py:988
  111.6 115.2 %all-gather.8.cloned.1.call-start = ((), (), s32[]{:S(2)}) async-start(), calls=%async_computation.6 | async-start | bytes 5308416 | tf_op jit(solution)/shard_map/all_gather | solution.py:988
  113.8 61.6 %collective-permute-start.1 = (bf16[512,768]{1,0:T(8,128)(2,1)}, bf16[512,768]{1,0:T(8,128)(2,1)}, u32[]{:S(2)}, u32[]{:S(2)}) collective-permute-start(bf16[512,768]{1,0:T(8,128)(2,1)} %dynamic-slice_bitcast_fusion.1), channel_id=1, source_target_pairs={{0,1},{1,0},{2,3},{3,2},{4,5},{5,4},{6,7},{7,6},{8,9},{9,8},{10,11... | collective-permute-start | bytes 2359304 | tf_op jit(solution)/shard_map/ppermute | solution.py:215
  113.8 238.1 %reduce-scatter.5.cloned.1.call-start = ((), (), s32[]{:S(2)}) async-start(), calls=%async_computation.7 | async-start | bytes 5308416 | tf_op jit(solution)/shard_map/reduce_scatter | solution.py:1006
  115.8 48.6 %copy-start.36 = (f32[768]{0:T(1024)}, f32[768]{0:T(1024)S(1)}, u32[]{:S(2)}) copy-start(f32[768]{0:T(1024)S(1)} %get-tuple-element.117) | copy-start | bytes 9220
  122.0 26.3 %copy-start.4 = (bf16[1024,2304]{1,0:T(8,128)(2,1)}, bf16[1024,2304]{1,0:T(8,128)(2,1)S(1)}, u32[]{:S(2)}) copy-start(bf16[1024,2304]{1,0:T(8,128)(2,1)S(1)} %add_convert_fusion.1.qkv_ref) | copy-start | bytes 14155780
  125.3 23.0 %copy-start = (f32[1024,1024]{1,0:T(8,128)}, f32[1024,1024]{1,0:T(8,128)S(1)}, u32[]{:S(2)}) copy-start(f32[1024,1024]{1,0:T(8,128)S(1)} %fusion.17.bias_ref) | copy-start | bytes 12582916
  152.2 14.8 %copy-start.17 = (f32[1024,768]{1,0:T(8,128)S(1)}, f32[1024,768]{1,0:T(8,128)}, u32[]{:S(2)}) copy-start(f32[1024,768]{1,0:T(8,128)} %copy-done.16) | copy-start | bytes 9437188
  179.8 6.7 %copy-start.1 = (f32[1024,1024]{1,0:T(8,128)S(1)}, f32[1024,1024]{1,0:T(8,128)}, u32[]{:S(2)}) copy-start(f32[1024,1024]{1,0:T(8,128)} %copy-done) | copy-start | bytes 12582916
  186.5 22.9 %copy-start.5 = (bf16[1024,2304]{1,0:T(8,128)(2,1)}, bf16[1024,2304]{1,0:T(8,128)(2,1)S(1)}, u32[]{:S(2)}) copy-start(bf16[1024,2304]{1,0:T(8,128)(2,1)S(1)} %add_convert_fusion.qkv_ref) | copy-start | bytes 14155780
  186.5 22.9 %copy-start.13 = (f32[1024,768]{1,0:T(8,128)S(1)}, f32[1024,768]{1,0:T(8,128)}, u32[]{:S(2)}) copy-start(f32[1024,768]{1,0:T(8,128)} %copy-done.12) | copy-start | bytes 9437188
  186.5 22.9 %copy-start.40 = (bf16[4,2,96,768]{3,2,1,0:T(8,128)(2,1)S(1)}, bf16[4,2,96,768]{3,2,1,0:T(8,128)(2,1)}, u32[]{:S(2)}) copy-start(bf16[4,2,96,768]{3,2,1,0:T(8,128)(2,1)} %get-tuple-element.51) | copy-start | bytes 3538948
  252.2 156.9 %reduce-scatter.7.cloned.1.call-start = ((), (), s32[]{:S(2)}) async-start(), calls=%async_computation.8 | async-start | bytes 5308416 | tf_op jit(solution)/shard_map/reduce_scatter | solution.py:1006
  252.2 15.5 %copy-start.21 = (f32[1024,768]{1,0:T(8,128)S(1)}, f32[1024,768]{1,0:T(8,128)}, u32[]{:S(2)}) copy-start(f32[1024,768]{1,0:T(8,128)} %copy-done.20) | copy-start | bytes 9437188
  275.8 172.1 %reduce-scatter.11.cloned.1.call-start = ((), (), s32[]{:S(2)}) async-start(), calls=%async_computation.10 | async-start | bytes 1327104 | tf_op jit(solution)/shard_map/reduce_scatter | solution.py:1006
  278.7 12.9 %copy-start.22 = (f32[1024,768]{1,0:T(8,128)S(1)}, f32[1024,768]{1,0:T(8,128)}, u32[]{:S(2)}) copy-start(f32[1024,768]{1,0:T(8,128)} %copy-done.20) | copy-start | bytes 9437188
  278.7 70.7 %collective-permute-start = (bf16[512,768]{1,0:T(8,128)(2,1)}, bf16[512,768]{1,0:T(8,128)(2,1)}, u32[]{:S(2)}, u32[]{:S(2)}) collective-permute-start(bf16[512,768]{1,0:T(8,128)(2,1)} %get-tuple-element.139), channel_id=1, source_target_pairs={{0,1},{1,0},{2,3},{3,2},{4,5},{5,4},{6,7},{7,6},{8,9},{9,8},{10,11... | collective-permute-start | bytes 2359304 | tf_op jit(solution)/shard_map/ppermute | solution.py:215
  296.5 159.2 %reduce-scatter.9.cloned.1.call-start = ((), (), s32[]{:S(2)}) async-start(), calls=%async_computation.9 | async-start | bytes 3981312 | tf_op jit(solution)/shard_map/reduce_scatter | solution.py:1006
  299.4 28.9 %copy-start.14 = (f32[1024,768]{1,0:T(8,128)S(1)}, f32[1024,768]{1,0:T(8,128)}, u32[]{:S(2)}) copy-start(f32[1024,768]{1,0:T(8,128)} %copy-done.12) | copy-start | bytes 9437188
  339.5 10.0 %copy-start.30 = (bf16[512,768]{1,0:T(8,128)(2,1)S(1)}, bf16[512,768]{1,0:T(8,128)(2,1)}, u32[]{:S(2)}) copy-start(bf16[512,768]{1,0:T(8,128)(2,1)} %get-tuple-element.138) | copy-start | bytes 2359300
  355.2 14.3 %slice-start.2 = ((s8[4718592]{0:T(1024)(128)(4,1)}), s8[4194304]{0:T(1024)(128)(4,1)S(1)}, s32[]{:S(2)}) async-start(s8[4718592]{0:T(1024)(128)(4,1)} %bitcast.130), calls=%async_computation.13 | async-start | bytes 8388608
  356.4 13.2 %copy-start.26 = (f32[1024,768]{1,0:T(8,128)}, f32[1024,768]{1,0:T(8,128)S(1)}, u32[]{:S(2)}) copy-start(f32[1024,768]{1,0:T(8,128)S(1)} %get-tuple-element.125) | copy-start | bytes 9437188
  356.4 13.2 %copy-start.18 = (f32[1024,768]{1,0:T(8,128)S(1)}, f32[1024,768]{1,0:T(8,128)}, u32[]{:S(2)}) copy-start(f32[1024,768]{1,0:T(8,128)} %copy-done.16) | copy-start | bytes 9437188
  356.4 13.2 %slice-start.3 = ((s8[4718592]{0:T(1024)(128)(4,1)}), s8[524288]{0:T(1024)(128)(4,1)S(1)}, s32[]{:S(2)}) async-start(s8[4718592]{0:T(1024)(128)(4,1)} %bitcast.130), calls=%async_computation.14 | async-start | bytes 1048576
  376.8 32.3 %copy-start.28 = (f32[1024,768]{1,0:T(8,128)}, f32[1024,768]{1,0:T(8,128)S(1)}, u32[]{:S(2)}) copy-start(f32[1024,768]{1,0:T(8,128)S(1)} %get-tuple-element.127) | copy-start | bytes 9437188
  409.1 9.1 %copy-start.15 = (bf16[1024,2304]{1,0:T(8,128)(2,1)S(1)}, bf16[1024,2304]{1,0:T(8,128)(2,1)}, u32[]{:S(2)}) copy-start(bf16[1024,2304]{1,0:T(8,128)(2,1)} %shard_map.174) | copy-start | bytes 14155780
  424.8 7.9 %slice-start.4 = ((s8[6291456]{0:T(1024)(128)(4,1)}), s8[4194304]{0:T(1024)(128)(4,1)S(1)}, s32[]{:S(2)}) async-start(s8[6291456]{0:T(1024)(128)(4,1)} %bitcast.142), calls=%async_computation.15 | async-start | bytes 8388608
  427.3 13.2 %slice-start.6 = ((s8[6291456]{0:T(1024)(128)(4,1)}), s8[4194304]{0:T(1024)(128)(4,1)S(1)}, s32[]{:S(2)}) async-start(s8[6291456]{0:T(1024)(128)(4,1)} %bitcast.144), calls=%async_computation.17 | async-start | bytes 8388608
  432.7 7.9 %copy-start.27 = (f32[1024,768]{1,0:T(8,128)S(1)}, f32[1024,768]{1,0:T(8,128)}, u32[]{:S(2)}) copy-start(f32[1024,768]{1,0:T(8,128)} %copy-done.26) | copy-start | bytes 9437188
  432.7 7.9 %slice-start.7 = ((s8[6291456]{0:T(1024)(128)(4,1)}), s8[2097152]{0:T(1024)(128)(4,1)S(1)}, s32[]{:S(2)}) async-start(s8[6291456]{0:T(1024)(128)(4,1)} %bitcast.144), calls=%async_computation.18 | async-start | bytes 4194304
  (31 other events, 109.7 us)
Sparse Core Ops, SparseCore 0:
  111.0 34.0 all-gather.3
  147.0 38.9 all-gather.5
  187.8 38.9 all-gather.7
  252.3 53.8 reduce-scatter.4
  309.9 53.8 reduce-scatter.6
  367.0 36.7 reduce-scatter.10
  407.6 48.0 reduce-scatter.8

commit v5 on v4

--- a/solution.py
+++ b/solution.py
@@ -294,29 +294,21 @@
     grad_two = norm_backward(grad_y, normed_two, inv_two, vectors[6])
     grad_down_low = grad_two.astype(BF16)
     grad_bias_down = jnp.sum(grad_down_low.astype(F32), axis=0)
-    grad_mat_down, grad_down_low = settle(
-        jnp.einsum("tf,td->fd", act_low, grad_down_low, preferred_element_type=F32), grad_down_low
-    )
+    grad_mat_down, grad_down_low = settle("down", act_low, grad_down_low)
     grad_act = jnp.einsum("td,fd->tf", grad_down_low, mat_down, preferred_element_type=F32)
     grad_pre = (grad_act * slope.astype(F32)).astype(BF16)
     grad_bias_hidden = jnp.sum(grad_pre.astype(F32), axis=0)
-    grad_mat_up, grad_pre = settle(
-        jnp.einsum("td,tf->df", first_out, grad_pre, preferred_element_type=F32), grad_pre
-    )
+    grad_mat_up, grad_pre = settle("up", first_out, grad_pre)
     grad_first = grad_two + jnp.einsum("tf,df->td", grad_pre, mat_up, preferred_element_type=F32)
     grad_gain_one = jnp.sum(grad_first * normed_one, axis=0)
     grad_shift_one = jnp.sum(grad_first, axis=0)
     grad_one = norm_backward(grad_first, normed_one, inv_one, vectors[4])
     grad_branch = grad_one.astype(BF16)
     grad_bias_out = jnp.sum(grad_branch.astype(F32), axis=0)
-    grad_mat_out, grad_branch = settle(
-        jnp.einsum("td,te->de", mixture, grad_branch, preferred_element_type=F32), grad_branch
-    )
+    grad_mat_out, grad_branch = settle("out", mixture, grad_branch)
     grad_mix = jnp.einsum("te,de->td", grad_branch, mat_out, preferred_element_type=F32)
     grad_qkv = after(attend_back(first, count, qkv, grad_mix.astype(BF16), bias, lse))
-    grad_mat_qkv, grad_qkv = settle(
-        jnp.einsum("td,te->de", hidden, grad_qkv, preferred_element_type=F32), grad_qkv
-    )
+    grad_mat_qkv, grad_qkv = settle("qkv", hidden, grad_qkv)
     grad_hidden = grad_one + jnp.einsum("te,de->td", grad_qkv, mat_qkv, preferred_element_type=F32)
     bias_qkv = jnp.sum(grad_qkv.astype(F32), axis=0)
     grad_rows = jnp.stack(
@@ -579,7 +571,11 @@
     return [(begin, min(PIECE, rs)) for begin in range(0, rs, PIECE)]
 
 
-def gather_kernel(rows, cols, full_count, lined_count, *refs):
+FULL = ((0, 0), (1, 0), (2, 0), (3, 0), (1, 1))
+ALONG = ((0, 1), (2, 1), (3, 1))
+
+
+def gather_kernel(rows, cols, *refs):
     refs = list(refs)
 
     def take(number):
@@ -587,7 +583,10 @@
         del refs[:number]
         return taken
 
-    full, lined, (small, tokens, marks) = take(full_count), take(lined_count), take(3)
+    full_count, lined_count = len(FULL), len(ALONG)
+    mats, (small, tokens, marks) = take(4), take(3)
+    full = [mats[index].at[layer] for index, layer in FULL]
+    lined = [mats[index].at[layer] for index, layer in ALONG]
     full_out, lined_out = take(full_count), take(lined_count)
     small_out, hidden, marks_out = take(3)
     slots, wide, lined_slots = take(full_count), take(full_count), take(lined_count)
@@ -630,7 +629,9 @@
     run_stages(items)
 
 
-def gather_all(rows, cols, full, lined, small, tokens, marks):
+def gather_all(rows, cols, mats, small, tokens, marks):
+    full = [jax.ShapeDtypeStruct(mats[index].shape[1:], BF16) for index, _ in FULL]
+    lined = [jax.ShapeDtypeStruct(mats[index].shape[1:], BF16) for index, _ in ALONG]
     number = sum(len(row_pieces(x.shape[0])) for x in full)
     phases = rows.bit_length() - 2
     like = lambda x, lead=(): jax.ShapeDtypeStruct(lead + x.shape, x.dtype)
@@ -639,9 +640,9 @@
     outs += [jax.ShapeDtypeStruct((x.shape[0], cols * x.shape[1]), BF16) for x in lined]
     outs += [like(small, (cols,)), like(tokens), like(marks)]
     return pl.pallas_call(
-        functools.partial(gather_kernel, rows, cols, len(full), len(lined)),
+        functools.partial(gather_kernel, rows, cols),
         out_shape=tuple(outs),
-        in_specs=[ANY_SPEC] * (len(full) + len(lined) + 3),
+        in_specs=[ANY_SPEC] * 7,
         out_specs=(ANY_SPEC,) * len(full) + (VMEM_SPEC,) * len(lined) + (ANY_SPEC,) * 3,
         scratch_shapes=[pltpu.VMEM((cols,) + x.shape, BF16) for x in full]
         + [pltpu.VMEM(shape, BF16) for shape in wide]
@@ -656,7 +657,7 @@
         compiler_params=pltpu.CompilerParams(
             collective_id=0, has_side_effects=True, vmem_limit_bytes=50 << 20
         ),
-    )(*full, *lined, small, tokens, marks)
+    )(*mats, small, tokens, marks)
 
 
 class LineReduce:
@@ -735,12 +736,31 @@
     )
 
 
-def reduce_item(place, partial, out, sums, from_core, from_chips, slots, from_line, piece, sems):
+def chunk_columns(x, y):
+    width = y.shape[1] // max(1, x.shape[1] * y.shape[1] // (768 * 768))
+    width = -(-width // 128) * 128
+    return [slice(at, at + width) for at in range(0, y.shape[1], width)]
+
+
+def product_step(place, x, y, sums, away, chunk):
+    cols = chunk_columns(x, y)[chunk]
+    result = lax.dot_general(
+        x[...], y[:, cols], (((0,), (0,)), ((), ())), preferred_element_type=F32
+    ).astype(BF16)
+    size = sums.shape[1]
+    for pair in range(place.rows // 2):
+        even = result[2 * pair * size : (2 * pair + 1) * size]
+        odd = result[(2 * pair + 1) * size : (2 * pair + 2) * size]
+        sums[pair, :, cols] = jnp.where(place.core == 0, even, odd)
+        away[pair, :, cols] = jnp.where(place.core == 0, odd, even)
+
+
+def reduce_item(place, partial, away, out, sums, from_core, from_chips, slots, from_line, piece, sems):
     local_sem, core_sems, chip_sems, line_sems = sems
     phases = len(place.bits)
     rows = pl.ds(*piece)
     core_copy = lambda: remote(
-        partial.at[:, 1 - place.core, rows],
+        away.at[:, rows] if partial is None else partial.at[:, 1 - place.core, rows],
         from_core.at[:, rows],
         core_sems.at[0],
         core_sems.at[1],
@@ -780,11 +800,13 @@
 
     def first():
         core_copy().start()
-        load().start()
+        if partial is not None:
+            load().start()
 
     def chip_stage(phase):
         if phase == 0:
-            load().wait()
+            if partial is not None:
+                load().wait()
             core_copy().wait_recv()
 
             def add(pair, carry):
@@ -844,7 +866,13 @@
     )
 
 
-def reduce_kernel(rows, cols, full, lined, *refs):
+READY = ((1, 1), (0, 0))
+PRODUCTS = ((2, 0), (1, 0), (3, 0))
+LINED = ((0, 1), (2, 1), (3, 1))
+SHARER, SHARED = 4, 1
+
+
+def reduce_kernel(rows, cols, *refs):
     phases = rows.bit_length() - 2
     refs = list(refs)
 
@@ -853,11 +881,12 @@
         del refs[:number]
         return taken
 
-    full_in, line_in, (small_in, tokens) = take(full), take(lined), take(2)
-    mats_out, (small_out, tokens_out) = take(full), take(2)
-    full_out, line_out = [ref.at[0] for ref in mats_out], [ref.at[1] for ref in mats_out]
+    ready, factors, line_in = take(len(READY)), take(2 * len(PRODUCTS)), take(len(LINED))
+    (small_in, tokens), mats_out, (small_out, tokens_out) = take(2), take(4), take(2)
+    shard_of = lambda name: mats_out[name[0]].at[name[1]]
+    held, [factor_sems] = take(2 * len(PRODUCTS) - 1), take(1)
+    held.insert(SHARER, held[SHARED])
     place = Place(rows, cols)
-    place.greet()
     items = []
     small_sums, small_arrived, small_line, small_sems, small_line_sems = take(5)
     [token_sems] = take(1)
@@ -865,16 +894,35 @@
     token_copy = lambda: remote(
         tokens, tokens_out, token_sems.at[0], token_sems.at[1], (place.row, place.col + 1 - 2 * parity)
     )
-    time = 0
-    for index in range(full):
+    starts, steps = {(0, 0): 0, (1, 1): 1, (2, 0): 2, (1, 0): 3, (3, 0): 4}, []
+    times = {(2, 0): (0, 0, 1, 1), (1, 0): (2,), (3, 0): (2, 2, 3, 3)}
+    loads = [
+        pltpu.make_async_copy(factors[i], held[i], factor_sems.at[i]) for i in range(len(factors))
+    ]
+    for index, load in enumerate(loads):
+        if index != SHARER:
+            load.start()
+    place.greet()
+    for index, name in enumerate(READY + PRODUCTS):
         sums, from_core, slots, from_line = take(4)
         from_chips = take(phases)
         local_sems, core_sems, chip_sems, line_sems = take(4)
-        for number, piece in enumerate(row_pieces(full_in[index].shape[2])):
+        partial, away = (ready[index], None) if name in READY else (None, *take(1))
+        if partial is None:
+            at = 2 * (index - len(READY))
+            x, y = held[at], held[at + 1]
+            steps.append((times[name][0], [lambda at=at: (loads[at].wait(), loads[at + 1].wait())]))
+            for chunk in range(len(chunk_columns(x, y))):
+                step = functools.partial(product_step, place, x, y, sums, away, chunk)
+                steps.append((times[name][chunk], [step]))
+            if at + 1 == SHARED:
+                steps.append((times[name][-1], [loads[SHARER].start]))
+        for number, piece in enumerate(row_pieces(sums.shape[1])):
             stages = reduce_item(
                 place,
-                full_in[index],
-                full_out[index],
+                partial,
+                away,
+                shard_of(name),
                 sums,
                 from_core,
                 from_chips,
@@ -883,12 +931,11 @@
                 piece,
                 (local_sems.at[number], core_sems.at[number], chip_sems.at[number], line_sems.at[number]),
             )
-            items.append((time, stages))
-            time += 1
-    for index in range(lined):
+            items.append((starts[name] + number, stages))
+    for index, name in enumerate(LINED):
         slots, from_line, line_sems = take(3)
         items.append(
-            (index, reduce_line_item(place, line_in[index], line_out[index], slots, from_line, line_sems))
+            (index, reduce_line_item(place, line_in[index], shard_of(name), slots, from_line, line_sems))
         )
     items.append(
         (1, reduce_small_item(place, small_in, small_out, small_sums, small_arrived, small_line, small_sems, small_line_sems))
@@ -896,17 +943,22 @@
     items.append(
         (0, [lambda: token_copy().start()] + [lambda: None] * 12 + [lambda: token_copy().wait()])
     )
-    run_stages(items)
-
-
-def reduce_all(rows, cols, full, lined, small, tokens):
+    run_stages(items + steps)
+
+
+def reduce_all(rows, cols, ready, products, lined, small, tokens):
     phases = rows.bit_length() - 2
     hops = cols - 1
-    shard = lambda x: (x.shape[-2], x.shape[-1] // cols)
-    outs = [jax.ShapeDtypeStruct((2,) + shard(x), F32) for x in full]
+    full = [x.shape[2:] for x in ready] + [(x.shape[1] // rows, y.shape[1]) for x, y in products]
+    shard = lambda shape: (shape[0], shape[1] // cols)
+    shapes = dict(zip(READY + PRODUCTS, full)) | {n: x.shape for n, x in zip(LINED, lined)}
+    outs = [jax.ShapeDtypeStruct((2,) + shard(shapes[index, 0]), F32) for index in range(4)]
     outs.append(jax.ShapeDtypeStruct(small.shape[1:], F32))
     outs.append(jax.ShapeDtypeStruct(tokens.shape, tokens.dtype))
-    scratch = [
+    factors = [factor for pair in products for factor in pair]
+    scratch = [pltpu.VMEM(x.shape, BF16) for i, x in enumerate(factors) if i != SHARER]
+    scratch.append(DMA((len(factors),)))
+    scratch += [
         pltpu.VMEM(small.shape, F32),
         pltpu.VMEM((phases + 1,) + small.shape, F32),
         pltpu.VMEM((2, hops) + small.shape[1:], F32),
@@ -914,16 +966,16 @@
         DMA((2, 2, hops)),
         DMA((2,)),
     ]
-    for x in full:
-        count = len(row_pieces(x.shape[2]))
+    for index, shape in enumerate(full):
+        count = len(row_pieces(shape[0]))
         scratch += [
-            pltpu.VMEM((rows // 2,) + x.shape[2:], BF16),
-            pltpu.VMEM((rows // 2,) + x.shape[2:], BF16),
-            pltpu.VMEM((cols,) + shard(x), BF16),
-            pltpu.VMEM((2, hops) + shard(x), BF16),
+            pltpu.VMEM((rows // 2,) + shape, BF16),
+            pltpu.VMEM((rows // 2,) + shape, BF16),
+            pltpu.VMEM((cols,) + shard(shape), BF16),
+            pltpu.VMEM((2, hops) + shard(shape), BF16),
         ]
         scratch += [
-            pltpu.VMEM((2 ** (phases - 1 - phase),) + x.shape[2:], BF16) for phase in range(phases)
+            pltpu.VMEM((2 ** (phases - 1 - phase),) + shape, BF16) for phase in range(phases)
         ]
         scratch += [
             DMA((count,)),
@@ -931,22 +983,26 @@
             DMA((count, 2, phases, 2, 2 ** (phases - 1))),
             DMA((count, 2, 2, hops)),
         ]
+        if index >= len(ready):
+            scratch.append(pltpu.VMEM((rows // 2,) + shape, BF16))
     for x in lined:
         scratch += [
-            pltpu.VMEM((cols,) + shard(x), BF16),
-            pltpu.VMEM((2, hops) + shard(x), BF16),
+            pltpu.VMEM((cols,) + shard(x.shape), BF16),
+            pltpu.VMEM((2, hops) + shard(x.shape), BF16),
             DMA((2, 2, hops)),
         ]
     return pl.pallas_call(
-        functools.partial(reduce_kernel, rows, cols, len(full), len(lined)),
+        functools.partial(reduce_kernel, rows, cols),
         out_shape=tuple(outs),
-        in_specs=[ANY_SPEC] * len(full) + [VMEM_SPEC] * (len(lined) + 1) + [ANY_SPEC],
-        out_specs=(VMEM_SPEC,) * (len(full) + 1) + (ANY_SPEC,),
+        in_specs=[ANY_SPEC] * (len(ready) + len(factors))
+        + [VMEM_SPEC] * (len(lined) + 1)
+        + [ANY_SPEC],
+        out_specs=(VMEM_SPEC,) * 5 + (ANY_SPEC,),
         scratch_shapes=scratch,
         compiler_params=pltpu.CompilerParams(
-            collective_id=1, has_side_effects=True, vmem_limit_bytes=60 << 20
+            collective_id=1, has_side_effects=True, vmem_limit_bytes=62 << 20
         ),
-    )(*full, *lined, small, tokens)
+    )(*ready, *factors, *lined, small, tokens)
 
 
 def shards(
@@ -965,15 +1021,7 @@
     small = jnp.concatenate([layer_vectors.reshape(-1, part), bias_up.reshape(-1, part)])
     small_rows = small.shape[0]
     small = jnp.pad(small, ((0, -small_rows % 16), (0, 0)))
-    got = gather_all(
-        rows,
-        cols,
-        [w_qkv[0], w_out[0], w_up[0], w_down[0], w_out[1]],
-        [w_qkv[1], w_up[1], w_down[1]],
-        small,
-        tokens,
-        marks,
-    )
+    got = gather_all(rows, cols, (w_qkv, w_out, w_up, w_down), small, tokens, marks)
     vectors = got[8][:, : layers * 8].transpose(1, 0, 2).reshape(layers, 8, -1).astype(F32)
     up_biases = got[8][:, layers * 8 : small_rows].reshape(cols, layers, -1).transpose(1, 0, 2)
     up_biases = up_biases.reshape(layers, -1).astype(F32)
@@ -998,16 +1046,21 @@
     output = from_sequence(hidden, parity, BF16)
     flow = to_sequence(d_out, parity).astype(F32)
 
-    def settle_none(mat, following):
-        return mat.astype(BF16), following
-
-    def settle_rows(mat, following):
-        mat, following = lax.optimization_barrier((mat.astype(BF16), following))
-        return lax.psum_scatter(mat, "row", scatter_dimension=0, tiled=True), following
+    def product(x, y):
+        return jnp.einsum("td,te->de", x, y, preferred_element_type=F32).astype(BF16)
+
+    def settle_first(kind, x, y):
+        return (product(x, y) if kind == "qkv" else (x, y)), y
+
+    def settle_second(kind, x, y):
+        mat, y = lax.optimization_barrier((product(x, y), y))
+        if kind != "out":
+            mat = lax.psum_scatter(mat, "row", scatter_dimension=0, tiled=True)
+        return mat, y
 
     grads, vec_grads, up_grads = [None] * layers, [None] * layers, [None] * layers
     flow, grads[1], vec_grads[1], up_grads[1] = layer_backward(
-        flow, weights[1], kept[1], pattern, settle_rows, lambda x: x
+        flow, weights[1], kept[1], pattern, settle_second, lambda x: x
     )
     qkv, out, up, down = grads[1]
     flow, down = lax.optimization_barrier((flow, down))
@@ -1019,11 +1072,11 @@
         return x
 
     flow, grads[0], vec_grads[0], up_grads[0] = layer_backward(
-        flow, weights[0], kept[0], pattern, settle_none, after
-    )
-    grads[1] = (qkv, out, held[0], down)
-    full = [mat.reshape(rows // 2, 2, -1, mat.shape[1]) for mat in grads[0]]
-    lined = grads[1]
+        flow, weights[0], kept[0], pattern, settle_first, after
+    )
+    split_rows = lambda mat: mat.reshape(rows // 2, 2, -1, mat.shape[1])
+    ready = [split_rows(out), split_rows(grads[0][0])]
+    lined = [qkv, held[0], down]
     small = jnp.concatenate(
         [
             jnp.stack(vec_grads).reshape(layers * 8, cols, part).transpose(1, 0, 2),
@@ -1032,7 +1085,9 @@
         axis=1,
     )
     halves = flow.reshape(2, half, -1)
-    summed = reduce_all(rows, cols, full, lined, small, pick(halves, 1 - parity).astype(BF16))
+    products = [grads[0][i] for i in (2, 1, 3)]
+    leaving = pick(halves, 1 - parity).astype(BF16)
+    summed = reduce_all(rows, cols, ready, products, lined, small, leaving)
     mine = jnp.arange(2)[:, None, None] == parity
     d_tokens = jnp.where(mine, pick(halves, parity)[None], summed[5].astype(F32)[None])
     mats = summed[:4]

time: 577 us -> 556 us (0.964)
  matrix products: 173 us -> 146 us
    dot_general x8 -> x5, matrix products: 48.3 us -> 30.8 us  [product(): jnp.einsum('td,te->de', x, y, preferred_element_type=F32).astype(BF16)]
    reduce_scatter x4 -> x3, waiting for transfers between devices: 7.92 us -> 0.01 us  [settle_second(): mat = lax.psum_scatter(mat, 'row', scatter_dimension=0, tiled=True)]
    all_gather x3, waiting for transfers between devices: 0.99 us -> 8.73 us  [shards(): lax.all_gather(g, 'row', axis=0, tiled=True)]
    unnamed x115 -> x124, local copies, waits for them, and re-layouts: 21.3 us -> 25 us
  transfers between devices with their start and end apart: 9 -> 8, of which waited for: 2 -> 1; matrix products, arithmetic and copies ran while one was open for 34% -> 30% of each run, Pallas kernels for 18% -> 19%
where the time goes in v5:
time: 556 us; the launch traced here: 546 us
  Pallas kernels  300 us (54%)
  matrix products  146 us (26%)
  other arithmetic  37.2 us (7%)
  local copies, waits for them, and re-layouts  36.1 us (6%)
  between operations  15.4 us (3%)
  waiting for transfers between devices  9.52 us (2%)
    pallas_call x1, Pallas kernels, reduce_all(): pl.pallas_call(functools.partial(reduce_kernel, rows, cols), out_shape=tu...  101 us
    pallas_call x1, Pallas kernels, gather_all(): pl.pallas_call(functools.partial(gather_kernel, rows, cols), out_shape=tu...  95.7 us
    pallas_call x2, Pallas kernels, attend_back(): pl.pallas_call(attend_back_kernel, out_shape=jax.ShapeDtypeStruct((length...  57.8 us
    pallas_call x2, Pallas kernels, attend(): pl.pallas_call(attend_kernel, out_shape=(jax.ShapeDtypeStruct((length, mo...  45.6 us
    dot_general x5, matrix products, product(): jnp.einsum('td,te->de', x, y, preferred_element_type=F32).astype(BF16)  30.8 us
    dot_general x2, matrix products, layer_backward(): jnp.einsum('td,fd->tf', grad_down_low, mat_down, preferred_element_type=F32)  25.7 us
    unnamed x124, local copies, waits for them, and re-layouts  25 us
    dot_general x2, matrix products, layer_forward(): pre_act = jnp.dot(first_out, mat_up, preferred_element_type=F32) + up_bias  21 us
  transfers between devices with their start and end apart: 8, of which 1 were waited for; matrix products, arithmetic and copies ran while one was open for 30% of the time, Pallas kernels for 19%

profile of v5, /device:TPU:0, one launch (start us, length us, event | category | flops | bytes accessed | tf_op | source)
XLA Modules:
  0.0 545.9 jit_solution(8715434245170907782)
XLA Ops:
  14.9 95.7 %shard_map.170 = (bf16[4,2,96,2304]{3,2,1,0:T(8,128)(2,1)}, bf16[4,2,96,768]{3,2,1,0:T(8,128)(2,1)S(1)}, bf16[4,2,96,3072]{3,2,1,0:T(8,128)(2,1)}, bf16[4,2,384,...) custom-call(bf16[2,96,576]{2,1,0:T(8,128)(2,1)S(1)} %copy-done.8, ...), custom_call_target="tpu_custom_call" | custom-call | tf_op jit(solution)/shard_map/pallas_call | solution.py:642
  114.5 6.3 %add_convert_fusion.1.qkv_ref = bf16[1024,2304]{1,0:T(8,128)(2,1)S(1)} fusion(bf16[1024,768]{1,0:T(8,128)(2,1)} %bitcast.121, bf16[768,2304]{1,0:T(8,128)(2,1)} %bitcast.119, f32[2304]{0:T(1024)S(1)} %get-tuple-element.152), kind=kOutput, calls=%fused_computation.23 | convolution fusion | flops 3628597248 | bytes 9839616 | tf_op jit(solution)/shard_map/dot_general | solution.py:265
  120.9 3.3 fusion.17.bias_ref
  124.2 22.7 %shard_map.171 = (bf16[1024,768]{1,0:T(8,128)(2,1)S(1)}, f32[6,8,256]{2,1,0:T(8,128)S(1)}) custom-call(s32[8]{0:T(128)S(1)} %get-tuple-element.136.first_ref, s32[8]{0:T(128)S(1)} %get-tuple-element.135.count_ref, bf16[1024,2304]{1,0:T(8,128)(2,1)S(1)} %add_convert_fusion.1.qkv_ref, f32[1024,1024]{1,0:T(8,128)S(1)} %fusion.17.bias_ref), custom_call_target="tpu_custom_call" | custom-call | tf_op jit(solution)/shard_map/pallas_call | solution.py:155
  150.3 8.6 %multiply_convert_fusion.3 = (bf16[1024,3072]{1,0:T(8,128)(2,1)S(1)}, f32[1024,3072]{1,0:T(8,128)}) fusion(f32[3072]{0:T(1024)S(1)} %bitcast.102, bf16[1024,768]{1,0:T(8,128)(2,1)S(1)} %add_convert_fusion.5.refs_2_, bf16[768,3072]{1,0:T(8,128)(2,1)S(1)} %bitcast.111), kind=kOutput, calls=%fused_computation.18 | convolution fusion | flops 4850712576 | bytes 25178112 | tf_op jit(solution)/shard_map/dot_general | solution.py:272
  159.0 2.7 copy-done.28
  161.7 5.3 fusion.39
  172.0 6.6 %add_convert_fusion.qkv_ref = bf16[1024,2304]{1,0:T(8,128)(2,1)S(1)} fusion(bf16[768,2304]{1,0:T(8,128)(2,1)} %all-gather.4.cloned.1.call-done, f32[2304]{0:T(1024)S(1)} %get-tuple-element.151, f32[1024,768]{1,0:T(8,128)S(1)} %get-tuple-element.158, f32[768]{0:T(1024)S(1)} %get-tuple-element.114, f32[768]{0:T(1024)S(1)} %get-tuple-element.115, ...), kind=kOutput, calls=%fused_computation.22 | convolution fusion | flops 3632529408 | bytes 11426816 | tf_op jit(solution)/shard_map/dot_general | solution.py:265
  178.6 22.9 %shard_map.172 = (bf16[1024,768]{1,0:T(8,128)(2,1)S(1)}, f32[6,8,256]{2,1,0:T(8,128)S(1)}) custom-call(s32[8]{0:T(128)S(1)} %get-tuple-element.136.first_ref, s32[8]{0:T(128)S(1)} %get-tuple-element.135.count_ref, bf16[1024,2304]{1,0:T(8,128)(2,1)S(1)} %add_convert_fusion.qkv_ref, f32[1024,1024]{1,0:T(8,128)S(1)} %copy-done.1), custom_call_target="tpu_custom_call" | custom-call | tf_op jit(solution)/shard_map/pallas_call | solution.py:155
  205.6 12.4 %multiply_convert_fusion.2 = (bf16[1024,3072]{1,0:T(8,128)(2,1)}, f32[1024,3072]{1,0:T(8,128)}) fusion(f32[3072]{0:T(1024)S(1)} %bitcast.104, bf16[768,3072]{1,0:T(8,128)(2,1)} %all-gather.6.cloned.1.call-done, f32[1024,768]{1,0:T(8,128)} %copy-done.19, f32[768]{0:T(1024)S(1)} %get-tuple-element.109, f32[768]{0:T(1024)S(1)} %get-tuple-element.110, ...), kind=kOutput, calls=%fused_computation.16 | convolution fusion | flops 4854644736 | bytes 26765312 | tf_op jit(solution)/shard_map/dot_general | solution.py:272
  217.9 8.7 %all-gather.8.cloned.1.call-done = bf16[3072,768]{1,0:T(8,128)(2,1)} async-done(((bf16[384,768]{1,0:T(8,128)(2,1)}), bf16[3072,768]{1,0:T(8,128)(2,1)}) %all-gather.8.cloned.1.call-update) | async-done | bytes 4718608 | tf_op jit(solution)/shard_map/all_gather | solution.py:1036
  226.6 9.3 %fusion.41 = (f32[1024]{0:T(1024)S(1)}, f32[1024,768]{1,0:T(8,128)S(1)}) fusion(f32[768]{0:T(1024)S(1)} %get-tuple-element.108, bf16[1024,3072]{1,0:T(8,128)(2,1)} %get-tuple-element.161, bf16[3072,768]{1,0:T(8,128)(2,1)} %all-gather.8.cloned.1.call-done, f32[768]{0:T(1024)S(1)} %get-tuple-element.109, f32[768]{0:T(1024)S(1)} %get-tuple-element.110, ...), kind=kOutput, calls=%fused_computation.173 | convolution fusion | flops 4838915072 | bytes 17323008 | tf_op jit(solution)/shard_map/dot_general | solution.py:275
  238.5 2.6 fusion.21
  241.1 2.8 convert_reduce_fusion.7
  245.2 6.9 %convolution_convert_fusion.1 = bf16[3072,768]{1,0:T(8,128)(2,1)} fusion(bf16[1024,3072]{1,0:T(8,128)(2,1)S(1)} %bitcast.127, bf16[1024,768]{1,0:T(8,128)(2,1)S(1)} %get-tuple-element.54), kind=kOutput, calls=%fused_computation.25 | convolution fusion | flops 4834197504 | bytes 12582912 | tf_op jit(solution)/shard_map/td,te->de/dot_general | solution.py:1050
  252.2 13.2 %convert_reduce_fusion = (f32[3072]{0:T(1024)S(1)}, bf16[1024,3072]{1,0:T(8,128)(2,1)S(1)}) fusion(f32[1024,3072]{1,0:T(8,128)} %get-tuple-element.162, f32[3072]{0:T(1024)S(1)} %bitcast.105, bf16[1024,768]{1,0:T(8,128)(2,1)} %copy-done.34, bf16[3072,768]{1,0:T(8,128)(2,1)} %all-gather.8.cloned.1.call-done), kind=kOutput, calls=%fused_computation.12 | convolution fusion | flops 4879021056 | bytes 25190400 | tf_op jit(solution)/shard_map/td,fd->tf/dot_general | solution.py:298
  265.4 2.6 copy-done.48
  268.0 7.9 %convolution_convert_fusion = bf16[768,3072]{1,0:T(8,128)(2,1)} fusion(bf16[1024,3072]{1,0:T(8,128)(2,1)S(1)} %get-tuple-element.55, f32[1024,768]{1,0:T(8,128)S(1)} %copy-done.20, f32[768]{0:T(1024)S(1)} %get-tuple-element.109, f32[768]{0:T(1024)S(1)} %get-tuple-element.110, f32[1024]{0:T(1024)S(1)} %add_rsqrt_fusion.1, f32[1024]{0:T(1024)S(1)} %broadcast_multiply_fusion.9), kind=kOutput, calls=%fused_computation.24 | convolution fusion | flops 4838129664 | bytes 14170112 | tf_op jit(solution)/shard_map/td,te->de/dot_general | solution.py:1050
  276.1 2.8 dynamic-slice_bitcast_fusion.3
  280.3 11.4 %multiply_reduce_fusion = (f32[768]{0:T(1024)S(1)}, f32[1024]{0:T(1024)S(1)}, f32[1024]{0:T(1024)S(1)}, f32[768]{0:T(1024)S(1)}, f32[1024,768]{1,0:T(8,128)S(1)}) fusion(f32[1024,768]{1,0:T(8,128)} %copy-done.19, f32[1024]{0:T(1024)S(1)} %add_rsqrt_fusion.1, f32[1024]{0:T(1024)S(1)} %broadcast_multiply_fusion.9, f32[768]{0:T(1024)S(1)} %get-tuple-element.110, ...), kind=kOutput, calls=%fused_computation.47 | convolution fusion | flops 4848349184 | bytes 22065152 | tf_op jit(solution)/shard_map/tf,df->td/dot_general | solution.py:302
  298.8 28.9 %shard_map.173 = bf16[1024,2304]{1,0:T(8,128)(2,1)} custom-call(s32[8]{0:T(128)S(1)} %get-tuple-element.136.first_ref, s32[8]{0:T(128)S(1)} %get-tuple-element.135.count_ref, bf16[1024,2304]{1,0:T(8,128)(2,1)} %copy-done.5, bf16[1024,768]{1,0:T(8,128)(2,1)S(1)} %convolution_convert_fusion.5.grad_ref, f32[1024,1024]{1,0:T(8,128)S(1)} %copy-done.2, ...), custom_call_target="tpu_custom_call" | custom-call | tf_op jit(solution)/shard_map/pallas_call | solution.py:171
  327.7 8.0 %convolution_convert_fusion.3 = bf16[768,2304]{1,0:T(8,128)(2,1)} fusion(bf16[1024,2304]{1,0:T(8,128)(2,1)} %shard_map.173, f32[1024,768]{1,0:T(8,128)S(1)} %copy-done.18, f32[768]{0:T(1024)S(1)} %get-tuple-element.114, f32[768]{0:T(1024)S(1)} %get-tuple-element.115, f32[1024]{0:T(1024)S(1)} %add_rsqrt_fusion.2, f32[1024]{0:T(1024)S(1)} %broadcast_multiply_fusion.10), kind=kOutput, calls=%fused_computation.27 | convolution fusion | flops 3629580288 | bytes 11417600 | tf_op jit(solution)/shard_map/td,te->de/dot_general | solution.py:1050
  335.6 3.0 convert_reduce_fusion.2
  338.8 10.0 %convolution_add_fusion.3 = f32[1024,768]{1,0:T(8,128)} fusion(f32[1024,768]{1,0:T(8,128)} %get-tuple-element.134, bf16[1024,2304]{1,0:T(8,128)(2,1)} %shard_map.173, bf16[768,2304]{1,0:T(8,128)(2,1)} %all-gather.4.cloned.1.call-done), kind=kOutput, calls=%fused_computation.82 | convolution fusion | flops 3624665088 | bytes 14548992 | tf_op jit(solution)/shard_map/te,de->td/dot_general | solution.py:312
  351.4 3.2 multiply_reduce_fusion.1
  355.8 12.5 %convert_reduce_fusion.1 = (f32[3072]{0:T(1024)S(1)}, bf16[1024,3072]{1,0:T(8,128)(2,1)S(1)}) fusion(f32[1024,3072]{1,0:T(8,128)} %get-tuple-element.156, f32[3072]{0:T(1024)S(1)} %bitcast.103, bf16[1024,768]{1,0:T(8,128)(2,1)S(1)} %get-tuple-element.125.refs_7_, bf16[3072,768]{1,0:T(8,128)(2,1)} %bitcast.115), kind=kOutput, calls=%fused_computation.13 | convolution fusion | flops 4879021056 | bytes 25190400 | tf_op jit(solution)/shard_map/td,fd->tf/dot_general | solution.py:298
  368.5 6.1 %multiply_reduce_fusion.2 = (f32[768]{0:T(1024)S(1)}, f32[1024]{0:T(1024)S(1)}, f32[1024]{0:T(1024)S(1)}, f32[768]{0:T(1024)S(1)}, f32[1024,768]{1,0:T(8,128)S(1)}) fusion(f32[1024,768]{1,0:T(8,128)S(1)} %copy-done.13, f32[1024]{0:T(1024)S(1)} %copy-done.43, f32[1024]{0:T(1024)S(1)} %copy-done.39, f32[768]{0:T(1024)S(1)} %copy-done.41, ...), kind=kOutput, calls=%fused_computation.51 | convolution fusion | flops 4839698432 | bytes 20472832 | tf_op jit(solution)/shard_map/tf,df->td/dot_general | solution.py:302
  380.1 28.9 %shard_map.174 = bf16[1024,2304]{1,0:T(8,128)(2,1)} custom-call(s32[8]{0:T(128)S(1)} %get-tuple-element.136.first_ref, s32[8]{0:T(128)S(1)} %get-tuple-element.135.count_ref, bf16[1024,2304]{1,0:T(8,128)(2,1)} %copy-done.4, bf16[1024,768]{1,0:T(8,128)(2,1)S(1)} %convolution_convert_fusion.4.grad_ref, f32[1024,1024]{1,0:T(8,128)S(1)} %copy-done.3, ...), custom_call_target="tpu_custom_call" | custom-call | tf_op jit(solution)/shard_map/pallas_call | solution.py:171
  409.0 3.2 convert_reduce_fusion.3
  413.1 7.1 %convolution_add_fusion.2 = f32[1024,768]{1,0:T(8,128)S(1)} fusion(f32[1024,768]{1,0:T(8,128)S(1)} %copy-done.30, bf16[1024,2304]{1,0:T(8,128)(2,1)} %shard_map.174, bf16[768,2304]{1,0:T(8,128)(2,1)} %bitcast.120), kind=kOutput, calls=%fused_computation.81 | convolution fusion | flops 3624665088 | bytes 14548992 | tf_op jit(solution)/shard_map/te,de->td/dot_general | solution.py:312
  421.9 5.5 %convolution_convert_fusion.2 = bf16[768,2304]{1,0:T(8,128)(2,1)} fusion(bf16[1024,768]{1,0:T(8,128)(2,1)S(1)} %bitcast.123, bf16[1024,2304]{1,0:T(8,128)(2,1)S(1)} %bitcast.87), kind=kOutput, calls=%fused_computation.26 | convolution fusion | flops 3625648128 | bytes 9830400 | tf_op jit(solution)/shard_map/td,te->de/dot_general | solution.py:1050
  427.4 101.0 %shard_map.175 = (f32[2,96,576]{2,1,0:T(8,128)}, f32[2,96,192]{2,1,0:T(8,128)}, f32[2,96,768]{2,1,0:T(8,128)}, f32[2,384,192]{2,1,0:T(8,128)}, f32[24,192]{1,0:T(8,128)}, /*index=5*/bf16[512,768]{1,0:T(8,128)(2,1)}) custom-call(bf16[4,2,96,768]{3,2,1,0:T(8,128)(2,1)} %bitcast.92, bf16[4,2,96,2304]{3,2,1,0:T(8,128)(2,1)} %bitcast.89, ...), custom_call_target="tpu_custom_call" | custom-call | tf_op jit(solution)/shard_map/pallas_call | solution.py:994
  (245 shorter events, 58.2 us)
Async XLA Ops:
  7.2 164.8 %all-gather.4.cloned.1.call-start = ((), (), s32[]{:S(2)}) async-start(), calls=%async_computation.3 | async-start | bytes 3981312 | tf_op jit(solution)/shard_map/all_gather | solution.py:1036
  14.9 96.6 %copy-start.32 = (bf16[2,512,768]{2,1,0:T(8,128)(2,1)S(1)}, bf16[2,512,768]{2,1,0:T(8,128)(2,1)}, u32[]{:S(2)}) copy-start(bf16[2,512,768]{2,1,0:T(8,128)(2,1)} %param.21) | copy-start | bytes 4718596
  110.6 36.3 %copy-start.10 = (bf16[4,2,96,768]{3,2,1,0:T(8,128)(2,1)}, bf16[4,2,96,768]{3,2,1,0:T(8,128)(2,1)S(1)}, u32[]{:S(2)}) copy-start(bf16[4,2,96,768]{3,2,1,0:T(8,128)(2,1)S(1)} %get-tuple-element.46) | copy-start | bytes 3538948
  110.7 94.9 %all-gather.6.cloned.1.call-start = ((), (), s32[]{:S(2)}) async-start(), calls=%async_computation.4 | async-start | bytes 5308416 | tf_op jit(solution)/shard_map/all_gather | solution.py:1036
  111.4 115.2 %all-gather.8.cloned.1.call-start = ((), (), s32[]{:S(2)}) async-start(), calls=%async_computation.5 | async-start | bytes 5308416 | tf_op jit(solution)/shard_map/all_gather | solution.py:1036
  112.4 55.1 %collective-permute-start.1 = (bf16[512,768]{1,0:T(8,128)(2,1)}, bf16[512,768]{1,0:T(8,128)(2,1)}, u32[]{:S(2)}, u32[]{:S(2)}) collective-permute-start(bf16[512,768]{1,0:T(8,128)(2,1)} %dynamic-slice_bitcast_fusion.1), channel_id=1, source_target_pairs={{0,1},{1,0},{2,3},{3,2},{4,5},{5,4},{6,7},{7,6},{8,9},{9,8},{10,11... | collective-permute-start | bytes 2359304 | tf_op jit(solution)/shard_map/ppermute | solution.py:215
  112.5 238.9 %reduce-scatter.4.cloned.1.call-start = ((), (), s32[]{:S(2)}) async-start(), calls=%async_computation.6 | async-start | bytes 5308416 | tf_op jit(solution)/shard_map/reduce_scatter | solution.py:1058
  114.5 34.7 %copy-start.40 = (f32[768]{0:T(1024)}, f32[768]{0:T(1024)S(1)}, u32[]{:S(2)}) copy-start(f32[768]{0:T(1024)S(1)} %get-tuple-element.118) | copy-start | bytes 9220
  120.8 26.1 %copy-start.4 = (bf16[1024,2304]{1,0:T(8,128)(2,1)}, bf16[1024,2304]{1,0:T(8,128)(2,1)S(1)}, u32[]{:S(2)}) copy-start(bf16[1024,2304]{1,0:T(8,128)(2,1)S(1)} %add_convert_fusion.1.qkv_ref) | copy-start | bytes 14155780
  124.2 22.7 %copy-start = (f32[1024,1024]{1,0:T(8,128)}, f32[1024,1024]{1,0:T(8,128)S(1)}, u32[]{:S(2)}) copy-start(f32[1024,1024]{1,0:T(8,128)S(1)} %fusion.17.bias_ref) | copy-start | bytes 12582916
  124.2 22.8 %copy-start.44 = (bf16[2,512,768]{2,1,0:T(8,128)(2,1)S(1)}, bf16[2,512,768]{2,1,0:T(8,128)(2,1)}, u32[]{:S(2)}) copy-start(bf16[2,512,768]{2,1,0:T(8,128)(2,1)} %get-tuple-element.41) | copy-start | bytes 4718596
  124.2 26.1 %slice-start.2 = ((s8[4718592]{0:T(1024)(128)(4,1)}), s8[524288]{0:T(1024)(128)(4,1)S(1)}, s32[]{:S(2)}) async-start(s8[4718592]{0:T(1024)(128)(4,1)} %bitcast.109), calls=%async_computation.11 | async-start | bytes 1048576
  149.1 9.9 %copy-start.42 = (f32[1024]{0:T(1024)}, f32[1024]{0:T(1024)S(1)}, u32[]{:S(2)}) copy-start(f32[1024]{0:T(1024)S(1)} %add_rsqrt_fusion.3) | copy-start | bytes 12292
  149.2 12.5 %slice-start.6 = ((s8[4718592]{0:T(1024)(128)(4,1)}), s8[4194304]{0:T(1024)(128)(4,1)S(1)}, s32[]{:S(2)}) async-start(s8[4718592]{0:T(1024)(128)(4,1)} %bitcast.116), calls=%async_computation.15 | async-start | bytes 8388608
  150.3 11.4 %slice-start.7 = ((s8[4718592]{0:T(1024)(128)(4,1)}), s8[524288]{0:T(1024)(128)(4,1)S(1)}, s32[]{:S(2)}) async-start(s8[4718592]{0:T(1024)(128)(4,1)} %bitcast.116), calls=%async_computation.16 | async-start | bytes 1048576
  178.6 22.9 %copy-start.5 = (bf16[1024,2304]{1,0:T(8,128)(2,1)}, bf16[1024,2304]{1,0:T(8,128)(2,1)S(1)}, u32[]{:S(2)}) copy-start(bf16[1024,2304]{1,0:T(8,128)(2,1)S(1)} %add_convert_fusion.qkv_ref) | copy-start | bytes 14155780
  178.6 22.9 %copy-start.17 = (f32[1024,768]{1,0:T(8,128)S(1)}, f32[1024,768]{1,0:T(8,128)}, u32[]{:S(2)}) copy-start(f32[1024,768]{1,0:T(8,128)} %copy-done.16) | copy-start | bytes 9437188
  178.6 22.9 %copy-start.46 = (bf16[4,2,96,768]{3,2,1,0:T(8,128)(2,1)S(1)}, bf16[4,2,96,768]{3,2,1,0:T(8,128)(2,1)}, u32[]{:S(2)}) copy-start(bf16[4,2,96,768]{3,2,1,0:T(8,128)(2,1)} %get-tuple-element.51) | copy-start | bytes 3538948
  252.1 156.9 %reduce-scatter.6.cloned.1.call-start = ((), (), s32[]{:S(2)}) async-start(), calls=%async_computation.7 | async-start | bytes 5308416 | tf_op jit(solution)/shard_map/reduce_scatter | solution.py:1058
  252.2 15.8 %copy-start.20 = (f32[1024,768]{1,0:T(8,128)S(1)}, f32[1024,768]{1,0:T(8,128)}, u32[]{:S(2)}) copy-start(f32[1024,768]{1,0:T(8,128)} %copy-done.19) | copy-start | bytes 9437188
  275.9 151.4 %reduce-scatter.8.cloned.1.call-start = ((), (), s32[]{:S(2)}) async-start(), calls=%async_computation.8 | async-start | bytes 3981312 | tf_op jit(solution)/shard_map/reduce_scatter | solution.py:1058
  278.9 12.9 %copy-start.21 = (f32[1024,768]{1,0:T(8,128)S(1)}, f32[1024,768]{1,0:T(8,128)}, u32[]{:S(2)}) copy-start(f32[1024,768]{1,0:T(8,128)} %copy-done.19) | copy-start | bytes 9437188
  278.9 69.9 %collective-permute-start = (bf16[512,768]{1,0:T(8,128)(2,1)}, bf16[512,768]{1,0:T(8,128)(2,1)}, u32[]{:S(2)}, u32[]{:S(2)}) collective-permute-start(bf16[512,768]{1,0:T(8,128)(2,1)} %get-tuple-element.141), channel_id=1, source_target_pairs={{0,1},{1,0},{2,3},{3,2},{4,5},{5,4},{6,7},{7,6},{8,9},{9,8},{10,11... | collective-permute-start | bytes 2359304 | tf_op jit(solution)/shard_map/ppermute | solution.py:215
  298.8 28.9 %copy-start.18 = (f32[1024,768]{1,0:T(8,128)S(1)}, f32[1024,768]{1,0:T(8,128)}, u32[]{:S(2)}) copy-start(f32[1024,768]{1,0:T(8,128)} %copy-done.16) | copy-start | bytes 9437188
  338.8 10.0 %copy-start.31 = (bf16[512,768]{1,0:T(8,128)(2,1)S(1)}, bf16[512,768]{1,0:T(8,128)(2,1)}, u32[]{:S(2)}) copy-start(bf16[512,768]{1,0:T(8,128)(2,1)} %get-tuple-element.140) | copy-start | bytes 2359300
  354.6 13.8 %slice-start.4 = ((s8[4718592]{0:T(1024)(128)(4,1)}), s8[4194304]{0:T(1024)(128)(4,1)S(1)}, s32[]{:S(2)}) async-start(s8[4718592]{0:T(1024)(128)(4,1)} %bitcast.112), calls=%async_computation.13 | async-start | bytes 8388608
  355.8 12.6 %copy-start.25 = (bf16[1024,768]{1,0:T(8,128)(2,1)}, bf16[1024,768]{1,0:T(8,128)(2,1)S(1)}, u32[]{:S(2)}) copy-start(bf16[1024,768]{1,0:T(8,128)(2,1)S(1)} %get-tuple-element.125.refs_7_) | copy-start | bytes 4718596
  355.8 12.6 %copy-start.13 = (f32[1024,768]{1,0:T(8,128)S(1)}, f32[1024,768]{1,0:T(8,128)}, u32[]{:S(2)}) copy-start(f32[1024,768]{1,0:T(8,128)} %copy-done.12) | copy-start | bytes 9437188
  355.8 12.6 %copy-start.39 = (f32[1024]{0:T(1024)S(1)}, f32[1024]{0:T(1024)}, u32[]{:S(2)}) copy-start(f32[1024]{0:T(1024)} %copy-done.38) | copy-start | bytes 12292
  355.8 12.6 %copy-start.41 = (f32[768]{0:T(1024)S(1)}, f32[768]{0:T(1024)}, u32[]{:S(2)}) copy-start(f32[768]{0:T(1024)} %copy-done.40) | copy-start | bytes 9220
  355.8 12.6 %copy-start.43 = (f32[1024]{0:T(1024)S(1)}, f32[1024]{0:T(1024)}, u32[]{:S(2)}) copy-start(f32[1024]{0:T(1024)} %copy-done.42) | copy-start | bytes 12292
  355.8 12.6 %slice-start.5 = ((s8[4718592]{0:T(1024)(128)(4,1)}), s8[524288]{0:T(1024)(128)(4,1)S(1)}, s32[]{:S(2)}) async-start(s8[4718592]{0:T(1024)(128)(4,1)} %bitcast.112), calls=%async_computation.14 | async-start | bytes 1048576
  (35 other events, 117.9 us)
Sparse Core Ops, SparseCore 0:
  110.8 34.0 all-gather.3
  146.8 38.9 all-gather.5
  187.7 38.9 all-gather.7
  252.2 53.8 reduce-scatter.3
  309.8 53.8 reduce-scatter.5
  367.1 48.1 reduce-scatter.7

commit v6 on v5

--- a/solution.py
+++ b/solution.py
@@ -12,7 +12,7 @@
 VMEM_SPEC = pl.BlockSpec(memory_space=pltpu.VMEM)
 UNROLL = 6
 UNROLL_BACK = 6
-WIDTHS = (3, 4, 5, 6, 8)
+WIDTHS = (2, 3, 4, 5, 6, 8)
 SCALE = HEAD ** (-0.5)
 NT = (((1,), (1,)), ((), ()))
 F32 = jnp.float32
@@ -161,7 +161,7 @@
         in_specs=[SMEM_SPEC, SMEM_SPEC, VMEM_SPEC, VMEM_SPEC],
         out_specs=(VMEM_SPEC, VMEM_SPEC),
         scratch_shapes=[pltpu.VMEM((model, length), BF16)],
-        compiler_params=pltpu.CompilerParams(vmem_limit_bytes=40 << 20),
+        compiler_params=pltpu.CompilerParams(vmem_limit_bytes=20 << 20),
     )(first, count, qkv, bias)
 
 
@@ -178,7 +178,7 @@
             pltpu.VMEM((length, model), F32),
             pltpu.VMEM((length, model), F32),
         ],
-        compiler_params=pltpu.CompilerParams(vmem_limit_bytes=48 << 20),
+        compiler_params=pltpu.CompilerParams(vmem_limit_bytes=30 << 20),
     )(first, count, qkv, grad_mix, bias, lse)
 
 NEG_FILL = -1e30
@@ -219,19 +219,19 @@
     return lax.dynamic_index_in_dim(array, index, 0, keepdims=False)
 
 
+def chosen_by(parity, own, other):
+    mine = jnp.arange(2).reshape((2,) + (1,) * other.ndim) == parity
+    return jnp.where(mine, own, other[None])
+
+
 def to_sequence(halves, parity):
-    own = pick(halves, parity)
-    other = swapped(pick(halves, 1 - parity))
-    first = parity == 0
-    return jnp.concatenate([jnp.where(first, own, other), jnp.where(first, other, own)])
-
-
-def from_sequence(whole, parity, narrow):
+    both = chosen_by(parity, halves, swapped(pick(halves, 1 - parity)))
+    return both.reshape((-1,) + both.shape[2:])
+
+
+def from_sequence(whole, parity):
     halves = whole.reshape((2, -1) + whole.shape[1:])
-    own = pick(halves, parity)
-    other = swapped(pick(halves, 1 - parity).astype(narrow)).astype(whole.dtype)
-    mine = jnp.arange(2)[:, None, None] == parity
-    return jnp.where(mine, own[None], other[None])
+    return chosen_by(parity, halves, swapped(pick(halves, 1 - parity)))
 
 
 def key_pattern(seg, pad, rand):
@@ -1043,7 +1043,7 @@
     for layer in range(layers):
         hidden, saved = layer_forward(hidden, weights[layer], pattern)
         kept.append(saved)
-    output = from_sequence(hidden, parity, BF16)
+    output = from_sequence(hidden, parity)
     flow = to_sequence(d_out, parity).astype(F32)
 
     def product(x, y):
@@ -1088,8 +1088,7 @@
     products = [grads[0][i] for i in (2, 1, 3)]
     leaving = pick(halves, 1 - parity).astype(BF16)
     summed = reduce_all(rows, cols, ready, products, lined, small, leaving)
-    mine = jnp.arange(2)[:, None, None] == parity
-    d_tokens = jnp.where(mine, pick(halves, parity)[None], summed[5].astype(F32)[None])
+    d_tokens = chosen_by(parity, halves, summed[5].astype(F32))
     mats = summed[:4]
     vec = summed[4][: layers * 8].reshape(layers, 8, part)
     ups = summed[4][layers * 8 :].reshape(layers, -1)

time: 556 us -> 548 us (0.986)
  Pallas kernels: 300 us -> 293 us
    pallas_call x2, Pallas kernels: 57.8 us -> 49 us  [attend_back(): pl.pallas_call(attend_back_kernel, out_shape=jax.ShapeDtypeStruct((length...]
    unnamed x124 -> x135, local copies, waits for them, and re-layouts: 25 us -> 28 us
  transfers between devices with their start and end apart: 8 -> 8, of which waited for: 1 -> 1; matrix products, arithmetic and copies ran while one was open for 30% -> 30% of each run, Pallas kernels for 19% -> 17%
where the time goes in v6:
time: 548 us; the launch traced here: 540 us
  Pallas kernels  293 us (53%)
  matrix products  145 us (26%)
  local copies, waits for them, and re-layouts  37.5 us (7%)
  other arithmetic  36.6 us (7%)
  between operations  15.5 us (3%)
  waiting for transfers between devices  11.8 us (2%)
    pallas_call x1, Pallas kernels, reduce_all(): pl.pallas_call(functools.partial(reduce_kernel, rows, cols), out_shape=tu...  103 us
    pallas_call x1, Pallas kernels, gather_all(): pl.pallas_call(functools.partial(gather_kernel, rows, cols), out_shape=tu...  95.7 us
    pallas_call x2, Pallas kernels, attend_back(): pl.pallas_call(attend_back_kernel, out_shape=jax.ShapeDtypeStruct((length...  49 us
    pallas_call x2, Pallas kernels, attend(): pl.pallas_call(attend_kernel, out_shape=(jax.ShapeDtypeStruct((length, mo...  45 us
    dot_general x5, matrix products, product(): jnp.einsum('td,te->de', x, y, preferred_element_type=F32).astype(BF16)  28.7 us
    unnamed x135, local copies, waits for them, and re-layouts  28 us
    dot_general x2, matrix products, layer_backward(): jnp.einsum('td,fd->tf', grad_down_low, mat_down, preferred_element_type=F32)  25.3 us
    dot_general x2, matrix products, layer_forward(): pre_act = jnp.dot(first_out, mat_up, preferred_element_type=F32) + up_bias  21 us
  transfers between devices with their start and end apart: 8, of which 1 were waited for; matrix products, arithmetic and copies ran while one was open for 30% of the time, Pallas kernels for 17%

profile of v6, /device:TPU:0, one launch (start us, length us, event | category | flops | bytes accessed | tf_op | source)
XLA Modules:
  0.0 540.5 jit_solution(2927937082965489940)
XLA Ops:
  14.9 95.7 %shard_map.170 = (bf16[4,2,96,2304]{3,2,1,0:T(8,128)(2,1)}, bf16[4,2,96,768]{3,2,1,0:T(8,128)(2,1)S(1)}, bf16[4,2,96,3072]{3,2,1,0:T(8,128)(2,1)}, bf16[4,2,384,...) custom-call(bf16[2,96,576]{2,1,0:T(8,128)(2,1)S(1)} %copy-done.10, ...), custom_call_target="tpu_custom_call" | custom-call | tf_op jit(solution)/shard_map/pallas_call | solution.py:642
  114.6 6.3 %add_convert_fusion.1.qkv_ref = bf16[1024,2304]{1,0:T(8,128)(2,1)S(1)} fusion(bf16[1024,768]{1,0:T(8,128)(2,1)} %bitcast.139, bf16[768,2304]{1,0:T(8,128)(2,1)} %bitcast.137, f32[2304]{0:T(1024)S(1)} %get-tuple-element.150), kind=kOutput, calls=%fused_computation.23 | convolution fusion | flops 3628597248 | bytes 9839616 | tf_op jit(solution)/shard_map/dot_general | solution.py:265
  120.9 3.3 fusion.14.bias_ref
  124.3 22.5 %shard_map.171 = (bf16[1024,768]{1,0:T(8,128)(2,1)S(1)}, f32[6,8,256]{2,1,0:T(8,128)S(1)}) custom-call(s32[8]{0:T(128)S(1)} %get-tuple-element.138.first_ref, s32[8]{0:T(128)S(1)} %get-tuple-element.137.count_ref, bf16[1024,2304]{1,0:T(8,128)(2,1)S(1)} %add_convert_fusion.1.qkv_ref, f32[1024,1024]{1,0:T(8,128)S(1)} %fusion.14.bias_ref), custom_call_target="tpu_custom_call" | custom-call | tf_op jit(solution)/shard_map/pallas_call | solution.py:155
  150.2 8.7 %multiply_convert_fusion.3 = (bf16[1024,3072]{1,0:T(8,128)(2,1)S(1)}, f32[1024,3072]{1,0:T(8,128)}) fusion(f32[3072]{0:T(1024)S(1)} %bitcast.120, bf16[1024,768]{1,0:T(8,128)(2,1)S(1)} %add_convert_fusion.5.refs_2_, bf16[768,3072]{1,0:T(8,128)(2,1)S(1)} %bitcast.129), kind=kOutput, calls=%fused_computation.18 | convolution fusion | flops 4850712576 | bytes 25178112 | tf_op jit(solution)/shard_map/dot_general | solution.py:272
  158.9 5.3 fusion.38
  166.8 3.3 convert_reduce_fusion.6
  170.1 6.6 %add_convert_fusion.qkv_ref = bf16[1024,2304]{1,0:T(8,128)(2,1)S(1)} fusion(bf16[768,2304]{1,0:T(8,128)(2,1)} %all-gather.4.cloned.1.call-done, f32[2304]{0:T(1024)S(1)} %get-tuple-element.149, f32[1024,768]{1,0:T(8,128)S(1)} %get-tuple-element.156, f32[768]{0:T(1024)S(1)} %get-tuple-element.114, f32[768]{0:T(1024)S(1)} %get-tuple-element.115, ...), kind=kOutput, calls=%fused_computation.22 | convolution fusion | flops 3632529408 | bytes 11426816 | tf_op jit(solution)/shard_map/dot_general | solution.py:265
  176.8 22.5 %shard_map.172 = (bf16[1024,768]{1,0:T(8,128)(2,1)S(1)}, f32[6,8,256]{2,1,0:T(8,128)S(1)}) custom-call(s32[8]{0:T(128)S(1)} %get-tuple-element.138.first_ref, s32[8]{0:T(128)S(1)} %get-tuple-element.137.count_ref, bf16[1024,2304]{1,0:T(8,128)(2,1)S(1)} %add_convert_fusion.qkv_ref, f32[1024,1024]{1,0:T(8,128)S(1)} %copy-done.1), custom_call_target="tpu_custom_call" | custom-call | tf_op jit(solution)/shard_map/pallas_call | solution.py:155
  203.3 12.4 %multiply_convert_fusion.2 = (bf16[1024,3072]{1,0:T(8,128)(2,1)}, f32[1024,3072]{1,0:T(8,128)}) fusion(f32[3072]{0:T(1024)S(1)} %bitcast.122, bf16[768,3072]{1,0:T(8,128)(2,1)} %all-gather.6.cloned.1.call-done, f32[1024,768]{1,0:T(8,128)} %copy-done.20, f32[768]{0:T(1024)S(1)} %get-tuple-element.109, f32[768]{0:T(1024)S(1)} %get-tuple-element.110, ...), kind=kOutput, calls=%fused_computation.16 | convolution fusion | flops 4854644736 | bytes 26765312 | tf_op jit(solution)/shard_map/dot_general | solution.py:272
  215.7 11.0 %all-gather.8.cloned.1.call-done = bf16[3072,768]{1,0:T(8,128)(2,1)} async-done(((bf16[384,768]{1,0:T(8,128)(2,1)}), bf16[3072,768]{1,0:T(8,128)(2,1)}) %all-gather.8.cloned.1.call-update) | async-done | bytes 4718608 | tf_op jit(solution)/shard_map/all_gather | solution.py:1036
  226.6 9.3 %fusion.40 = (f32[1024]{0:T(1024)S(1)}, f32[1024,768]{1,0:T(8,128)S(1)}) fusion(f32[768]{0:T(1024)S(1)} %get-tuple-element.108, bf16[1024,3072]{1,0:T(8,128)(2,1)} %get-tuple-element.159, bf16[3072,768]{1,0:T(8,128)(2,1)} %all-gather.8.cloned.1.call-done, f32[768]{0:T(1024)S(1)} %get-tuple-element.109, f32[768]{0:T(1024)S(1)} %get-tuple-element.110, ...), kind=kOutput, calls=%fused_computation.169 | convolution fusion | flops 4838915072 | bytes 17323008 | tf_op jit(solution)/shard_map/dot_general | solution.py:275
  238.6 2.7 convert_reduce_fusion.7
  242.5 7.0 %convolution_convert_fusion.1 = bf16[3072,768]{1,0:T(8,128)(2,1)} fusion(bf16[1024,3072]{1,0:T(8,128)(2,1)S(1)} %bitcast.145, bf16[1024,768]{1,0:T(8,128)(2,1)S(1)} %get-tuple-element.54), kind=kOutput, calls=%fused_computation.25 | convolution fusion | flops 4834197504 | bytes 12582912 | tf_op jit(solution)/shard_map/td,te->de/dot_general | solution.py:1050
  249.6 12.9 %convert_reduce_fusion = (f32[3072]{0:T(1024)S(1)}, bf16[1024,3072]{1,0:T(8,128)(2,1)S(1)}) fusion(f32[1024,3072]{1,0:T(8,128)} %get-tuple-element.160, f32[3072]{0:T(1024)S(1)} %bitcast.123, bf16[1024,768]{1,0:T(8,128)(2,1)} %copy-done.35, bf16[3072,768]{1,0:T(8,128)(2,1)} %all-gather.8.cloned.1.call-done), kind=kOutput, calls=%fused_computation.12 | convolution fusion | flops 4879021056 | bytes 25190400 | tf_op jit(solution)/shard_map/td,fd->tf/dot_general | solution.py:298
  262.5 2.6 copy-done.49
  265.1 7.9 %convolution_convert_fusion = bf16[768,3072]{1,0:T(8,128)(2,1)} fusion(bf16[1024,3072]{1,0:T(8,128)(2,1)S(1)} %get-tuple-element.55, f32[1024,768]{1,0:T(8,128)S(1)} %copy-done.21, f32[768]{0:T(1024)S(1)} %get-tuple-element.109, f32[768]{0:T(1024)S(1)} %get-tuple-element.110, f32[1024]{0:T(1024)S(1)} %add_rsqrt_fusion.1, f32[1024]{0:T(1024)S(1)} %broadcast_multiply_fusion.8), kind=kOutput, calls=%fused_computation.24 | convolution fusion | flops 4838129664 | bytes 14170112 | tf_op jit(solution)/shard_map/td,te->de/dot_general | solution.py:1050
  275.5 11.1 %multiply_reduce_fusion = (f32[768]{0:T(1024)S(1)}, f32[1024]{0:T(1024)S(1)}, f32[1024]{0:T(1024)S(1)}, f32[768]{0:T(1024)S(1)}, f32[1024,768]{1,0:T(8,128)S(1)}) fusion(f32[1024,768]{1,0:T(8,128)} %copy-done.20, f32[1024]{0:T(1024)S(1)} %add_rsqrt_fusion.1, f32[1024]{0:T(1024)S(1)} %broadcast_multiply_fusion.8, f32[768]{0:T(1024)S(1)} %get-tuple-element.110, ...), kind=kOutput, calls=%fused_computation.48 | convolution fusion | flops 4839698432 | bytes 20472832 | tf_op jit(solution)/shard_map/tf,df->td/dot_general | solution.py:302
  289.0 2.5 convolution_convert_fusion.6
  293.8 24.5 %shard_map.173 = bf16[1024,2304]{1,0:T(8,128)(2,1)S(1)} custom-call(s32[8]{0:T(128)S(1)} %get-tuple-element.138.first_ref, s32[8]{0:T(128)S(1)} %get-tuple-element.137.count_ref, bf16[1024,2304]{1,0:T(8,128)(2,1)S(1)} %bitcast.99, bf16[1024,768]{1,0:T(8,128)(2,1)S(1)} %convolution_convert_fusion.5.grad_ref, f32[1024,1024]{1,0:T(8,128)S(1)} %copy-done.2, ...), custom_call_target="tpu_custom_call" | custom-call | tf_op jit(solution)/shard_map/pallas_call | solution.py:171
  320.4 5.8 %convolution_convert_fusion.3 = bf16[768,2304]{1,0:T(8,128)(2,1)} fusion(bf16[1024,2304]{1,0:T(8,128)(2,1)S(1)} %shard_map.173, f32[1024,768]{1,0:T(8,128)S(1)} %copy-done.18, f32[768]{0:T(1024)S(1)} %get-tuple-element.114, f32[768]{0:T(1024)S(1)} %get-tuple-element.115, f32[1024]{0:T(1024)S(1)} %add_rsqrt_fusion.2, f32[1024]{0:T(1024)S(1)} %broadcast_multiply_fusion.9), kind=kOutput, calls=%fused_computation.27 | convolution fusion | flops 3629580288 | bytes 11417600 | tf_op jit(solution)/shard_map/td,te->de/dot_general | solution.py:1050
  326.2 3.0 convert_reduce_fusion.2
  329.4 10.4 %convolution_add_fusion.3 = f32[1024,768]{1,0:T(8,128)} fusion(f32[1024,768]{1,0:T(8,128)} %get-tuple-element.135, bf16[1024,2304]{1,0:T(8,128)(2,1)} %copy-done.7, bf16[768,2304]{1,0:T(8,128)(2,1)} %all-gather.4.cloned.1.call-done), kind=kOutput, calls=%fused_computation.83 | convolution fusion | flops 3624665088 | bytes 14548992 | tf_op jit(solution)/shard_map/te,de->td/dot_general | solution.py:312
  339.8 2.5 broadcast_select_fusion.2
  342.3 3.3 multiply_reduce_fusion.1
  346.9 12.4 %convert_reduce_fusion.1 = (f32[3072]{0:T(1024)S(1)}, bf16[1024,3072]{1,0:T(8,128)(2,1)S(1)}) fusion(f32[1024,3072]{1,0:T(8,128)} %get-tuple-element.154, f32[3072]{0:T(1024)S(1)} %bitcast.121, bf16[1024,768]{1,0:T(8,128)(2,1)S(1)} %get-tuple-element.125.refs_7_, bf16[3072,768]{1,0:T(8,128)(2,1)} %bitcast.133), kind=kOutput, calls=%fused_computation.13 | convolution fusion | flops 4879021056 | bytes 25190400 | tf_op jit(solution)/shard_map/td,fd->tf/dot_general | solution.py:298
  359.4 6.0 %multiply_reduce_fusion.2 = (f32[768]{0:T(1024)S(1)}, f32[1024]{0:T(1024)S(1)}, f32[1024]{0:T(1024)S(1)}, f32[768]{0:T(1024)S(1)}, f32[1024,768]{1,0:T(8,128)S(1)}) fusion(f32[1024,768]{1,0:T(8,128)S(1)} %copy-done.15, f32[1024]{0:T(1024)S(1)} %copy-done.44, f32[1024]{0:T(1024)S(1)} %copy-done.40, f32[768]{0:T(1024)S(1)} %copy-done.42, ...), kind=kOutput, calls=%fused_computation.52 | convolution fusion | flops 4839698432 | bytes 20472832 | tf_op jit(solution)/shard_map/tf,df->td/dot_general | solution.py:302
  372.3 24.5 %shard_map.174 = bf16[1024,2304]{1,0:T(8,128)(2,1)S(1)} custom-call(s32[8]{0:T(128)S(1)} %get-tuple-element.138.first_ref, s32[8]{0:T(128)S(1)} %get-tuple-element.137.count_ref, bf16[1024,2304]{1,0:T(8,128)(2,1)S(1)} %bitcast.97, bf16[1024,768]{1,0:T(8,128)(2,1)S(1)} %convolution_convert_fusion.4.grad_ref, f32[1024,1024]{1,0:T(8,128)S(1)} %copy-done.3, ...), custom_call_target="tpu_custom_call" | custom-call | tf_op jit(solution)/shard_map/pallas_call | solution.py:171
  399.0 3.0 convert_reduce_fusion.3
  403.0 8.6 %convolution_add_fusion.2 = f32[1024,768]{1,0:T(8,128)S(1)} fusion(f32[1024,768]{1,0:T(8,128)} %get-tuple-element.129, bf16[1024,2304]{1,0:T(8,128)(2,1)} %copy-done.6, bf16[768,2304]{1,0:T(8,128)(2,1)} %bitcast.138), kind=kOutput, calls=%fused_computation.82 | convolution fusion | flops 3624665088 | bytes 14548992 | tf_op jit(solution)/shard_map/te,de->td/dot_general | solution.py:312
  414.3 5.5 %convolution_convert_fusion.2 = bf16[768,2304]{1,0:T(8,128)(2,1)} fusion(bf16[1024,768]{1,0:T(8,128)(2,1)S(1)} %bitcast.141, bf16[1024,2304]{1,0:T(8,128)(2,1)S(1)} %bitcast.101), kind=kOutput, calls=%fused_computation.26 | convolution fusion | flops 3625648128 | bytes 9830400 | tf_op jit(solution)/shard_map/td,te->de/dot_general | solution.py:1050
  419.8 102.9 %shard_map.175 = (f32[2,96,576]{2,1,0:T(8,128)}, f32[2,96,192]{2,1,0:T(8,128)}, f32[2,96,768]{2,1,0:T(8,128)}, f32[2,384,192]{2,1,0:T(8,128)}, f32[24,192]{1,0:T(8,128)}, /*index=5*/bf16[512,768]{1,0:T(8,128)(2,1)}) custom-call(bf16[4,2,96,768]{3,2,1,0:T(8,128)(2,1)} %bitcast.109, bf16[4,2,96,2304]{3,2,1,0:T(8,128)(2,1)} %bitcast.108, ...), custom_call_target="tpu_custom_call" | custom-call | tf_op jit(solution)/shard_map/pallas_call | solution.py:994
  (257 shorter events, 59.1 us)
Async XLA Ops:
  7.2 162.9 %all-gather.4.cloned.1.call-start = ((), (), s32[]{:S(2)}) async-start(), calls=%async_computation.3 | async-start | bytes 3981312 | tf_op jit(solution)/shard_map/all_gather | solution.py:1036
  14.9 96.6 %copy-start.33 = (bf16[2,512,768]{2,1,0:T(8,128)(2,1)S(1)}, bf16[2,512,768]{2,1,0:T(8,128)(2,1)}, u32[]{:S(2)}) copy-start(bf16[2,512,768]{2,1,0:T(8,128)(2,1)} %param.21) | copy-start | bytes 4718596
  110.6 36.2 %copy-start.12 = (bf16[4,2,96,768]{3,2,1,0:T(8,128)(2,1)}, bf16[4,2,96,768]{3,2,1,0:T(8,128)(2,1)S(1)}, u32[]{:S(2)}) copy-start(bf16[4,2,96,768]{3,2,1,0:T(8,128)(2,1)S(1)} %get-tuple-element.46) | copy-start | bytes 3538948
  110.7 92.6 %all-gather.6.cloned.1.call-start = ((), (), s32[]{:S(2)}) async-start(), calls=%async_computation.4 | async-start | bytes 5308416 | tf_op jit(solution)/shard_map/all_gather | solution.py:1036
  111.4 115.2 %all-gather.8.cloned.1.call-start = ((), (), s32[]{:S(2)}) async-start(), calls=%async_computation.5 | async-start | bytes 5308416 | tf_op jit(solution)/shard_map/all_gather | solution.py:1036
  112.4 52.3 %collective-permute-start.1 = (bf16[512,768]{1,0:T(8,128)(2,1)}, bf16[512,768]{1,0:T(8,128)(2,1)}, u32[]{:S(2)}, u32[]{:S(2)}) collective-permute-start(bf16[512,768]{1,0:T(8,128)(2,1)} %dynamic-slice_bitcast_fusion), channel_id=1, source_target_pairs={{0,1},{1,0},{2,3},{3,2},{4,5},{5,4},{6,7},{7,6},{8,9},{9,8},{10,11... | collective-permute-start | bytes 2359304 | tf_op jit(solution)/shard_map/ppermute | solution.py:215
  112.5 229.8 %reduce-scatter.4.cloned.1.call-start = ((), (), s32[]{:S(2)}) async-start(), calls=%async_computation.6 | async-start | bytes 5308416 | tf_op jit(solution)/shard_map/reduce_scatter | solution.py:1058
  114.5 34.5 %copy-start.41 = (f32[768]{0:T(1024)}, f32[768]{0:T(1024)S(1)}, u32[]{:S(2)}) copy-start(f32[768]{0:T(1024)S(1)} %get-tuple-element.118) | copy-start | bytes 9220
  120.9 25.9 %copy-start.4 = (bf16[1024,2304]{1,0:T(8,128)(2,1)}, bf16[1024,2304]{1,0:T(8,128)(2,1)S(1)}, u32[]{:S(2)}) copy-start(bf16[1024,2304]{1,0:T(8,128)(2,1)S(1)} %add_convert_fusion.1.qkv_ref) | copy-start | bytes 14155780
  124.2 22.6 %copy-start = (f32[1024,1024]{1,0:T(8,128)}, f32[1024,1024]{1,0:T(8,128)S(1)}, u32[]{:S(2)}) copy-start(f32[1024,1024]{1,0:T(8,128)S(1)} %fusion.14.bias_ref) | copy-start | bytes 12582916
  124.2 22.6 %copy-start.45 = (bf16[2,512,768]{2,1,0:T(8,128)(2,1)S(1)}, bf16[2,512,768]{2,1,0:T(8,128)(2,1)}, u32[]{:S(2)}) copy-start(bf16[2,512,768]{2,1,0:T(8,128)(2,1)} %get-tuple-element.41) | copy-start | bytes 4718596
  124.2 25.9 %slice-start.6 = ((s8[4718592]{0:T(1024)(128)(4,1)}), s8[4194304]{0:T(1024)(128)(4,1)S(1)}, s32[]{:S(2)}) async-start(s8[4718592]{0:T(1024)(128)(4,1)} %bitcast.127), calls=%async_computation.15 | async-start | bytes 8388608
  176.7 22.6 %copy-start.5 = (bf16[1024,2304]{1,0:T(8,128)(2,1)}, bf16[1024,2304]{1,0:T(8,128)(2,1)S(1)}, u32[]{:S(2)}) copy-start(bf16[1024,2304]{1,0:T(8,128)(2,1)S(1)} %add_convert_fusion.qkv_ref) | copy-start | bytes 14155780
  176.7 22.6 %copy-start.17 = (f32[1024,768]{1,0:T(8,128)S(1)}, f32[1024,768]{1,0:T(8,128)}, u32[]{:S(2)}) copy-start(f32[1024,768]{1,0:T(8,128)} %copy-done.16) | copy-start | bytes 9437188
  176.7 22.6 %copy-start.47 = (bf16[4,2,96,768]{3,2,1,0:T(8,128)(2,1)S(1)}, bf16[4,2,96,768]{3,2,1,0:T(8,128)(2,1)}, u32[]{:S(2)}) copy-start(bf16[4,2,96,768]{3,2,1,0:T(8,128)(2,1)} %get-tuple-element.51) | copy-start | bytes 3538948
  241.3 31.8 %copy-start.24 = (bf16[1024,768]{1,0:T(8,128)(2,1)}, bf16[1024,768]{1,0:T(8,128)(2,1)S(1)}, u32[]{:S(2)}) copy-start(bf16[1024,768]{1,0:T(8,128)(2,1)S(1)} %get-tuple-element.139) | copy-start | bytes 4718596
  249.5 149.5 %reduce-scatter.6.cloned.1.call-start = ((), (), s32[]{:S(2)}) async-start(), calls=%async_computation.7 | async-start | bytes 5308416 | tf_op jit(solution)/shard_map/reduce_scatter | solution.py:1058
  249.6 15.5 %copy-start.21 = (f32[1024,768]{1,0:T(8,128)S(1)}, f32[1024,768]{1,0:T(8,128)}, u32[]{:S(2)}) copy-start(f32[1024,768]{1,0:T(8,128)} %copy-done.20) | copy-start | bytes 9437188
  273.0 146.8 %reduce-scatter.8.cloned.1.call-start = ((), (), s32[]{:S(2)}) async-start(), calls=%async_computation.8 | async-start | bytes 3981312 | tf_op jit(solution)/shard_map/reduce_scatter | solution.py:1058
  274.1 65.6 %collective-permute-start = (bf16[512,768]{1,0:T(8,128)(2,1)}, bf16[512,768]{1,0:T(8,128)(2,1)}, u32[]{:S(2)}, u32[]{:S(2)}) collective-permute-start(bf16[512,768]{1,0:T(8,128)(2,1)} %dynamic-slice_bitcast_fusion.1), channel_id=1, source_target_pairs={{0,1},{1,0},{2,3},{3,2},{4,5},{5,4},{6,7},{7,6},{8,9},{9,8},{10,11... | collective-permute-start | bytes 2359304 | tf_op jit(solution)/shard_map/ppermute | solution.py:215
  275.5 11.1 %copy-start.22 = (f32[1024,768]{1,0:T(8,128)S(1)}, f32[1024,768]{1,0:T(8,128)}, u32[]{:S(2)}) copy-start(f32[1024,768]{1,0:T(8,128)} %copy-done.20) | copy-start | bytes 9437188
  293.8 26.6 %copy-start.18 = (f32[1024,768]{1,0:T(8,128)S(1)}, f32[1024,768]{1,0:T(8,128)}, u32[]{:S(2)}) copy-start(f32[1024,768]{1,0:T(8,128)} %copy-done.16) | copy-start | bytes 9437188
  345.6 13.8 %slice-start.8 = ((s8[4718592]{0:T(1024)(128)(4,1)}), s8[4194304]{0:T(1024)(128)(4,1)S(1)}, s32[]{:S(2)}) async-start(s8[4718592]{0:T(1024)(128)(4,1)} %bitcast.130), calls=%async_computation.17 | async-start | bytes 8388608
  346.8 12.5 %copy-start.26 = (bf16[1024,768]{1,0:T(8,128)(2,1)}, bf16[1024,768]{1,0:T(8,128)(2,1)S(1)}, u32[]{:S(2)}) copy-start(bf16[1024,768]{1,0:T(8,128)(2,1)S(1)} %get-tuple-element.125.refs_7_) | copy-start | bytes 4718596
  346.8 12.5 %copy-start.15 = (f32[1024,768]{1,0:T(8,128)S(1)}, f32[1024,768]{1,0:T(8,128)}, u32[]{:S(2)}) copy-start(f32[1024,768]{1,0:T(8,128)} %copy-done.14) | copy-start | bytes 9437188
  346.8 12.5 %copy-start.40 = (f32[1024]{0:T(1024)S(1)}, f32[1024]{0:T(1024)}, u32[]{:S(2)}) copy-start(f32[1024]{0:T(1024)} %copy-done.39) | copy-start | bytes 12292
  346.8 12.5 %copy-start.42 = (f32[768]{0:T(1024)S(1)}, f32[768]{0:T(1024)}, u32[]{:S(2)}) copy-start(f32[768]{0:T(1024)} %copy-done.41) | copy-start | bytes 9220
  346.8 12.5 %copy-start.44 = (f32[1024]{0:T(1024)S(1)}, f32[1024]{0:T(1024)}, u32[]{:S(2)}) copy-start(f32[1024]{0:T(1024)} %copy-done.43) | copy-start | bytes 12292
  346.9 12.5 %slice-start.9 = ((s8[4718592]{0:T(1024)(128)(4,1)}), s8[524288]{0:T(1024)(128)(4,1)S(1)}, s32[]{:S(2)}) async-start(s8[4718592]{0:T(1024)(128)(4,1)} %bitcast.130), calls=%async_computation.18 | async-start | bytes 1048576
  402.2 12.1 %slice-start.4 = ((s8[4718592]{0:T(1024)(128)(4,1)}), s8[524288]{0:T(1024)(128)(4,1)S(1)}, s32[]{:S(2)}) async-start(s8[4718592]{0:T(1024)(128)(4,1)} %bitcast.100), calls=%async_computation.13 | async-start | bytes 1048576
  403.0 11.3 %slice-start.5 = ((s8[4718592]{0:T(1024)(128)(4,1)}), s8[4194304]{0:T(1024)(128)(4,1)S(1)}, s32[]{:S(2)}) async-start(s8[4718592]{0:T(1024)(128)(4,1)} %bitcast.100), calls=%async_computation.14 | async-start | bytes 8388608
  403.0 11.3 %copy-start.46 = (bf16[2,512,768]{2,1,0:T(8,128)(2,1)S(1)}, bf16[2,512,768]{2,1,0:T(8,128)(2,1)}, u32[]{:S(2)}) copy-start(bf16[2,512,768]{2,1,0:T(8,128)(2,1)} %get-tuple-element.41) | copy-start | bytes 4718596
  (40 other events, 142.8 us)
Sparse Core Ops, SparseCore 0:
  110.8 34.0 all-gather.3
  146.8 38.9 all-gather.5
  187.6 38.9 all-gather.7
  249.6 53.8 reduce-scatter.3
  307.2 53.8 reduce-scatter.5
  364.5 48.0 reduce-scatter.7
